TPU v7x, 512 devices: a whole 4x8x8 slice. The times are simulated.
512 devices in a mesh: seq: 64 (over z, y_lo, x), head: 8 (over y_hi, core).
Axes of the slice: x: 4, y: 8 (y_hi: 4, y_lo: 2; y = y_hi * 2 + y_lo), z: 8, core: 2. Of those that a mesh axis runs over, the one named last changes fastest.
Arguments:
- queries: bfloat16 [98304, 3072], P(('seq', 'head'))
- keys: bfloat16 [98304, 3072], P(('seq', 'head'))
- values: bfloat16 [98304, 3072], P(('seq', 'head')), may hold values from -6 to 6
- neighbours: int32 [24, 768, 12], P(None, 'seq'), may hold values from 0 to 767, as said below
- counts: int32 [24, 768], P(None, 'seq'), may hold values from 1 to 12
Outputs:
- attended: bfloat16 [98304, 3072], P(('seq', 'head'))
Inputs may be any that keep to these rules, and one draw needn't show every extreme that they name: `neighbours`: slot 0 names the tile itself. For head h and tile n, the slots name distinct tiles c - 6 to c + 6, where c is n clamped to the range 6 to 768 - 7.
All inputs are finite; a program needn't handle non-finite values.
Results may differ from a plain program's by a relative error of at most 0.011.
Values may be sent and summed in bfloat16 or wider, within the bound.
No kernel may reach another device: no remote copies, remote signals or barrier semaphores. Data moves between devices by JAX's collectives and lax.ppermute only.
A program may use at most 64 MiB of HBM per device.

v0:
```python
import math

import jax
import jax.numpy as jnp
from jax import lax
from jax.sharding import PartitionSpec as P


def with_halo(array, sides, width):
    for axis, dim in sides:
        count, length = (lax.axis_size(axis), array.shape[dim])
        up = [(i, (i + 1) % count) for i in range(count - 1)]
        down = [(j, i) for i, j in up]
        last = lax.slice_in_dim(array, length - width, length, axis=dim)
        leading = lax.slice_in_dim(array, 0, width, axis=dim)
        before = lax.ppermute(last, axis, up)
        after = lax.ppermute(leading, axis, down)
        array = jnp.concatenate([before, array, after], axis=dim)
    return array


def sign_table(size):
    position = jnp.arange(size, dtype=jnp.int32)
    common = jnp.bitwise_and(position[:, None], position[None, :])
    parity = jnp.zeros((size, size), jnp.int32)
    for bit_level in range(max(size.bit_length() - 1, 1)):
        parity = parity + jnp.bitwise_and(jnp.right_shift(common, bit_level), 1)
    return (1 - 2 * jnp.bitwise_and(parity, 1)).astype(jnp.bfloat16)


def attend(query_rot, key_tiles, value_tiles, listed, limit, tile_len):
    tiles_here = listed.shape[0]
    head_dim = query_rot.shape[-1]
    score_scale = 1.0 / math.sqrt(head_dim)
    query_tiles = query_rot.reshape(tiles_here, tile_len, head_dim)
    start = (
        jnp.full((tiles_here, tile_len), -jnp.inf, jnp.float32),
        jnp.zeros((tiles_here, tile_len), jnp.float32),
        jnp.zeros((tiles_here, tile_len, head_dim), jnp.float32),
    )

    def step(slot_index, carry):
        running, total, accumulated = carry
        chosen = lax.dynamic_index_in_dim(listed, slot_index, 1, keepdims=False)
        keys_now = jnp.take(key_tiles, chosen, axis=0)
        values_now = jnp.take(value_tiles, chosen, axis=0)
        scores = (
            jnp.einsum("tqd,tkd->tqk", query_tiles, keys_now, preferred_element_type=jnp.float32)
            * score_scale
        )
        active = slot_index < limit
        scores = jnp.where(active[:, None, None], scores, -jnp.inf)
        newest = jnp.maximum(running, jnp.max(scores, axis=2))
        fade = jnp.exp(running - newest)
        weights = jnp.exp(scores - newest[:, :, None])
        total = total * fade + jnp.sum(weights, axis=2)
        update = jnp.einsum(
            "tqk,tkd->tqd",
            weights.astype(jnp.bfloat16),
            values_now,
            preferred_element_type=jnp.float32,
        )
        accumulated = accumulated * fade[:, :, None] + update
        return (newest, total, accumulated)

    running, total, accumulated = lax.fori_loop(0, jnp.max(limit), step, start)
    return (
        (accumulated / total[:, :, None])
        .astype(jnp.bfloat16)
        .reshape(tiles_here * tile_len, head_dim)
    )


def body(queries, keys, values, neighbours, counts):
    group_size = lax.axis_size("head")
    local_tokens, feature_width = queries.shape
    head_count, tiles_here = counts.shape
    head_dim = feature_width // head_count
    per_device = head_count // group_size
    tile_len = local_tokens * group_size // tiles_here
    signs = sign_table(head_dim)
    rotate_scale = 1.0 / math.sqrt(head_dim)
    query_heads = queries.reshape(local_tokens, head_count, head_dim)
    key_heads = keys.reshape(local_tokens, head_count, head_dim)
    value_heads = values.reshape(local_tokens, head_count, head_dim)
    head_order = jnp.arange(head_count, dtype=jnp.int32)
    query_heads, key_heads, value_heads = (
        lax.all_to_all(query_heads, "head", split_axis=1, concat_axis=0, tiled=True),
        lax.all_to_all(key_heads, "head", split_axis=1, concat_axis=0, tiled=True),
        lax.all_to_all(value_heads, "head", split_axis=1, concat_axis=0, tiled=True),
    )
    mine = lax.dynamic_slice_in_dim(head_order, lax.axis_index("head") * per_device, per_device, 0)
    listed_mine = jnp.take(neighbours, mine, axis=0)
    limit_mine = jnp.take(counts, mine, axis=0)
    key_rot = (
        jnp.einsum("thd,de->hte", key_heads, signs, preferred_element_type=jnp.float32)
        * rotate_scale
    ).astype(jnp.bfloat16)
    query_rot = (
        jnp.einsum("thd,de->hte", query_heads, signs, preferred_element_type=jnp.float32)
        * rotate_scale
    ).astype(jnp.bfloat16)
    stacked = jnp.stack([key_rot, jnp.moveaxis(value_heads, 1, 0)])
    padded = with_halo(stacked, (("seq", 2),), local_tokens * group_size)
    first_tile = lax.axis_index("seq") * tiles_here - tiles_here
    span = padded.shape[2] // tile_len
    key_tiles = padded[0].reshape(per_device, span, tile_len, head_dim)
    value_tiles = padded[1].reshape(per_device, span, tile_len, head_dim)

    def one_head(pieces):
        query_one, key_one, value_one, listed_one, limit_one = pieces
        return attend(query_one, key_one, value_one, listed_one, limit_one, tile_len)

    result = lax.map(
        one_head, (query_rot, key_tiles, value_tiles, listed_mine - first_tile, limit_mine)
    )
    result = jnp.moveaxis(result, 0, 1)
    result = lax.all_to_all(result, "head", split_axis=0, concat_axis=1, tiled=True)
    return result.reshape(local_tokens, feature_width)


def solution(mesh):
    placed = (
        P(("seq", "head"), None),
        P(("seq", "head"), None),
        P(("seq", "head"), None),
        P(None, "seq", None),
        P(None, "seq"),
    )
    return jax.shard_map(
        body, mesh=mesh, in_specs=placed, out_specs=P(("seq", "head"), None), check_vma=False
    )
```

profile of v0, /device:TPU:448, one launch (start us, length us, event | category | flops | bytes accessed | tf_op | source)
XLA Modules:
  0.0 440.5 jit_solution(12146190005698002250)
XLA Ops:
  2.6 7.2 %all-to-all-start.1 = ((bf16[192,24,128]{2,0,1:T(8,128)(2,1)}), bf16[192,24,128]{2,0,1:T(8,128)(2,1)S(1)}, u32[]{:S(2)}, u32[]{:S(2)}) async-start(bf16[192,24,128]{2,0,1:T(8,128)(2,1)} %copy_bitcast_fusion.3), calls=%async_computation.1 | async-start | bytes 2359296 | tf_op jit(solution)/shard_map/all_to_all | solution.py:90
  11.2 30.5 %all-to-all-done.1 = bf16[192,24,128]{2,0,1:T(8,128)(2,1)S(1)} async-done(((bf16[192,24,128]{2,0,1:T(8,128)(2,1)}), bf16[192,24,128]{2,0,1:T(8,128)(2,1)S(1)}, u32[]{:S(2)}, u32[]{:S(2)}) %all-to-all-start.1) | async-done | bytes 1179680 | tf_op jit(solution)/shard_map/all_to_all | solution.py:90
  41.7 3.6 all-to-all-start
  46.3 1.6 copy.46
  47.9 29.5 %all-to-all-done = bf16[192,24,128]{2,0,1:T(8,128)(2,1)S(1)} async-done(((bf16[192,24,128]{2,0,1:T(8,128)(2,1)}), bf16[192,24,128]{2,0,1:T(8,128)(2,1)S(1)}, u32[]{:S(2)}, u32[]{:S(2)}) %all-to-all-start) | async-done | bytes 1179680 | tf_op jit(solution)/shard_map/all_to_all | solution.py:89
  78.0 1.6 pad_maximum_fusion.1
  79.6 3.4 collective-permute-start
  83.0 5.5 %collective-permute-start.1 = (bf16[2,3,1536,128]{2,3,1,0:T(8,128)(2,1)}, bf16[2,3,1536,128]{2,3,1,0:T(8,128)(2,1)}, u32[]{:S(2)}, u32[]{:S(2)}) collective-permute-start(bf16[2,3,1536,128]{2,3,1,0:T(8,128)(2,1)} %pad_maximum_fusion.1), channel_id=1, source_target_pairs={{8,0},{16,8},{24,16},{32,24},{40,32},{48,40},{56,48},{64,56},{72,6... | collective-permute-start | bytes 7077896 | tf_op jit(solution)/shard_map/ppermute | solution.py:17
  89.9 4.3 all-to-all-start.2
  94.2 1.7 copy.41
  97.9 2.1 gather_fusion.3
  102.8 58.8 %all-to-all-done.2 = bf16[192,24,128]{2,0,1:T(8,128)(2,1)} async-done(((bf16[192,24,128]{2,0,1:T(8,128)(2,1)}), bf16[192,24,128]{2,0,1:T(8,128)(2,1)}, u32[]{:S(2)}, u32[]{:S(2)}) %all-to-all-start.2) | async-done | bytes 1179680 | tf_op jit(solution)/shard_map/all_to_all | solution.py:88
  162.9 1.5 fusion.18
  164.4 3.2 pad_maximum_fusion
  167.6 3.8 fusion.44
  171.4 5.8 %copy.47 = bf16[1,3,4608,128]{3,2,1,0:T(8,128)(2,1)} copy(bf16[1,3,4608,128]{2,3,1,0:T(8,128)(2,1)} %get-tuple-element.174) | data formatting | bytes 7077888 | tf_op jit(solution)/shard_map/slice | solution.py:107
  177.2 5.7 %copy.48 = bf16[1,3,4608,128]{3,2,1,0:T(8,128)(2,1)} copy(bf16[1,3,4608,128]{2,3,1,0:T(8,128)(2,1)} %get-tuple-element.173) | data formatting | bytes 7077888 | tf_op jit(solution)/shard_map/slice | solution.py:108
  182.9 139.5 %while.25 = (s32[]{:T(128)}, bf16[3,1536,128]{2,1,0:T(8,128)(2,1)}, s32[3,12]{1,0:T(4,128)S(1)}, s32[3,12,12]{2,1,0:T(8,128)}, bf16[3,36,128,128]{3,2,1,0:T(8,12...) while((s32[]{:T(128)}, bf16[3,1536,128]{2,1,0:T(8,128)(2,1)}, ...), condition=%wide.region_6.8_spmd, body=%wide.region_0.7_spmd.sunk | while | flops 103223392 | bytes 15853176 | solution.py:114
  182.9 3.4 dynamic-slice_bitcast_fusion.3
  189.9 14.0 %while.26 = (s32[]{:T(128)}, f32[12,128]{1,0:T(8,128)S(1)}, f32[12,128]{1,0:T(8,128)S(1)}, f32[12,128,128]{2,1,0:T(8,128)S(1)}, s32[]{:T(128)}, /*index=5*/s32[1...) while((s32[]{:T(128)}, f32[12,128]{1,0:T(8,128)S(1)}, ...), condition=%wide.region_5.6_spmd, body=%wide.region_2.5_spmd.sunk | while | flops 102830168 | bytes 6787587 | solution.py:66
  190.6 1.9 gather_fusion
  194.1 1.9 gather_fusion.1
  197.2 1.9 gather_fusion
  200.8 1.9 gather_fusion.1
  204.9 3.4 dynamic-slice_bitcast_fusion.3
  211.9 20.7 %while.26 = (s32[]{:T(128)}, f32[12,128]{1,0:T(8,128)S(1)}, f32[12,128]{1,0:T(8,128)S(1)}, f32[12,128,128]{2,1,0:T(8,128)S(1)}, s32[]{:T(128)}, /*index=5*/s32[1...) while((s32[]{:T(128)}, f32[12,128]{1,0:T(8,128)S(1)}, ...), condition=%wide.region_5.6_spmd, body=%wide.region_2.5_spmd.sunk | while | flops 102830168 | bytes 6787587 | solution.py:66
  212.6 1.9 gather_fusion
  214.5 1.4 fusion.61
  216.1 1.9 gather_fusion.1
  219.2 1.9 gather_fusion
  222.7 1.9 gather_fusion.1
  225.9 1.9 gather_fusion
  229.4 1.9 gather_fusion.1
  233.6 3.4 dynamic-slice_bitcast_fusion.3
  240.5 80.9 %while.26 = (s32[]{:T(128)}, f32[12,128]{1,0:T(8,128)S(1)}, f32[12,128]{1,0:T(8,128)S(1)}, f32[12,128,128]{2,1,0:T(8,128)S(1)}, s32[]{:T(128)}, /*index=5*/s32[1...) while((s32[]{:T(128)}, f32[12,128]{1,0:T(8,128)S(1)}, ...), condition=%wide.region_5.6_spmd, body=%wide.region_2.5_spmd.sunk | while | flops 102830168 | bytes 6787587 | solution.py:66
  241.2 1.9 gather_fusion
  244.7 1.9 gather_fusion.1
  247.9 1.9 gather_fusion
  249.8 1.4 fusion.61
  251.4 1.9 gather_fusion.1
  254.6 1.9 gather_fusion
  256.5 1.4 fusion.61
  258.1 1.9 gather_fusion.1
  261.3 1.9 gather_fusion
  264.8 1.9 gather_fusion.1
  268.0 1.9 gather_fusion
  271.5 1.9 gather_fusion.1
  274.7 1.9 gather_fusion
  278.2 1.9 gather_fusion.1
  281.4 1.9 gather_fusion
  284.9 1.9 gather_fusion.1
  288.0 1.9 gather_fusion
  291.6 1.9 gather_fusion.1
  294.7 1.9 gather_fusion
  298.2 1.9 gather_fusion.1
  301.4 1.9 gather_fusion
  304.9 1.9 gather_fusion.1
  308.1 1.9 gather_fusion
  311.6 1.9 gather_fusion.1
  314.8 1.9 gather_fusion
  318.3 1.9 gather_fusion.1
  322.5 7.2 %copy.67 = bf16[3,1536,128]{2,0,1:T(4,128)(2,1)S(1)} copy(bf16[3,1536,128]{2,1,0:T(8,128)(2,1)} %get-tuple-element.97) | data formatting | bytes 2359296 | tf_op jit(solution)/shard_map/while | solution.py:114
  329.7 108.1 %all_to_all.69 = bf16[1536,3,128]{2,1,0:T(4,128)(2,1)S(1)} all-to-all(bf16[1536,3,128]{2,1,0:T(4,128)(2,1)S(1)} %bitcast.87), channel_id=1, replica_groups=mesh['seq'=64,'head'=8] {'head'}, dimensions={0} | all-to-all | bytes 2359296 | tf_op jit(solution)/shard_map/all_to_all | solution.py:118
  438.3 2.2 reshape.38
  (189 shorter events, 60.1 us)
Async XLA Ops:
  0.0 1.3 copy-start
  2.6 7.2 %copy-start.1 = (bf16[192,3072]{1,0:T(8,128)(2,1)S(1)}, bf16[192,3072]{1,0:T(8,128)(2,1)}, u32[]{:S(2)}) copy-start(bf16[192,3072]{1,0:T(8,128)(2,1)} %param.12) | copy-start | bytes 3538948
  2.6 39.1 %all-to-all-start.1 = ((bf16[192,24,128]{2,0,1:T(8,128)(2,1)}), bf16[192,24,128]{2,0,1:T(8,128)(2,1)S(1)}, u32[]{:S(2)}, u32[]{:S(2)}) async-start(bf16[192,24,128]{2,0,1:T(8,128)(2,1)} %copy_bitcast_fusion.3), calls=%async_computation.1 | async-start | bytes 2359296 | tf_op jit(solution)/shard_map/all_to_all | solution.py:90
  41.7 35.7 %all-to-all-start = ((bf16[192,24,128]{2,0,1:T(8,128)(2,1)}), bf16[192,24,128]{2,0,1:T(8,128)(2,1)S(1)}, u32[]{:S(2)}, u32[]{:S(2)}) async-start(bf16[192,24,128]{2,0,1:T(8,128)(2,1)} %copy_bitcast_fusion.4), calls=%async_computation | async-start | bytes 2359296 | tf_op jit(solution)/shard_map/all_to_all | solution.py:89
  78.0 10.5 %copy-start.2 = (bf16[192,3072]{1,0:T(8,128)(2,1)S(1)}, bf16[192,3072]{1,0:T(8,128)(2,1)}, u32[]{:S(2)}) copy-start(bf16[192,3072]{1,0:T(8,128)(2,1)} %param.11) | copy-start | bytes 3538948
  79.6 84.8 %collective-permute-start = (bf16[2,3,1536,128]{2,3,1,0:T(8,128)(2,1)}, bf16[2,3,1536,128]{2,3,1,0:T(8,128)(2,1)}, u32[]{:S(2)}, u32[]{:S(2)}) collective-permute-start(bf16[2,3,1536,128]{2,3,1,0:T(8,128)(2,1)} %pad_maximum_fusion.1), channel_id=1, source_target_pairs={{0,8},{8,16},{16,24},{24,32},{32,40},{40,48},{48,56},{56,64},{64,7... | collective-permute-start | bytes 7077896 | tf_op jit(solution)/shard_map/ppermute | solution.py:16
  83.0 81.4 %collective-permute-start.1 = (bf16[2,3,1536,128]{2,3,1,0:T(8,128)(2,1)}, bf16[2,3,1536,128]{2,3,1,0:T(8,128)(2,1)}, u32[]{:S(2)}, u32[]{:S(2)}) collective-permute-start(bf16[2,3,1536,128]{2,3,1,0:T(8,128)(2,1)} %pad_maximum_fusion.1), channel_id=1, source_target_pairs={{8,0},{16,8},{24,16},{32,24},{40,32},{48,40},{56,48},{64,56},{72,6... | collective-permute-start | bytes 7077896 | tf_op jit(solution)/shard_map/ppermute | solution.py:17
  89.9 71.6 %all-to-all-start.2 = ((bf16[192,24,128]{2,0,1:T(8,128)(2,1)}), bf16[192,24,128]{2,0,1:T(8,128)(2,1)}, u32[]{:S(2)}, u32[]{:S(2)}) async-start(bf16[192,24,128]{2,0,1:T(8,128)(2,1)} %copy_bitcast_fusion.2), calls=%async_computation.2 | async-start | bytes 2359296 | tf_op jit(solution)/shard_map/all_to_all | solution.py:88
  97.3 0.6 copy-start.3
where the time goes:
time: 445 us; the launch traced here: 440 us
  local copies, waits for them, and re-layouts  126 us (28%)
  waiting for transfers between devices  119 us (27%)
  blocking collectives  108 us (24%)
  matrix products  36.2 us (8%)
  starting transfers between devices  23.9 us (5%)
  loops' own time  14.3 us (3%)
  other arithmetic  13.3 us (3%)
    all_to_all x1, blocking collectives, body(): lax.all_to_all(result, 'head', split_axis=0, concat_axis=1, tiled=True)  108 us
    all_to_all x1, waiting for transfers between devices, body(): lax.all_to_all(query_heads, 'head', split_axis=1, concat_axis=0, tiled=True)  58.8 us
    gather x17, local copies, waits for them, and re-layouts, step(): keys_now = jnp.take(key_tiles, chosen, axis=0)  32.2 us
    gather x17, local copies, waits for them, and re-layouts, step(): values_now = jnp.take(value_tiles, chosen, axis=0)  32.2 us
    all_to_all x1, waiting for transfers between devices, body(): lax.all_to_all(value_heads, 'head', split_axis=1, concat_axis=0, tiled=True)  30.5 us
    all_to_all x1, waiting for transfers between devices, body(): lax.all_to_all(key_heads, 'head', split_axis=1, concat_axis=0, tiled=True)  29.5 us
    dot_general x17, matrix products, step(): jnp.einsum('tqd,tkd->tqk', query_tiles, keys_now, preferred_element_type=...  24.6 us
    another operation x3, loops' own time, attend(): running, total, accumulated = lax.fori_loop(0, jnp.max(limit), step, start)  14.2 us
  transfers between devices with their start and end apart: 5, of which 3 were waited for; matrix products, arithmetic and copies ran while one was open for 4% of the time, Pallas kernels for 0%

commit v1 on v0

v1 whole, which is shorter than its diff:
```python
import math

import jax
import jax.numpy as jnp
from jax import lax
from jax.experimental import pallas as pl
from jax.experimental.pallas import tpu as pltpu
from jax.sharding import PartitionSpec as P

VMEM_BYTES = 40 * 1024 * 1024


def sign_block(size):
    row = lax.broadcasted_iota(jnp.int32, (size, size), 0)
    column = lax.broadcasted_iota(jnp.int32, (size, size), 1)
    common = jnp.bitwise_and(row, column)
    parity = jnp.zeros((size, size), jnp.int32)
    for bit_level in range(max(size.bit_length() - 1, 1)):
        parity = parity + jnp.bitwise_and(jnp.right_shift(common, bit_level), 1)
    return (1 - 2 * jnp.bitwise_and(parity, 1)).astype(jnp.float32).astype(jnp.bfloat16)


def prepare(arrays, rotated, group_size, per_device, head_dim):
    tokens = arrays[0].shape[0]
    width = per_device * head_dim
    scale = 1.0 / math.sqrt(head_dim)

    def kernel(*refs):
        out_ref = refs[-1]
        signs = sign_block(head_dim)
        for index, ref in enumerate(refs[:-1]):
            for head in range(per_device):
                block = ref[:, head * head_dim : (head + 1) * head_dim]
                if rotated[index]:
                    turned = jnp.dot(block, signs, preferred_element_type=jnp.float32)
                    block = (turned * scale).astype(jnp.bfloat16)
                out_ref[0, index, head] = block

    count = len(arrays)
    return pl.pallas_call(
        kernel,
        grid=(group_size,),
        in_specs=[pl.BlockSpec((tokens, width), lambda g: (0, g))] * count,
        out_specs=pl.BlockSpec(
            (1, count, per_device, tokens, head_dim), lambda g: (g, 0, 0, 0, 0)
        ),
        out_shape=jax.ShapeDtypeStruct(
            (group_size, count, per_device, tokens, head_dim), jnp.bfloat16
        ),
        cost_estimate=pl.CostEstimate(
            flops=2 * tokens * width * group_size * head_dim * sum(rotated),
            bytes_accessed=4 * tokens * width * group_size * count,
            transcendentals=0,
        ),
    )(*arrays)


def attend(own, left, right, query, listed, counts, place, tile_len):
    sources, _, heads, tokens, head_dim = own.shape
    half = left.shape[0]
    span_sources = sources + 2 * half
    rows = sources * tokens
    span_rows = span_sources * tokens
    tiles_here = rows // tile_len
    span_tiles = span_rows // tile_len
    slots = listed.shape[1] // tiles_here
    factor = math.log2(math.e) / math.sqrt(head_dim)

    def kernel(place_ref, listed_ref, counts_ref, own_ref, left_ref, right_ref, query_ref, out_ref,
               key_buf, value_buf, query_buf, sems):
        def copies(head):
            found = []
            for index, buf in ((0, key_buf), (1, value_buf)):
                first = 0
                for ref, length in ((left_ref, half), (own_ref, sources), (right_ref, half)):
                    found.append(
                        pltpu.make_async_copy(
                            ref.at[:, index, head],
                            buf.at[head, pl.ds(first, length)],
                            sems.at[head, len(found)],
                        )
                    )
                    first += length
            found.append(
                pltpu.make_async_copy(
                    query_ref.at[:, 0, head], query_buf.at[head], sems.at[head, len(found)]
                )
            )
            return found

        for head in range(heads):
            for copy in copies(head):
                copy.start()
        first_head = place_ref[0]
        first_tile = place_ref[1]

        for head in range(heads):
            for copy in copies(head):
                copy.wait()
            key_rows = key_buf.at[head].reshape(span_rows, head_dim)
            value_rows = value_buf.at[head].reshape(span_rows, head_dim)
            query_rows = query_buf.at[head].reshape(rows, head_dim)
            row = first_head + head

            @pl.loop(0, tiles_here)
            def _(tile):
                limit = counts_ref[row, tile]
                token = pl.multiple_of(tile * tile_len, tile_len)

                def place_of(slot):
                    at = listed_ref[row, tile * slots + slot] - first_tile
                    at = jnp.clip(at, 0, span_tiles - 1)
                    return pl.ds(pl.multiple_of(at * tile_len, tile_len), tile_len)

                def work(used):
                    query_now = query_rows[pl.ds(token, tile_len), :]
                    scores = []
                    peak = None
                    places = [place_of(slot) for slot in range(used)]
                    for slot in range(0, used, 2):
                        keys_now = jnp.concatenate(
                            [key_rows[places[slot], :], key_rows[places[slot + 1], :]], axis=0
                        )
                        pair = lax.dot_general(
                            query_now, keys_now, (((1,), (1,)), ((), ())),
                            preferred_element_type=jnp.float32,
                        )
                        one, two = pair[:, :tile_len], pair[:, tile_len:]
                        if slot + 2 >= used:
                            two = jnp.where(limit >= used, two, -jnp.inf)
                        scores += [one, two]
                        larger = jnp.maximum(one, two)
                        peak = larger if peak is None else jnp.maximum(peak, larger)
                    peak = jnp.max(peak, axis=1, keepdims=True)
                    total = None
                    mixed = None
                    for slot in range(0, used, 2):
                        one = jnp.exp2((scores[slot] - peak) * factor)
                        two = jnp.exp2((scores[slot + 1] - peak) * factor)
                        both = one + two
                        total = both if total is None else total + both
                        weights = jnp.concatenate(
                            [one.astype(jnp.bfloat16), two.astype(jnp.bfloat16)], axis=1
                        )
                        values_now = jnp.concatenate(
                            [value_rows[places[slot], :], value_rows[places[slot + 1], :]], axis=0
                        )
                        update = jnp.dot(weights, values_now, preferred_element_type=jnp.float32)
                        mixed = update if mixed is None else mixed + update
                    total = jnp.sum(total, axis=1, keepdims=True)
                    out_ref[pl.ds(token, tile_len), head * head_dim : (head + 1) * head_dim] = (
                        mixed / total
                    ).astype(jnp.bfloat16)

                for used in range(2, slots + 1, 2):
                    @pl.when((limit + 1) // 2 == used // 2)
                    def _():
                        work(used)

    smem = pl.BlockSpec(memory_space=pltpu.SMEM)
    hbm = pl.BlockSpec(memory_space=pl.ANY)
    pairs = heads * tiles_here * slots
    return pl.pallas_call(
        kernel,
        in_specs=[smem, smem, smem, hbm, hbm, hbm, hbm],
        out_specs=pl.BlockSpec(memory_space=pltpu.VMEM),
        out_shape=jax.ShapeDtypeStruct((rows, heads * head_dim), jnp.bfloat16),
        scratch_shapes=[
            pltpu.VMEM((heads, span_sources, tokens, head_dim), jnp.bfloat16),
            pltpu.VMEM((heads, span_sources, tokens, head_dim), jnp.bfloat16),
            pltpu.VMEM((heads, sources, tokens, head_dim), jnp.bfloat16),
            pltpu.SemaphoreType.DMA((heads, 7)),
        ],
        compiler_params=pltpu.CompilerParams(vmem_limit_bytes=VMEM_BYTES),
        cost_estimate=pl.CostEstimate(
            flops=4 * pairs * tile_len * tile_len * head_dim,
            bytes_accessed=2 * heads * head_dim * (2 * span_rows + 2 * rows),
            transcendentals=pairs * tile_len * tile_len,
        ),
    )(place, listed, counts, own, left, right, query)


def body(queries, keys, values, neighbours, counts):
    group_size = lax.axis_size("head")
    blocks = lax.axis_size("seq")
    local_tokens, feature_width = queries.shape
    head_count, tiles_here = counts.shape
    head_dim = feature_width // head_count
    per_device = head_count // group_size
    tile_len = local_tokens * group_size // tiles_here
    half = group_size // 2
    halo_tiles = half * local_tokens // tile_len

    def exchange(array):
        return lax.all_to_all(array, "head", split_axis=0, concat_axis=0, tiled=True)

    packed = prepare([keys, values], [True, False], group_size, per_device, head_dim)
    own = exchange(packed)
    packed = prepare([queries], [True], group_size, per_device, head_dim)
    query = exchange(packed)
    up = [(i, i + 1) for i in range(blocks - 1)]
    down = [(i + 1, i) for i in range(blocks - 1)]
    left = lax.ppermute(own[group_size - half :], "seq", up)
    right = lax.ppermute(own[:half], "seq", down)
    place = jnp.stack(
        [
            lax.axis_index("head") * per_device,
            lax.axis_index("seq") * tiles_here - halo_tiles,
        ]
    ).astype(jnp.int32)
    listed = neighbours.reshape(head_count, -1)
    result = attend(own, left, right, query, listed, counts, place, tile_len)
    result = exchange(result.reshape(group_size, local_tokens, per_device * head_dim))
    return jnp.moveaxis(result, 0, 1).reshape(local_tokens, feature_width)


def solution(mesh):
    placed = (
        P(("seq", "head"), None),
        P(("seq", "head"), None),
        P(("seq", "head"), None),
        P(None, "seq", None),
        P(None, "seq"),
    )
    return jax.shard_map(
        body, mesh=mesh, in_specs=placed, out_specs=P(("seq", "head"), None), check_vma=False
    )
```

time: 445 us -> 193 us (0.43)
  local copies, waits for them, and re-layouts: 126 us -> 7.42 us
  blocking collectives: 108 us -> 39.4 us
  matrix products: 36.2 us -> 0 us
  Pallas kernels: 0 us -> 33.3 us
  waiting for transfers between devices: 119 us -> 92.1 us
  loops' own time: 14.3 us -> 0 us
  other arithmetic: 13.3 us -> 0.07 us
    all_to_all x1, blocking collectives: 108 us -> 39.4 us  [exchange(): lax.all_to_all(array, 'head', split_axis=0, concat_axis=0, tiled=True)]
    gather x36 -> x0, local copies, waits for them, and re-layouts: 67.1 us -> none  [the longest x17 32.2 us: step(): keys_now = jnp.take(key_tiles, chosen, axis=0)]
    all_to_all x3 -> x2, waiting for transfers between devices: 119 us -> 69.1 us  [exchange(): lax.all_to_all(array, 'head', split_axis=0, concat_axis=0, tiled=True)]
    dot_general x36 -> x0, matrix products: 36.2 us -> none  [the longest x17 24.6 us: step(): jnp.einsum('tqd,tkd->tqk', query_tiles, keys_now, preferred_element_type=...]
    pallas_call x0 -> x3, Pallas kernels: none -> 33.3 us  [the longest x1 20.6 us: attend(): pl.pallas_call(kernel, in_specs=[smem, smem, smem, hbm, hbm, hbm, hbm], o...]
    ppermute x2, waiting for transfers between devices: 0.01 us -> 23 us  [the longest x1 23 us: body(): left = lax.ppermute(own[group_size - half:], 'seq', up)]
    another operation x4 -> x0, loops' own time: 14.3 us -> none  [the longest x3 14.2 us: attend(): running, total, accumulated = lax.fori_loop(0, jnp.max(limit), step, start)]
    slice x3 -> x1, local copies, waits for them, and re-layouts: 15.3 us -> 1.61 us  [body(): right = lax.ppermute(own[:half], 'seq', down)]
  transfers between devices with their start and end apart: 5 -> 4, of which waited for: 3 -> 3; matrix products, arithmetic and copies ran while one was open for 4% -> 3% of each run, Pallas kernels for 0% -> 3%
where the time goes in v1:
time: 193 us; the launch traced here: 192 us
  waiting for transfers between devices  92.1 us (48%)
  blocking collectives  39.4 us (20%)
  Pallas kernels  33.3 us (17%)
  starting transfers between devices  19.5 us (10%)
  local copies, waits for them, and re-layouts  7.42 us (4%)
    all_to_all x2, waiting for transfers between devices, exchange(): lax.all_to_all(array, 'head', split_axis=0, concat_axis=0, tiled=True)  69.1 us
    all_to_all x1, blocking collectives, exchange(): lax.all_to_all(array, 'head', split_axis=0, concat_axis=0, tiled=True)  39.4 us
    ppermute x1, waiting for transfers between devices, body(): left = lax.ppermute(own[group_size - half:], 'seq', up)  23 us
    pallas_call x1, Pallas kernels, attend(): pl.pallas_call(kernel, in_specs=[smem, smem, smem, hbm, hbm, hbm, hbm], o...  20.6 us
    pallas_call x2, Pallas kernels, prepare(): pl.pallas_call(kernel, grid=(group_size,), in_specs=[pl.BlockSpec((tokens...  12.7 us
    all_to_all x2, starting transfers between devices, exchange(): lax.all_to_all(array, 'head', split_axis=0, concat_axis=0, tiled=True)  10.7 us
    ppermute x1, starting transfers between devices, body(): right = lax.ppermute(own[:half], 'seq', down)  5.46 us
  transfers between devices with their start and end apart: 4, of which 3 were waited for; matrix products, arithmetic and copies ran while one was open for 3% of the time, Pallas kernels for 3%

profile of v1, /device:TPU:448, one launch (start us, length us, event | category | flops | bytes accessed | tf_op | source)
XLA Modules:
  0.0 191.9 jit_solution(14632094509325549501)
XLA Ops:
  0.0 6.6 %shard_map.55 = bf16[8,2,3,192,128]{4,3,2,1,0:T(8,128)(2,1)} custom-call(bf16[192,3072]{1,0:T(8,128)(2,1)} %refs_0_.2, bf16[192,3072]{1,0:T(8,128)(2,1)} %refs_1_.1), custom_call_target="tpu_custom_call" | custom-call | flops 150994944 | bytes 4718592 | tf_op jit(solution)/shard_map/pallas_call | solution.py:40
  6.6 7.1 %all-to-all-start = ((bf16[8,2,3,192,128]{4,3,2,1,0:T(8,128)(2,1)}), bf16[8,2,3,192,128]{4,3,2,1,0:T(8,128)(2,1)S(1)}, u32[]{:S(2)}, u32[]{:S(2)}) async-start(bf16[8,2,3,192,128]{4,3,2,1,0:T(8,128)(2,1)} %shard_map.55), calls=%async_computation | async-start | bytes 4718592 | tf_op jit(solution)/shard_map/all_to_all | solution.py:195
  13.7 6.1 %shard_map.56 = bf16[8,1,3,192,128]{4,3,2,1,0:T(8,128)(2,1)} custom-call(bf16[192,3072]{1,0:T(8,128)(2,1)} %refs_0_.3), custom_call_target="tpu_custom_call" | custom-call | flops 150994944 | bytes 2359296 | tf_op jit(solution)/shard_map/pallas_call | solution.py:40
  19.8 51.0 %all-to-all-done.own_ref = bf16[8,2,3,192,128]{4,3,2,1,0:T(8,128)(2,1)S(1)} async-done(((bf16[8,2,3,192,128]{4,3,2,1,0:T(8,128)(2,1)}), bf16[8,2,3,192,128]{4,3,2,1,0:T(8,128)(2,1)S(1)}, u32[]{:S(2)}, u32[]{:S(2)}) %all-to-all-start) | async-done | bytes 2359328 | tf_op jit(solution)/shard_map/all_to_all | solution.py:195
  70.8 3.6 %all-to-all-start.1 = ((bf16[8,1,3,192,128]{4,3,2,1,0:T(8,128)(2,1)}), bf16[8,1,3,192,128]{4,3,2,1,0:T(8,128)(2,1)S(1)}, u32[]{:S(2)}, u32[]{:S(2)}) async-start(bf16[8,1,3,192,128]{4,3,2,1,0:T(8,128)(2,1)} %shard_map.56), calls=%async_computation.1 | async-start | bytes 2359296 | tf_op jit(solution)/shard_map/all_to_all | solution.py:195
  74.3 1.6 fusion
  76.0 3.4 %collective-permute-start = (bf16[4,2,3,192,128]{4,3,2,1,0:T(8,128)(2,1)}, bf16[4,2,3,192,128]{4,3,2,1,0:T(8,128)(2,1)}, u32[]{:S(2)}, u32[]{:S(2)}) collective-permute-start(bf16[4,2,3,192,128]{4,3,2,1,0:T(8,128)(2,1)} %get-tuple-element.6), channel_id=1, source_target_pairs={{0,8},{8,16},{16,24},{24,32},{32,40},{40,48},{48,56},{56,64},{64,7... | collective-permute-start | bytes 3538952 | tf_op jit(solution)/shard_map/ppermute | solution.py:203
  79.3 5.5 %collective-permute-start.1 = (bf16[4,2,3,192,128]{4,3,2,1,0:T(8,128)(2,1)}, bf16[4,2,3,192,128]{4,3,2,1,0:T(8,128)(2,1)}, u32[]{:S(2)}, u32[]{:S(2)}) collective-permute-start(bf16[4,2,3,192,128]{4,3,2,1,0:T(8,128)(2,1)} %get-tuple-element.5), channel_id=1, source_target_pairs={{8,0},{16,8},{24,16},{32,24},{40,32},{48,40},{56,48},{64,56},{72,6... | collective-permute-start | bytes 3538952 | tf_op jit(solution)/shard_map/ppermute | solution.py:204
  84.8 1.5 reshape.9
  86.3 1.6 copy.9.listed_ref
  87.9 0.8 copy.10.counts_ref
  88.7 0.1 pad_add_fusion.place_ref
  88.7 18.1 %all-to-all-done.1.query_ref = bf16[8,1,3,192,128]{4,3,2,1,0:T(8,128)(2,1)S(1)} async-done(((bf16[8,1,3,192,128]{4,3,2,1,0:T(8,128)(2,1)}), bf16[8,1,3,192,128]{4,3,2,1,0:T(8,128)(2,1)S(1)}, u32[]{:S(2)}, u32[]{:S(2)}) %all-to-all-start.1) | async-done | bytes 1179680 | tf_op jit(solution)/shard_map/all_to_all | solution.py:195
  106.9 23.0 %collective-permute-done.left_ref = bf16[4,2,3,192,128]{4,3,2,1,0:T(8,128)(2,1)} collective-permute-done((bf16[4,2,3,192,128]{4,3,2,1,0:T(8,128)(2,1)}, bf16[4,2,3,192,128]{4,3,2,1,0:T(8,128)(2,1)}, u32[]{:S(2)}, u32[]{:S(2)}) %collective-permute-start) | collective-permute-done | bytes 1179680 | tf_op jit(solution)/shard_map/ppermute | solution.py:203
  129.9 0.0 collective-permute-done.1.right_ref
  129.9 0.0 copy-start
  129.9 0.7 copy-done
  130.7 20.6 %shard_map.57 = bf16[1536,384]{1,0:T(8,128)(2,1)S(1)} custom-call(s32[2]{0:T(128)S(1)} %pad_add_fusion.place_ref, s32[24,144]{1,0:T(8,128)S(1)} %copy-done, s32[24,12]{1,0:T(8,128)S(1)} %copy.10.counts_ref, bf16[8,2,3,192,128]{4,3,2,1,0:T(8,128)(2,1)S(1)} %all-to-all-done.own_ref, bf16[4,2,3,192,128]{4,3,2,1,0:T(8,128)(2,1)} %collective-permute-done.left_ref, ...), custom_call_target="tpu_custom_call" | custom-call | flops 3623878656 | bytes 7077888 | tf_op jit(solution)/shard_map/pallas_call | solution.py:163
  151.3 39.4 %all_to_all.15 = bf16[8,192,384]{2,1,0:T(8,128)(2,1)S(1)} all-to-all(bf16[8,192,384]{2,1,0:T(8,128)(2,1)S(1)} %bitcast.8), channel_id=1, replica_groups=mesh['seq'=64,'head'=8] {'head'}, dimensions={0} | all-to-all | bytes 2359296 | tf_op jit(solution)/shard_map/all_to_all | solution.py:195
  190.7 1.2 copy.12
Async XLA Ops:
  6.6 64.2 %all-to-all-start = ((bf16[8,2,3,192,128]{4,3,2,1,0:T(8,128)(2,1)}), bf16[8,2,3,192,128]{4,3,2,1,0:T(8,128)(2,1)S(1)}, u32[]{:S(2)}, u32[]{:S(2)}) async-start(bf16[8,2,3,192,128]{4,3,2,1,0:T(8,128)(2,1)} %shard_map.55), calls=%async_computation | async-start | bytes 4718592 | tf_op jit(solution)/shard_map/all_to_all | solution.py:195
  70.8 36.1 %all-to-all-start.1 = ((bf16[8,1,3,192,128]{4,3,2,1,0:T(8,128)(2,1)}), bf16[8,1,3,192,128]{4,3,2,1,0:T(8,128)(2,1)S(1)}, u32[]{:S(2)}, u32[]{:S(2)}) async-start(bf16[8,1,3,192,128]{4,3,2,1,0:T(8,128)(2,1)} %shard_map.56), calls=%async_computation.1 | async-start | bytes 2359296 | tf_op jit(solution)/shard_map/all_to_all | solution.py:195
  76.0 54.0 %collective-permute-start = (bf16[4,2,3,192,128]{4,3,2,1,0:T(8,128)(2,1)}, bf16[4,2,3,192,128]{4,3,2,1,0:T(8,128)(2,1)}, u32[]{:S(2)}, u32[]{:S(2)}) collective-permute-start(bf16[4,2,3,192,128]{4,3,2,1,0:T(8,128)(2,1)} %get-tuple-element.6), channel_id=1, source_target_pairs={{0,8},{8,16},{16,24},{24,32},{32,40},{40,48},{48,56},{56,64},{64,7... | collective-permute-start | bytes 3538952 | tf_op jit(solution)/shard_map/ppermute | solution.py:203
  79.3 50.6 %collective-permute-start.1 = (bf16[4,2,3,192,128]{4,3,2,1,0:T(8,128)(2,1)}, bf16[4,2,3,192,128]{4,3,2,1,0:T(8,128)(2,1)}, u32[]{:S(2)}, u32[]{:S(2)}) collective-permute-start(bf16[4,2,3,192,128]{4,3,2,1,0:T(8,128)(2,1)} %get-tuple-element.5), channel_id=1, source_target_pairs={{8,0},{16,8},{24,16},{32,24},{40,32},{48,40},{56,48},{64,56},{72,6... | collective-permute-start | bytes 3538952 | tf_op jit(solution)/shard_map/ppermute | solution.py:204
  129.9 0.7 copy-start

commit v2 on v1

--- a/solution.py
+++ b/solution.py
@@ -7,7 +7,8 @@
 from jax.experimental.pallas import tpu as pltpu
 from jax.sharding import PartitionSpec as P
 
-VMEM_BYTES = 40 * 1024 * 1024
+VMEM_BYTES = 60 * 1024 * 1024
+GROUP = 6
 
 
 def sign_block(size):
@@ -21,35 +22,43 @@
 
 
 def prepare(arrays, rotated, group_size, per_device, head_dim):
-    tokens = arrays[0].shape[0]
-    width = per_device * head_dim
+    tokens, width = arrays[0].shape
+    count = len(arrays)
+    step = tokens // 2
     scale = 1.0 / math.sqrt(head_dim)
 
     def kernel(*refs):
-        out_ref = refs[-1]
-        signs = sign_block(head_dim)
-        for index, ref in enumerate(refs[:-1]):
-            for head in range(per_device):
-                block = ref[:, head * head_dim : (head + 1) * head_dim]
-                if rotated[index]:
-                    turned = jnp.dot(block, signs, preferred_element_type=jnp.float32)
-                    block = (turned * scale).astype(jnp.bfloat16)
-                out_ref[0, index, head] = block
-
-    count = len(arrays)
+        out_ref, sign_ref = refs[-2:]
+
+        @pl.when(pl.program_id(0) == 0)
+        def _():
+            sign_ref[...] = sign_block(head_dim)
+
+        for index, ref in enumerate(refs[:-2]):
+            for group in range(group_size):
+                for head in range(per_device):
+                    column = (group * per_device + head) * head_dim
+                    block = ref[:, column : column + head_dim]
+                    if rotated[index]:
+                        turned = jnp.dot(block, sign_ref[...], preferred_element_type=jnp.float32)
+                        block = (turned * scale).astype(jnp.bfloat16)
+                    out_ref[group, index, head] = block
+
     return pl.pallas_call(
         kernel,
-        grid=(group_size,),
-        in_specs=[pl.BlockSpec((tokens, width), lambda g: (0, g))] * count,
+        grid=(tokens // step,),
+        in_specs=[pl.BlockSpec((step, width), lambda g: (g, 0))] * count,
         out_specs=pl.BlockSpec(
-            (1, count, per_device, tokens, head_dim), lambda g: (g, 0, 0, 0, 0)
+            (group_size, count, per_device, step, head_dim), lambda g: (0, 0, 0, g, 0)
         ),
         out_shape=jax.ShapeDtypeStruct(
             (group_size, count, per_device, tokens, head_dim), jnp.bfloat16
         ),
+        scratch_shapes=[pltpu.VMEM((head_dim, head_dim), jnp.bfloat16)],
+        compiler_params=pltpu.CompilerParams(vmem_limit_bytes=VMEM_BYTES),
         cost_estimate=pl.CostEstimate(
-            flops=2 * tokens * width * group_size * head_dim * sum(rotated),
-            bytes_accessed=4 * tokens * width * group_size * count,
+            flops=2 * tokens * width * head_dim * sum(rotated),
+            bytes_accessed=4 * tokens * width * count,
             transcendentals=0,
         ),
     )(*arrays)
@@ -94,29 +103,35 @@
         first_head = place_ref[0]
         first_tile = place_ref[1]
 
-        for head in range(heads):
+        @pl.loop(0, heads)
+        def _(head):
             for copy in copies(head):
                 copy.wait()
             key_rows = key_buf.at[head].reshape(span_rows, head_dim)
             value_rows = value_buf.at[head].reshape(span_rows, head_dim)
             query_rows = query_buf.at[head].reshape(rows, head_dim)
             row = first_head + head
-
-            @pl.loop(0, tiles_here)
-            def _(tile):
-                limit = counts_ref[row, tile]
-                token = pl.multiple_of(tile * tile_len, tile_len)
-
-                def place_of(slot):
+            column = pl.ds(pl.multiple_of(head * head_dim, head_dim), head_dim)
+
+            @pl.loop(0, tiles_here // GROUP)
+            def _(group):
+                tiles = [group * GROUP + member for member in range(GROUP)]
+                limits = [counts_ref[row, tile] for tile in tiles]
+                most = limits[0]
+                for limit in limits[1:]:
+                    most = jnp.maximum(most, limit)
+
+                def place_of(tile, slot):
                     at = listed_ref[row, tile * slots + slot] - first_tile
                     at = jnp.clip(at, 0, span_tiles - 1)
                     return pl.ds(pl.multiple_of(at * tile_len, tile_len), tile_len)
 
-                def work(used):
+                def first_part(tile, limit, used):
+                    token = pl.multiple_of(tile * tile_len, tile_len)
                     query_now = query_rows[pl.ds(token, tile_len), :]
                     scores = []
                     peak = None
-                    places = [place_of(slot) for slot in range(used)]
+                    places = [place_of(tile, slot) for slot in range(used)]
                     for slot in range(0, used, 2):
                         keys_now = jnp.concatenate(
                             [key_rows[places[slot], :], key_rows[places[slot + 1], :]], axis=0
@@ -126,15 +141,19 @@
                             preferred_element_type=jnp.float32,
                         )
                         one, two = pair[:, :tile_len], pair[:, tile_len:]
-                        if slot + 2 >= used:
-                            two = jnp.where(limit >= used, two, -jnp.inf)
+                        if slot > 0:
+                            one = jnp.where(limit > slot, one, -jnp.inf)
+                        two = jnp.where(limit > slot + 1, two, -jnp.inf)
                         scores += [one, two]
                         larger = jnp.maximum(one, two)
                         peak = larger if peak is None else jnp.maximum(peak, larger)
-                    peak = jnp.max(peak, axis=1, keepdims=True)
+                    return places, scores, jnp.max(peak, axis=1, keepdims=True)
+
+                def second_part(tile, places, scores, peak):
+                    token = pl.multiple_of(tile * tile_len, tile_len)
                     total = None
                     mixed = None
-                    for slot in range(0, used, 2):
+                    for slot in range(0, len(places), 2):
                         one = jnp.exp2((scores[slot] - peak) * factor)
                         two = jnp.exp2((scores[slot + 1] - peak) * factor)
                         both = one + two
@@ -148,14 +167,14 @@
                         update = jnp.dot(weights, values_now, preferred_element_type=jnp.float32)
                         mixed = update if mixed is None else mixed + update
                     total = jnp.sum(total, axis=1, keepdims=True)
-                    out_ref[pl.ds(token, tile_len), head * head_dim : (head + 1) * head_dim] = (
-                        mixed / total
-                    ).astype(jnp.bfloat16)
+                    out_ref[pl.ds(token, tile_len), column] = (mixed / total).astype(jnp.bfloat16)
 
                 for used in range(2, slots + 1, 2):
-                    @pl.when((limit + 1) // 2 == used // 2)
+                    @pl.when((most + 1) // 2 == used // 2)
                     def _():
-                        work(used)
+                        parts = [first_part(t, limit, used) for t, limit in zip(tiles, limits)]
+                        for tile, part in zip(tiles, parts):
+                            second_part(tile, *part)
 
     smem = pl.BlockSpec(memory_space=pltpu.SMEM)
     hbm = pl.BlockSpec(memory_space=pl.ANY)

time: 193 us -> 182 us (0.943)
  Pallas kernels: 33.3 us -> 14.9 us
  waiting for transfers between devices: 92.1 us -> 96.2 us
  blocking collectives: 39.4 us -> 43.5 us
    pallas_call x1, Pallas kernels: 20.6 us -> 8.95 us  [attend(): pl.pallas_call(kernel, in_specs=[smem, smem, smem, hbm, hbm, hbm, hbm], o...]
    pallas_call x2, Pallas kernels: 12.7 us -> 5.92 us  [prepare(): pl.pallas_call(kernel, grid=(tokens // step,), in_specs=[pl.BlockSpec((st...]
    all_to_all x2, waiting for transfers between devices: 69.1 us -> 73.3 us  [exchange(): lax.all_to_all(array, 'head', split_axis=0, concat_axis=0, tiled=True)]
    all_to_all x1, blocking collectives: 39.4 us -> 43.5 us  [exchange(): lax.all_to_all(array, 'head', split_axis=0, concat_axis=0, tiled=True)]
  transfers between devices with their start and end apart: 4 -> 4, of which waited for: 3 -> 3; matrix products, arithmetic and copies ran while one was open for 3% -> 3% of each run, Pallas kernels for 3% -> 2%
where the time goes in v2:
time: 182 us; the launch traced here: 181 us
  waiting for transfers between devices  96.2 us (53%)
  blocking collectives  43.5 us (24%)
  starting transfers between devices  19.5 us (11%)
  Pallas kernels  14.9 us (8%)
  local copies, waits for them, and re-layouts  6.24 us (3%)
    all_to_all x2, waiting for transfers between devices, exchange(): lax.all_to_all(array, 'head', split_axis=0, concat_axis=0, tiled=True)  73.3 us
    all_to_all x1, blocking collectives, exchange(): lax.all_to_all(array, 'head', split_axis=0, concat_axis=0, tiled=True)  43.5 us
    ppermute x1, waiting for transfers between devices, body(): left = lax.ppermute(own[group_size - half:], 'seq', up)  22.9 us
    all_to_all x2, starting transfers between devices, exchange(): lax.all_to_all(array, 'head', split_axis=0, concat_axis=0, tiled=True)  10.7 us
    pallas_call x1, Pallas kernels, attend(): pl.pallas_call(kernel, in_specs=[smem, smem, smem, hbm, hbm, hbm, hbm], o...  8.95 us
    pallas_call x2, Pallas kernels, prepare(): pl.pallas_call(kernel, grid=(tokens // step,), in_specs=[pl.BlockSpec((st...  5.92 us
    ppermute x1, starting transfers between devices, body(): right = lax.ppermute(own[:half], 'seq', down)  5.45 us
  transfers between devices with their start and end apart: 4, of which 3 were waited for; matrix products, arithmetic and copies ran while one was open for 3% of the time, Pallas kernels for 2%

profile of v2, /device:TPU:448, one launch (start us, length us, event | category | flops | bytes accessed | tf_op | source)
XLA Modules:
  0.0 181.1 jit_solution(13757710394263929407)
XLA Ops:
  0.0 3.2 %shard_map.55 = bf16[8,2,3,192,128]{4,3,2,1,0:T(8,128)(2,1)} custom-call(bf16[192,3072]{1,0:T(8,128)(2,1)} %refs_0_.2, bf16[192,3072]{1,0:T(8,128)(2,1)} %refs_1_.1), custom_call_target="tpu_custom_call" | custom-call | flops 150994944 | bytes 4718592 | tf_op jit(solution)/shard_map/pallas_call | solution.py:47
  3.2 7.1 %all-to-all-start = ((bf16[8,2,3,192,128]{4,3,2,1,0:T(8,128)(2,1)}), bf16[8,2,3,192,128]{4,3,2,1,0:T(8,128)(2,1)S(1)}, u32[]{:S(2)}, u32[]{:S(2)}) async-start(bf16[8,2,3,192,128]{4,3,2,1,0:T(8,128)(2,1)} %shard_map.55), calls=%async_computation | async-start | bytes 4718592 | tf_op jit(solution)/shard_map/all_to_all | solution.py:214
  10.3 2.7 %shard_map.56 = bf16[8,1,3,192,128]{4,3,2,1,0:T(8,128)(2,1)} custom-call(bf16[192,3072]{1,0:T(8,128)(2,1)} %refs_0_.3), custom_call_target="tpu_custom_call" | custom-call | flops 150994944 | bytes 2359296 | tf_op jit(solution)/shard_map/pallas_call | solution.py:47
  13.0 54.3 %all-to-all-done.own_ref = bf16[8,2,3,192,128]{4,3,2,1,0:T(8,128)(2,1)S(1)} async-done(((bf16[8,2,3,192,128]{4,3,2,1,0:T(8,128)(2,1)}), bf16[8,2,3,192,128]{4,3,2,1,0:T(8,128)(2,1)S(1)}, u32[]{:S(2)}, u32[]{:S(2)}) %all-to-all-start) | async-done | bytes 2359328 | tf_op jit(solution)/shard_map/all_to_all | solution.py:214
  67.3 0.0 copy-start
  67.3 3.6 %all-to-all-start.1 = ((bf16[8,1,3,192,128]{4,3,2,1,0:T(8,128)(2,1)}), bf16[8,1,3,192,128]{4,3,2,1,0:T(8,128)(2,1)S(1)}, u32[]{:S(2)}, u32[]{:S(2)}) async-start(bf16[8,1,3,192,128]{4,3,2,1,0:T(8,128)(2,1)} %shard_map.56), calls=%async_computation.1 | async-start | bytes 2359296 | tf_op jit(solution)/shard_map/all_to_all | solution.py:214
  70.9 0.0 copy-start.2
  70.9 1.7 fusion
  72.6 0.0 copy-done
  72.6 3.4 %collective-permute-start = (bf16[4,2,3,192,128]{4,3,2,1,0:T(8,128)(2,1)}, bf16[4,2,3,192,128]{4,3,2,1,0:T(8,128)(2,1)S(1)}, u32[]{:S(2)}, u32[]{:S(2)}) collective-permute-start(bf16[4,2,3,192,128]{4,3,2,1,0:T(8,128)(2,1)} %get-tuple-element.6), channel_id=1, source_target_pairs={{0,8},{8,16},{16,24},{24,32},{32,40},{40,48},{48,56},{56,64},{64,7... | collective-permute-start | bytes 3538952 | tf_op jit(solution)/shard_map/ppermute | solution.py:222
  76.0 5.4 %collective-permute-start.1 = (bf16[4,2,3,192,128]{4,3,2,1,0:T(8,128)(2,1)}, bf16[4,2,3,192,128]{4,3,2,1,0:T(8,128)(2,1)}, u32[]{:S(2)}, u32[]{:S(2)}) collective-permute-start(bf16[4,2,3,192,128]{4,3,2,1,0:T(8,128)(2,1)} %get-tuple-element.5), channel_id=1, source_target_pairs={{8,0},{16,8},{24,16},{32,24},{40,32},{48,40},{56,48},{64,56},{72,6... | collective-permute-start | bytes 3538952 | tf_op jit(solution)/shard_map/ppermute | solution.py:223
  81.5 0.9 reshape.9
  82.4 0.7 copy.9.listed_ref
  83.1 0.0 copy-done.2
  83.1 0.7 copy.10.counts_ref
  83.8 0.7 pad_add_fusion.place_ref
  84.4 19.0 %all-to-all-done.1.query_ref = bf16[8,1,3,192,128]{4,3,2,1,0:T(8,128)(2,1)S(1)} async-done(((bf16[8,1,3,192,128]{4,3,2,1,0:T(8,128)(2,1)}), bf16[8,1,3,192,128]{4,3,2,1,0:T(8,128)(2,1)S(1)}, u32[]{:S(2)}, u32[]{:S(2)}) %all-to-all-start.1) | async-done | bytes 1179680 | tf_op jit(solution)/shard_map/all_to_all | solution.py:214
  103.4 0.0 copy-start.1
  103.4 22.9 %collective-permute-done.left_ref = bf16[4,2,3,192,128]{4,3,2,1,0:T(8,128)(2,1)S(1)} collective-permute-done((bf16[4,2,3,192,128]{4,3,2,1,0:T(8,128)(2,1)}, bf16[4,2,3,192,128]{4,3,2,1,0:T(8,128)(2,1)S(1)}, u32[]{:S(2)}, u32[]{:S(2)}) %collective-permute-start) | collective-permute-done | bytes 1179680 | tf_op jit(solution)/shard_map/ppermute | solution.py:222
  126.4 0.0 copy-start.3
  126.4 0.0 collective-permute-done.1.right_ref
  126.4 0.0 copy-done.1
  126.4 1.1 copy-done.3
  127.4 8.9 %shard_map.57 = bf16[1536,384]{1,0:T(8,128)(2,1)} custom-call(s32[2]{0:T(128)} %pad_add_fusion.place_ref, s32[24,144]{1,0:T(8,128)} %copy.9.listed_ref, s32[24,12]{1,0:T(8,128)} %copy.10.counts_ref, bf16[8,2,3,192,128]{4,3,2,1,0:T(8,128)(2,1)} %copy-done, bf16[4,2,3,192,128]{4,3,2,1,0:T(8,128)(2,1)} %copy-done.3, ...), custom_call_target="tpu_custom_call" | custom-call | flops 3623878656 | bytes 7077888 | tf_op jit(solution)/shard_map/pallas_call | solution.py:182
  136.4 43.5 %all_to_all.15 = bf16[8,192,384]{2,1,0:T(8,128)(2,1)S(1)} all-to-all(bf16[8,192,384]{2,1,0:T(8,128)(2,1)} %bitcast.9), channel_id=1, replica_groups=mesh['seq'=64,'head'=8] {'head'}, dimensions={0} | all-to-all | bytes 2359296 | tf_op jit(solution)/shard_map/all_to_all | solution.py:214
  179.9 1.2 copy.12
Async XLA Ops:
  3.2 64.1 %all-to-all-start = ((bf16[8,2,3,192,128]{4,3,2,1,0:T(8,128)(2,1)}), bf16[8,2,3,192,128]{4,3,2,1,0:T(8,128)(2,1)S(1)}, u32[]{:S(2)}, u32[]{:S(2)}) async-start(bf16[8,2,3,192,128]{4,3,2,1,0:T(8,128)(2,1)} %shard_map.55), calls=%async_computation | async-start | bytes 4718592 | tf_op jit(solution)/shard_map/all_to_all | solution.py:214
  67.3 5.3 %copy-start = (bf16[8,2,3,192,128]{4,3,2,1,0:T(8,128)(2,1)}, bf16[8,2,3,192,128]{4,3,2,1,0:T(8,128)(2,1)S(1)}, u32[]{:S(2)}) copy-start(bf16[8,2,3,192,128]{4,3,2,1,0:T(8,128)(2,1)S(1)} %all-to-all-done.own_ref) | copy-start | bytes 7077892
  67.3 36.1 %all-to-all-start.1 = ((bf16[8,1,3,192,128]{4,3,2,1,0:T(8,128)(2,1)}), bf16[8,1,3,192,128]{4,3,2,1,0:T(8,128)(2,1)S(1)}, u32[]{:S(2)}, u32[]{:S(2)}) async-start(bf16[8,1,3,192,128]{4,3,2,1,0:T(8,128)(2,1)} %shard_map.56), calls=%async_computation.1 | async-start | bytes 2359296 | tf_op jit(solution)/shard_map/all_to_all | solution.py:214
  70.9 12.2 %copy-start.2 = (s32[24,12]{0,1:T(8,128)S(1)}, s32[24,12]{0,1:T(8,128)}, u32[]{:S(2)}) copy-start(s32[24,12]{0,1:T(8,128)} %param.9) | copy-start | bytes 3460
  72.6 53.8 %collective-permute-start = (bf16[4,2,3,192,128]{4,3,2,1,0:T(8,128)(2,1)}, bf16[4,2,3,192,128]{4,3,2,1,0:T(8,128)(2,1)S(1)}, u32[]{:S(2)}, u32[]{:S(2)}) collective-permute-start(bf16[4,2,3,192,128]{4,3,2,1,0:T(8,128)(2,1)} %get-tuple-element.6), channel_id=1, source_target_pairs={{0,8},{8,16},{16,24},{24,32},{32,40},{40,48},{48,56},{56,64},{64,7... | collective-permute-start | bytes 3538952 | tf_op jit(solution)/shard_map/ppermute | solution.py:222
  76.0 50.3 %collective-permute-start.1 = (bf16[4,2,3,192,128]{4,3,2,1,0:T(8,128)(2,1)}, bf16[4,2,3,192,128]{4,3,2,1,0:T(8,128)(2,1)}, u32[]{:S(2)}, u32[]{:S(2)}) collective-permute-start(bf16[4,2,3,192,128]{4,3,2,1,0:T(8,128)(2,1)} %get-tuple-element.5), channel_id=1, source_target_pairs={{8,0},{16,8},{24,16},{32,24},{40,32},{48,40},{56,48},{64,56},{72,6... | collective-permute-start | bytes 3538952 | tf_op jit(solution)/shard_map/ppermute | solution.py:223
  103.4 23.0 %copy-start.1 = (bf16[8,1,3,192,128]{4,3,2,1,0:T(8,128)(2,1)}, bf16[8,1,3,192,128]{4,3,2,1,0:T(8,128)(2,1)S(1)}, u32[]{:S(2)}) copy-start(bf16[8,1,3,192,128]{4,3,2,1,0:T(8,128)(2,1)S(1)} %all-to-all-done.1.query_ref) | copy-start | bytes 3538948
  126.4 1.1 copy-start.3

commit v3 on v2

--- a/solution.py
+++ b/solution.py
@@ -9,6 +9,7 @@
 
 VMEM_BYTES = 60 * 1024 * 1024
 GROUP = 6
+ROW = 4
 
 
 def sign_block(size):
@@ -21,6 +22,19 @@
     return (1 - 2 * jnp.bitwise_and(parity, 1)).astype(jnp.float32).astype(jnp.bfloat16)
 
 
+def odd_row(block):
+    return (block // ROW) % 2
+
+
+def owner_block(member, odd, group_size):
+    return ((member // 2 + (member % 2) * odd) % (group_size // 2)) * 2 + member % 2
+
+
+def owner_of(block, head_block, group_size):
+    shift = (head_block % 2) * odd_row(block)
+    return ((head_block // 2 - shift) % (group_size // 2)) * 2 + head_block % 2
+
+
 def prepare(arrays, rotated, group_size, per_device, head_dim):
     tokens, width = arrays[0].shape
     count = len(arrays)
@@ -34,11 +48,13 @@
         def _():
             sign_ref[...] = sign_block(head_dim)
 
+        odd = odd_row(lax.axis_index("seq"))
         for index, ref in enumerate(refs[:-2]):
             for group in range(group_size):
+                first = owner_block(group, odd, group_size) * per_device
                 for head in range(per_device):
-                    column = (group * per_device + head) * head_dim
-                    block = ref[:, column : column + head_dim]
+                    column = pl.multiple_of((first + head) * head_dim, head_dim)
+                    block = ref[:, pl.ds(column, head_dim)]
                     if rotated[index]:
                         turned = jnp.dot(block, sign_ref[...], preferred_element_type=jnp.float32)
                         block = (turned * scale).astype(jnp.bfloat16)
@@ -199,6 +215,29 @@
     )(place, listed, counts, own, left, right, query)
 
 
+def assemble(parts):
+    members, tokens, width = parts.shape
+    step = tokens // 2
+
+    def kernel(parts_ref, out_ref):
+        odd = odd_row(lax.axis_index("seq"))
+        for member in range(members):
+            column = pl.multiple_of(owner_block(member, odd, members) * width, width)
+            out_ref[:, pl.ds(column, width)] = parts_ref[member]
+
+    return pl.pallas_call(
+        kernel,
+        grid=(tokens // step,),
+        in_specs=[pl.BlockSpec((members, step, width), lambda g: (0, g, 0))],
+        out_specs=pl.BlockSpec((step, members * width), lambda g: (g, 0)),
+        out_shape=jax.ShapeDtypeStruct((tokens, members * width), parts.dtype),
+        compiler_params=pltpu.CompilerParams(vmem_limit_bytes=VMEM_BYTES),
+        cost_estimate=pl.CostEstimate(
+            flops=0, bytes_accessed=4 * tokens * members * width, transcendentals=0
+        ),
+    )(parts)
+
+
 def body(queries, keys, values, neighbours, counts):
     group_size = lax.axis_size("head")
     blocks = lax.axis_size("seq")
@@ -217,20 +256,27 @@
     own = exchange(packed)
     packed = prepare([queries], [True], group_size, per_device, head_dim)
     query = exchange(packed)
-    up = [(i, i + 1) for i in range(blocks - 1)]
-    down = [(i + 1, i) for i in range(blocks - 1)]
-    left = lax.ppermute(own[group_size - half :], "seq", up)
-    right = lax.ppermute(own[:half], "seq", down)
+    up = [
+        tuple(
+            at * group_size + owner_of(at, head_block, group_size) for at in (block, block + 1)
+        )
+        for block in range(blocks - 1)
+        for head_block in range(group_size)
+    ]
+    down = [(there, here) for here, there in up]
+    left = lax.ppermute(own[group_size - half :], ("seq", "head"), up)
+    right = lax.ppermute(own[:half], ("seq", "head"), down)
+    row_is_odd = odd_row(lax.axis_index("seq"))
     place = jnp.stack(
         [
-            lax.axis_index("head") * per_device,
+            owner_block(lax.axis_index("head"), row_is_odd, group_size) * per_device,
             lax.axis_index("seq") * tiles_here - halo_tiles,
         ]
     ).astype(jnp.int32)
     listed = neighbours.reshape(head_count, -1)
     result = attend(own, left, right, query, listed, counts, place, tile_len)
     result = exchange(result.reshape(group_size, local_tokens, per_device * head_dim))
-    return jnp.moveaxis(result, 0, 1).reshape(local_tokens, feature_width)
+    return assemble(result)
 
 
 def solution(mesh):

time: 182 us -> 180 us (0.989)
  blocking collectives: 43.5 us -> 41.6 us
    pallas_call x0 -> x1, Pallas kernels: none -> 2.14 us  [assemble(): pl.pallas_call(kernel, grid=(tokens // step,), in_specs=[pl.BlockSpec((me...]
    all_to_all x1, blocking collectives: 43.5 us -> 41.6 us  [exchange(): lax.all_to_all(array, 'head', split_axis=0, concat_axis=0, tiled=True)]
where the time goes in v3:
time: 180 us
  waiting for transfers between devices  96.2 us (53%)
  blocking collectives  41.6 us (23%)
  starting transfers between devices  19.5 us (11%)
  Pallas kernels  16.3 us (9%)
  local copies, waits for them, and re-layouts  5.03 us (3%)
    all_to_all x2, waiting for transfers between devices, exchange(): lax.all_to_all(array, 'head', split_axis=0, concat_axis=0, tiled=True)  72.9 us
    all_to_all x1, blocking collectives, exchange(): lax.all_to_all(array, 'head', split_axis=0, concat_axis=0, tiled=True)  41.6 us
    ppermute x1, waiting for transfers between devices, body(): left = lax.ppermute(own[group_size - half:], ('seq', 'head'), up)  23.3 us
    all_to_all x2, starting transfers between devices, exchange(): lax.all_to_all(array, 'head', split_axis=0, concat_axis=0, tiled=True)  10.7 us
    pallas_call x1, Pallas kernels, attend(): pl.pallas_call(kernel, in_specs=[smem, smem, smem, hbm, hbm, hbm, hbm], o...  8.3 us
    pallas_call x2, Pallas kernels, prepare(): pl.pallas_call(kernel, grid=(tokens // step,), in_specs=[pl.BlockSpec((st...  5.91 us
    ppermute x1, starting transfers between devices, body(): right = lax.ppermute(own[:half], ('seq', 'head'), down)  5.42 us
  transfers between devices with their start and end apart: 4, of which 3 were waited for; matrix products, arithmetic and copies ran while one was open for 3% of the time, Pallas kernels for 2%

profile of v3, /device:TPU:448, one launch (start us, length us, event | category | flops | bytes accessed | tf_op | source)
XLA Modules:
  0.0 179.5 jit_solution(2829543957708844075)
XLA Ops:
  0.0 3.2 %shard_map.55 = bf16[8,2,3,192,128]{4,3,2,1,0:T(8,128)(2,1)} custom-call(bf16[192,3072]{1,0:T(8,128)(2,1)} %refs_0_.2, bf16[192,3072]{1,0:T(8,128)(2,1)} %refs_1_.1), custom_call_target="tpu_custom_call" | custom-call | flops 150994944 | bytes 4718592 | tf_op jit(solution)/shard_map/pallas_call | solution.py:63
  3.2 7.1 %all-to-all-start = ((bf16[8,2,3,192,128]{4,3,2,1,0:T(8,128)(2,1)}), bf16[8,2,3,192,128]{4,3,2,1,0:T(8,128)(2,1)S(1)}, u32[]{:S(2)}, u32[]{:S(2)}) async-start(bf16[8,2,3,192,128]{4,3,2,1,0:T(8,128)(2,1)} %shard_map.55), calls=%async_computation | async-start | bytes 4718592 | tf_op jit(solution)/shard_map/all_to_all | solution.py:253
  10.3 2.8 %shard_map.56 = bf16[8,1,3,192,128]{4,3,2,1,0:T(8,128)(2,1)} custom-call(bf16[192,3072]{1,0:T(8,128)(2,1)} %refs_0_.3), custom_call_target="tpu_custom_call" | custom-call | flops 150994944 | bytes 2359296 | tf_op jit(solution)/shard_map/pallas_call | solution.py:63
  13.0 54.3 %all-to-all-done.own_ref = bf16[8,2,3,192,128]{4,3,2,1,0:T(8,128)(2,1)S(1)} async-done(((bf16[8,2,3,192,128]{4,3,2,1,0:T(8,128)(2,1)}), bf16[8,2,3,192,128]{4,3,2,1,0:T(8,128)(2,1)S(1)}, u32[]{:S(2)}, u32[]{:S(2)}) %all-to-all-start) | async-done | bytes 2359328 | tf_op jit(solution)/shard_map/all_to_all | solution.py:253
  67.3 0.0 copy-start
  67.3 3.6 %all-to-all-start.1 = ((bf16[8,1,3,192,128]{4,3,2,1,0:T(8,128)(2,1)}), bf16[8,1,3,192,128]{4,3,2,1,0:T(8,128)(2,1)S(1)}, u32[]{:S(2)}, u32[]{:S(2)}) async-start(bf16[8,1,3,192,128]{4,3,2,1,0:T(8,128)(2,1)} %shard_map.56), calls=%async_computation.1 | async-start | bytes 2359296 | tf_op jit(solution)/shard_map/all_to_all | solution.py:253
  70.9 0.0 copy-start.2
  70.9 1.7 fusion
  72.6 0.0 copy-done
  72.6 3.4 %collective-permute-start = (bf16[4,2,3,192,128]{4,3,2,1,0:T(8,128)(2,1)}, bf16[4,2,3,192,128]{4,3,2,1,0:T(8,128)(2,1)S(1)}, u32[]{:S(2)}, u32[]{:S(2)}) collective-permute-start(bf16[4,2,3,192,128]{4,3,2,1,0:T(8,128)(2,1)} %get-tuple-element.6), channel_id=1, source_target_pairs={{0,8},{1,9},{2,10},{3,11},{4,12},{5,13},{6,14},{7,15},{8,16},{9,17... | collective-permute-start | bytes 3538952 | tf_op jit(solution)/shard_map/ppermute | solution.py:267
  76.0 5.4 %collective-permute-start.1 = (bf16[4,2,3,192,128]{4,3,2,1,0:T(8,128)(2,1)}, bf16[4,2,3,192,128]{4,3,2,1,0:T(8,128)(2,1)}, u32[]{:S(2)}, u32[]{:S(2)}) collective-permute-start(bf16[4,2,3,192,128]{4,3,2,1,0:T(8,128)(2,1)} %get-tuple-element.5), channel_id=1, source_target_pairs={{8,0},{9,1},{10,2},{11,3},{12,4},{13,5},{14,6},{15,7},{16,8},{17,9... | collective-permute-start | bytes 3538952 | tf_op jit(solution)/shard_map/ppermute | solution.py:268
  81.5 0.9 reshape.6
  82.4 0.7 copy.8.listed_ref
  83.1 0.0 copy-done.2
  83.1 0.7 copy.9.counts_ref
  83.8 0.7 pad_add_fusion.place_ref
  84.4 18.6 %all-to-all-done.1.query_ref = bf16[8,1,3,192,128]{4,3,2,1,0:T(8,128)(2,1)S(1)} async-done(((bf16[8,1,3,192,128]{4,3,2,1,0:T(8,128)(2,1)}), bf16[8,1,3,192,128]{4,3,2,1,0:T(8,128)(2,1)S(1)}, u32[]{:S(2)}, u32[]{:S(2)}) %all-to-all-start.1) | async-done | bytes 1179680 | tf_op jit(solution)/shard_map/all_to_all | solution.py:253
  103.1 0.0 copy-start.1
  103.1 23.3 %collective-permute-done.left_ref = bf16[4,2,3,192,128]{4,3,2,1,0:T(8,128)(2,1)S(1)} collective-permute-done((bf16[4,2,3,192,128]{4,3,2,1,0:T(8,128)(2,1)}, bf16[4,2,3,192,128]{4,3,2,1,0:T(8,128)(2,1)S(1)}, u32[]{:S(2)}, u32[]{:S(2)}) %collective-permute-start) | collective-permute-done | bytes 1179680 | tf_op jit(solution)/shard_map/ppermute | solution.py:267
  126.4 0.0 copy-start.3
  126.4 0.0 collective-permute-done.1.right_ref
  126.4 0.0 copy-done.1
  126.4 1.1 copy-done.3
  127.4 8.3 %shard_map.57 = bf16[1536,384]{1,0:T(8,128)(2,1)} custom-call(s32[2]{0:T(128)} %pad_add_fusion.place_ref, s32[24,144]{1,0:T(8,128)} %copy.8.listed_ref, s32[24,12]{1,0:T(8,128)} %copy.9.counts_ref, bf16[8,2,3,192,128]{4,3,2,1,0:T(8,128)(2,1)} %copy-done, bf16[4,2,3,192,128]{4,3,2,1,0:T(8,128)(2,1)} %copy-done.3, ...), custom_call_target="tpu_custom_call" | custom-call | flops 3623878656 | bytes 7077888 | tf_op jit(solution)/shard_map/pallas_call | solution.py:198
  135.7 41.6 %all_to_all.15.parts_ref = bf16[8,192,384]{2,1,0:T(8,128)(2,1)} all-to-all(bf16[8,192,384]{2,1,0:T(8,128)(2,1)} %bitcast.5), channel_id=1, replica_groups=mesh['seq'=64,'head'=8] {'head'}, dimensions={0} | all-to-all | bytes 2359296 | tf_op jit(solution)/shard_map/all_to_all | solution.py:253
  177.4 2.1 %shard_map.58 = bf16[192,3072]{1,0:T(8,128)(2,1)} custom-call(bf16[8,192,384]{2,1,0:T(8,128)(2,1)} %all_to_all.15.parts_ref), custom_call_target="tpu_custom_call" | custom-call | bytes 2359296 | tf_op jit(solution)/shard_map/pallas_call | solution.py:228
Async XLA Ops:
  3.2 64.2 %all-to-all-start = ((bf16[8,2,3,192,128]{4,3,2,1,0:T(8,128)(2,1)}), bf16[8,2,3,192,128]{4,3,2,1,0:T(8,128)(2,1)S(1)}, u32[]{:S(2)}, u32[]{:S(2)}) async-start(bf16[8,2,3,192,128]{4,3,2,1,0:T(8,128)(2,1)} %shard_map.55), calls=%async_computation | async-start | bytes 4718592 | tf_op jit(solution)/shard_map/all_to_all | solution.py:253
  67.3 5.3 %copy-start = (bf16[8,2,3,192,128]{4,3,2,1,0:T(8,128)(2,1)}, bf16[8,2,3,192,128]{4,3,2,1,0:T(8,128)(2,1)S(1)}, u32[]{:S(2)}) copy-start(bf16[8,2,3,192,128]{4,3,2,1,0:T(8,128)(2,1)S(1)} %all-to-all-done.own_ref) | copy-start | bytes 7077892
  67.3 35.8 %all-to-all-start.1 = ((bf16[8,1,3,192,128]{4,3,2,1,0:T(8,128)(2,1)}), bf16[8,1,3,192,128]{4,3,2,1,0:T(8,128)(2,1)S(1)}, u32[]{:S(2)}, u32[]{:S(2)}) async-start(bf16[8,1,3,192,128]{4,3,2,1,0:T(8,128)(2,1)} %shard_map.56), calls=%async_computation.1 | async-start | bytes 2359296 | tf_op jit(solution)/shard_map/all_to_all | solution.py:253
  70.9 12.2 %copy-start.2 = (s32[24,12]{0,1:T(8,128)S(1)}, s32[24,12]{0,1:T(8,128)}, u32[]{:S(2)}) copy-start(s32[24,12]{0,1:T(8,128)} %param.9) | copy-start | bytes 3460
  72.6 53.8 %collective-permute-start = (bf16[4,2,3,192,128]{4,3,2,1,0:T(8,128)(2,1)}, bf16[4,2,3,192,128]{4,3,2,1,0:T(8,128)(2,1)S(1)}, u32[]{:S(2)}, u32[]{:S(2)}) collective-permute-start(bf16[4,2,3,192,128]{4,3,2,1,0:T(8,128)(2,1)} %get-tuple-element.6), channel_id=1, source_target_pairs={{0,8},{1,9},{2,10},{3,11},{4,12},{5,13},{6,14},{7,15},{8,16},{9,17... | collective-permute-start | bytes 3538952 | tf_op jit(solution)/shard_map/ppermute | solution.py:267
  76.0 50.3 %collective-permute-start.1 = (bf16[4,2,3,192,128]{4,3,2,1,0:T(8,128)(2,1)}, bf16[4,2,3,192,128]{4,3,2,1,0:T(8,128)(2,1)}, u32[]{:S(2)}, u32[]{:S(2)}) collective-permute-start(bf16[4,2,3,192,128]{4,3,2,1,0:T(8,128)(2,1)} %get-tuple-element.5), channel_id=1, source_target_pairs={{8,0},{9,1},{10,2},{11,3},{12,4},{13,5},{14,6},{15,7},{16,8},{17,9... | collective-permute-start | bytes 3538952 | tf_op jit(solution)/shard_map/ppermute | solution.py:268
  103.1 23.3 %copy-start.1 = (bf16[8,1,3,192,128]{4,3,2,1,0:T(8,128)(2,1)}, bf16[8,1,3,192,128]{4,3,2,1,0:T(8,128)(2,1)S(1)}, u32[]{:S(2)}) copy-start(bf16[8,1,3,192,128]{4,3,2,1,0:T(8,128)(2,1)S(1)} %all-to-all-done.1.query_ref) | copy-start | bytes 3538948
  126.4 1.1 copy-start.3

commit v4 on v2

v4 whole, which is shorter than its diff:
```python
import math

import jax
import jax.numpy as jnp
from jax import lax
from jax.experimental import pallas as pl
from jax.experimental.pallas import tpu as pltpu
from jax.sharding import PartitionSpec as P

VMEM_BYTES = 60 * 1024 * 1024
GROUP = 6
HALO_SLOTS = 8


def sign_block(size):
    row = lax.broadcasted_iota(jnp.int32, (size, size), 0)
    column = lax.broadcasted_iota(jnp.int32, (size, size), 1)
    common = jnp.bitwise_and(row, column)
    parity = jnp.zeros((size, size), jnp.int32)
    for bit_level in range(max(size.bit_length() - 1, 1)):
        parity = parity + jnp.bitwise_and(jnp.right_shift(common, bit_level), 1)
    return (1 - 2 * jnp.bitwise_and(parity, 1)).astype(jnp.float32).astype(jnp.bfloat16)


def prepare(arrays, rotated, group_size, per_device, head_dim):
    tokens, width = arrays[0].shape
    count = len(arrays)
    step = tokens // 2
    scale = 1.0 / math.sqrt(head_dim)

    def kernel(*refs):
        out_ref, sign_ref = refs[-2:]

        @pl.when(pl.program_id(0) == 0)
        def _():
            sign_ref[...] = sign_block(head_dim)

        for index, ref in enumerate(refs[:-2]):
            for group in range(group_size):
                for head in range(per_device):
                    column = (group * per_device + head) * head_dim
                    block = ref[:, column : column + head_dim]
                    if rotated[index]:
                        turned = jnp.dot(block, sign_ref[...], preferred_element_type=jnp.float32)
                        block = (turned * scale).astype(jnp.bfloat16)
                    out_ref[group, index, head] = block

    return pl.pallas_call(
        kernel,
        grid=(tokens // step,),
        in_specs=[pl.BlockSpec((step, width), lambda g: (g, 0))] * count,
        out_specs=pl.BlockSpec(
            (group_size, count, per_device, step, head_dim), lambda g: (0, 0, 0, g, 0)
        ),
        out_shape=jax.ShapeDtypeStruct(
            (group_size, count, per_device, tokens, head_dim), jnp.bfloat16
        ),
        scratch_shapes=[pltpu.VMEM((head_dim, head_dim), jnp.bfloat16)],
        compiler_params=pltpu.CompilerParams(vmem_limit_bytes=VMEM_BYTES),
        cost_estimate=pl.CostEstimate(
            flops=2 * tokens * width * head_dim * sum(rotated),
            bytes_accessed=4 * tokens * width * count,
            transcendentals=0,
        ),
    )(*arrays)


def scores_of(query_now, keys_of, limit, first_active):
    scores = []
    largest = None
    for slot in range(0, len(keys_of), 2):
        keys_now = jnp.concatenate([keys_of[slot](), keys_of[slot + 1]()], axis=0)
        pair = lax.dot_general(
            query_now, keys_now, (((1,), (1,)), ((), ())), preferred_element_type=jnp.float32
        )
        half = pair.shape[1] // 2
        one, two = pair[:, :half], pair[:, half:]
        if slot >= first_active:
            one = jnp.where(limit > slot, one, -jnp.inf)
        two = jnp.where(limit > slot + 1, two, -jnp.inf)
        scores += [one, two]
        larger = jnp.maximum(one, two)
        largest = larger if largest is None else jnp.maximum(largest, larger)
    return scores, largest


def mix(scores, level, factor, values_of):
    total = None
    mixed = None
    for slot in range(0, len(scores), 2):
        one = jnp.exp2(scores[slot] * factor - level)
        two = jnp.exp2(scores[slot + 1] * factor - level)
        both = one + two
        total = both if total is None else total + both
        weights = jnp.concatenate([one.astype(jnp.bfloat16), two.astype(jnp.bfloat16)], axis=1)
        values_now = jnp.concatenate([values_of[slot](), values_of[slot + 1]()], axis=0)
        update = jnp.dot(weights, values_now, preferred_element_type=jnp.float32)
        mixed = update if mixed is None else mixed + update
    return jnp.sum(total, axis=1, keepdims=True), mixed


def tile_rows(ref, at, count, tile_len):
    at = jnp.clip(at, 0, count - 1)
    return lambda: ref[pl.ds(pl.multiple_of(at * tile_len, tile_len), tile_len), :]


def attend_local(own, listed, counts, place, tile_len, reach):
    sources, _, heads, tokens, head_dim = own.shape
    rows = sources * tokens
    tiles_here = rows // tile_len
    slots = listed.shape[1] // tiles_here
    factor = math.log2(math.e) / math.sqrt(head_dim)
    group_count = tiles_here // GROUP

    def kernel(place_ref, listed_ref, counts_ref, own_ref, mixed_ref, stats_ref, halo_ref,
               buf, inside_ref, sems):
        def copies(head):
            return [
                pltpu.make_async_copy(
                    own_ref.at[:, index, head], buf.at[index, head], sems.at[head, index]
                )
                for index in range(3)
            ]

        for head in range(heads):
            for copy in copies(head):
                copy.start()
        first_head = place_ref[0]
        first_tile = place_ref[1]
        for member in range(GROUP):
            for slot in range(slots):
                inside_ref[member, slot] = 0

        @pl.loop(0, heads)
        def _(head):
            for copy in copies(head):
                copy.wait()
            key_rows, value_rows, query_rows = [
                buf.at[index, head].reshape(rows, head_dim) for index in range(3)
            ]
            row = first_head + head
            column = pl.ds(pl.multiple_of(head * head_dim, head_dim), head_dim)

            @pl.loop(0, group_count)
            def _(group):
                tiles = [group * GROUP + member for member in range(GROUP)]
                limits = []
                for member, tile in enumerate(tiles):
                    limit = counts_ref[row, tile]
                    line = head * tiles_here + tile
                    inside = jnp.int32(0)
                    outside = jnp.int32(0)
                    for spare in range(HALO_SLOTS):
                        halo_ref[line, spare] = 0
                    for slot in range(slots):
                        at = listed_ref[row, tile * slots + slot] - first_tile
                        active = slot < limit
                        is_inside = (at >= 0) & (at < tiles_here)
                        inside_ref[member, inside] = at
                        halo_ref[line, jnp.minimum(outside, HALO_SLOTS - 2)] = jnp.where(
                            at < 0, at + reach, at - tiles_here + reach
                        )
                        inside = inside + (active & is_inside).astype(jnp.int32)
                        outside = outside + (active & ~is_inside).astype(jnp.int32)
                    halo_ref[line, HALO_SLOTS - 1] = outside
                    limits.append(inside)
                most = limits[0]
                for limit in limits[1:]:
                    most = jnp.maximum(most, limit)

                def work(used):
                    begun = []
                    for member, tile in enumerate(tiles):
                        token = pl.multiple_of(tile * tile_len, tile_len)
                        query_now = query_rows[pl.ds(token, tile_len), :]
                        places = [inside_ref[member, slot] for slot in range(used)]
                        scores, largest = scores_of(
                            query_now,
                            [tile_rows(key_rows, at, tiles_here, tile_len) for at in places],
                            limits[member],
                            1,
                        )
                        begun.append((token, places, scores, jnp.max(largest, axis=1, keepdims=True)))
                    for token, places, scores, peak in begun:
                        total, mixed = mix(
                            scores,
                            peak * factor,
                            factor,
                            [tile_rows(value_rows, at, tiles_here, tile_len) for at in places],
                        )
                        mixed_ref[pl.ds(token, tile_len), column] = mixed / total
                        level = peak * factor + jnp.log2(total)
                        stats_ref[pl.ds(token, tile_len), column] = jnp.broadcast_to(
                            level, (tile_len, head_dim)
                        )

                for used in range(2, slots + 1, 2):
                    @pl.when((most + 1) // 2 == used // 2)
                    def _():
                        work(used)

    smem = pl.BlockSpec(memory_space=pltpu.SMEM)
    vmem = pl.BlockSpec(memory_space=pltpu.VMEM)
    pairs = heads * tiles_here * slots
    state = jax.ShapeDtypeStruct((rows, heads * head_dim), jnp.float32)
    return pl.pallas_call(
        kernel,
        in_specs=[smem, smem, smem, pl.BlockSpec(memory_space=pl.ANY)],
        out_specs=[vmem, vmem, smem],
        out_shape=[state, state, jax.ShapeDtypeStruct((heads * tiles_here, HALO_SLOTS), jnp.int32)],
        scratch_shapes=[
            pltpu.VMEM((3, heads, sources, tokens, head_dim), jnp.bfloat16),
            pltpu.SMEM((GROUP, slots), jnp.int32),
            pltpu.SemaphoreType.DMA((heads, 3)),
        ],
        compiler_params=pltpu.CompilerParams(vmem_limit_bytes=VMEM_BYTES // 3),
        cost_estimate=pl.CostEstimate(
            flops=4 * pairs * tile_len * tile_len * head_dim,
            bytes_accessed=2 * heads * head_dim * 7 * rows,
            transcendentals=pairs * tile_len * tile_len,
        ),
    )(place, listed, counts, own)


def attend_halo(own, left, right, mixed, stats, halo, tile_len):
    sources, _, heads, tokens, head_dim = own.shape
    half = left.shape[0]
    rows = sources * tokens
    halo_rows = 2 * half * tokens
    halo_tiles = halo_rows // tile_len
    tiles_here = rows // tile_len
    factor = math.log2(math.e) / math.sqrt(head_dim)

    def kernel(halo_ref, own_ref, left_ref, right_ref, mixed_ref, stats_ref, out_ref,
               buf, query_buf, sems):
        def copies(head):
            pairs = [(own_ref.at[:, 2, head], query_buf.at[head])]
            for index in range(2):
                pairs.append((left_ref.at[:, index, head], buf.at[index, head, pl.ds(0, half)]))
                pairs.append((right_ref.at[:, index, head], buf.at[index, head, pl.ds(half, half)]))
            return [
                pltpu.make_async_copy(there, here, sems.at[head, number])
                for number, (there, here) in enumerate(pairs)
            ]

        for head in range(heads):
            for copy in copies(head):
                copy.start()

        @pl.loop(0, heads)
        def _(head):
            for copy in copies(head):
                copy.wait()
            key_rows, value_rows = [
                buf.at[index, head].reshape(halo_rows, head_dim) for index in range(2)
            ]
            query_rows = query_buf.at[head].reshape(rows, head_dim)
            column = pl.ds(pl.multiple_of(head * head_dim, head_dim), head_dim)

            @pl.loop(0, tiles_here // 4)
            def _(group):
                last = tiles_here - 1
                tiles = [2 * group, 2 * group + 1, last - 2 * group, last - 1 - 2 * group]
                lines = [head * tiles_here + tile for tile in tiles]
                limits = [halo_ref[line, HALO_SLOTS - 1] for line in lines]
                most = limits[0]
                for limit in limits[1:]:
                    most = jnp.maximum(most, limit)

                def work(used):
                    begun = []
                    for line, tile, limit in zip(lines, tiles, limits):
                        here = pl.ds(pl.multiple_of(tile * tile_len, tile_len), tile_len)
                        if not used:
                            out_ref[here, column] = mixed_ref[here, column].astype(jnp.bfloat16)
                            continue
                        places = [halo_ref[line, slot] for slot in range(used)]
                        scores, largest = scores_of(
                            query_rows[here, :],
                            [tile_rows(key_rows, at, halo_tiles, tile_len) for at in places],
                            limit,
                            0,
                        )
                        level = stats_ref[here, column]
                        newest = jnp.maximum(level, jnp.max(largest, axis=1, keepdims=True) * factor)
                        begun.append((here, places, scores, newest, jnp.exp2(level - newest)))
                    for here, places, scores, newest, fade in begun:
                        added, update = mix(
                            scores,
                            newest,
                            factor,
                            [tile_rows(value_rows, at, halo_tiles, tile_len) for at in places],
                        )
                        out_ref[here, column] = (
                            (mixed_ref[here, column] * fade + update) / (fade + added)
                        ).astype(jnp.bfloat16)

                for used in range(0, HALO_SLOTS - 1, 2):
                    @pl.when((most + 1) // 2 == used // 2)
                    def _():
                        work(used)

    smem = pl.BlockSpec(memory_space=pltpu.SMEM)
    hbm = pl.BlockSpec(memory_space=pl.ANY)
    vmem = pl.BlockSpec(memory_space=pltpu.VMEM)
    pairs = heads * tiles_here * (HALO_SLOTS - 2) // 2
    return pl.pallas_call(
        kernel,
        in_specs=[smem, hbm, hbm, hbm, vmem, vmem],
        out_specs=vmem,
        out_shape=jax.ShapeDtypeStruct((rows, heads * head_dim), jnp.bfloat16),
        scratch_shapes=[
            pltpu.VMEM((2, heads, 2 * half, tokens, head_dim), jnp.bfloat16),
            pltpu.VMEM((heads, sources, tokens, head_dim), jnp.bfloat16),
            pltpu.SemaphoreType.DMA((heads, 5)),
        ],
        compiler_params=pltpu.CompilerParams(vmem_limit_bytes=VMEM_BYTES // 3),
        cost_estimate=pl.CostEstimate(
            flops=4 * pairs * tile_len * tile_len * head_dim,
            bytes_accessed=2 * heads * head_dim * (2 * halo_rows + 6 * rows),
            transcendentals=pairs * tile_len * tile_len,
        ),
    )(halo, own, left, right, mixed, stats)


def body(queries, keys, values, neighbours, counts):
    group_size = lax.axis_size("head")
    blocks = lax.axis_size("seq")
    local_tokens, feature_width = queries.shape
    head_count, tiles_here = counts.shape
    head_dim = feature_width // head_count
    per_device = head_count // group_size
    tile_len = local_tokens * group_size // tiles_here
    half = group_size // 2
    halo_tiles = half * local_tokens // tile_len

    def exchange(array):
        return lax.all_to_all(array, "head", split_axis=0, concat_axis=0, tiled=True)

    packed = prepare([keys, values, queries], [True, False, True], group_size, per_device, head_dim)
    own = exchange(packed)
    up = [(i, i + 1) for i in range(blocks - 1)]
    down = [(i + 1, i) for i in range(blocks - 1)]
    left = lax.ppermute(own[group_size - half :, :2], "seq", up)
    right = lax.ppermute(own[:half, :2], "seq", down)
    place = jnp.stack(
        [lax.axis_index("head") * per_device, lax.axis_index("seq") * tiles_here]
    ).astype(jnp.int32)
    listed = neighbours.reshape(head_count, -1)
    mixed, stats, halo = attend_local(own, listed, counts, place, tile_len, halo_tiles)
    result = attend_halo(own, left, right, mixed, stats, halo, tile_len)
    result = exchange(result.reshape(group_size, local_tokens, per_device * head_dim))
    return jnp.moveaxis(result, 0, 1).reshape(local_tokens, feature_width)


def solution(mesh):
    placed = (
        P(("seq", "head"), None),
        P(("seq", "head"), None),
        P(("seq", "head"), None),
        P(None, "seq", None),
        P(None, "seq"),
    )
    return jax.shard_map(
        body, mesh=mesh, in_specs=placed, out_specs=P(("seq", "head"), None), check_vma=False
    )
```

time: 182 us -> 176 us (0.967)
  waiting for transfers between devices: 96.2 us -> 6.51 us
  blocking collectives: 43.5 us -> 126 us
  Pallas kernels: 14.9 us -> 29.9 us
  starting transfers between devices: 19.5 us -> 5.83 us
    all_to_all x1 -> x2, blocking collectives: 43.5 us -> 126 us  [exchange(): lax.all_to_all(array, 'head', split_axis=0, concat_axis=0, tiled=True)]
    all_to_all x2 -> x0, waiting for transfers between devices: 73.3 us -> none  [exchange(): lax.all_to_all(array, 'head', split_axis=0, concat_axis=0, tiled=True)]
    pallas_call x1 -> x2, Pallas kernels: 8.95 us -> 25.7 us  [the longest x1 17.6 us: attend_local(): pl.pallas_call(kernel, in_specs=[smem, smem, smem, pl.BlockSpec(memory_sp...]
    ppermute x2, waiting for transfers between devices: 22.9 us -> 6.51 us  [the longest x1 4.94 us: body(): left = lax.ppermute(own[group_size - half:, :2], 'seq', up)]
    all_to_all x2 -> x0, starting transfers between devices: 10.7 us -> none  [exchange(): lax.all_to_all(array, 'head', split_axis=0, concat_axis=0, tiled=True)]
    ppermute x2, starting transfers between devices: 8.87 us -> 5.83 us  [the longest x1 3.92 us: body(): left = lax.ppermute(own[group_size - half:, :2], 'seq', up)]
    pallas_call x2 -> x1, Pallas kernels: 5.92 us -> 4.11 us  [prepare(): pl.pallas_call(kernel, grid=(tokens // step,), in_specs=[pl.BlockSpec((st...]
  transfers between devices with their start and end apart: 4 -> 2, of which waited for: 3 -> 2; matrix products, arithmetic and copies ran while one was open for 3% -> 2% of each run, Pallas kernels for 2% -> 10%
where the time goes in v4:
time: 176 us
  blocking collectives  126 us (72%)
  Pallas kernels  29.9 us (17%)
  local copies, waits for them, and re-layouts  7.4 us (4%)
  waiting for transfers between devices  6.51 us (4%)
  starting transfers between devices  5.83 us (3%)
    all_to_all x2, blocking collectives, exchange(): lax.all_to_all(array, 'head', split_axis=0, concat_axis=0, tiled=True)  126 us
    pallas_call x1, Pallas kernels, attend_local(): pl.pallas_call(kernel, in_specs=[smem, smem, smem, pl.BlockSpec(memory_sp...  17.6 us
    pallas_call x1, Pallas kernels, attend_halo(): pl.pallas_call(kernel, in_specs=[smem, hbm, hbm, hbm, vmem, vmem], out_sp...  8.13 us
    ppermute x1, waiting for transfers between devices, body(): left = lax.ppermute(own[group_size - half:, :2], 'seq', up)  4.94 us
    pallas_call x1, Pallas kernels, prepare(): pl.pallas_call(kernel, grid=(tokens // step,), in_specs=[pl.BlockSpec((st...  4.11 us
    ppermute x1, starting transfers between devices, body(): left = lax.ppermute(own[group_size - half:, :2], 'seq', up)  3.92 us
  transfers between devices with their start and end apart: 2, of which 2 were waited for; matrix products, arithmetic and copies ran while one was open for 2% of the time, Pallas kernels for 10%

profile of v4, /device:TPU:448, one launch (start us, length us, event | category | flops | bytes accessed | tf_op | source)
XLA Modules:
  0.0 175.9 jit_solution(10324769913065051197)
XLA Ops:
  0.0 4.1 %shard_map.55 = bf16[8,3,3,192,128]{4,3,2,1,0:T(8,128)(2,1)} custom-call(bf16[192,3072]{1,0:T(8,128)(2,1)} %refs_0_.1, bf16[192,3072]{1,0:T(8,128)(2,1)} %refs_1_.1, bf16[192,3072]{1,0:T(8,128)(2,1)} %refs_2_.1), custom_call_target="tpu_custom_call" | custom-call | flops 301989888 | bytes 7077888 | tf_op jit(solution)/shard_map/pallas_call | solution.py:48
  4.1 89.6 %all_to_all.10.own_ref = bf16[8,3,3,192,128]{4,3,2,1,0:T(8,128)(2,1)S(1)} all-to-all(bf16[8,3,3,192,128]{4,3,2,1,0:T(8,128)(2,1)} %shard_map.55), channel_id=1, replica_groups=mesh['seq'=64,'head'=8] {'head'}, dimensions={0} | all-to-all | bytes 7077888 | tf_op jit(solution)/shard_map/all_to_all | solution.py:338
  93.8 1.6 fusion
  95.4 1.9 %collective-permute-start.1 = (bf16[4,2,3,192,128]{4,3,2,1,0:T(8,128)(2,1)}, bf16[4,2,3,192,128]{4,3,2,1,0:T(8,128)(2,1)}, u32[]{:S(2)}, u32[]{:S(2)}) collective-permute-start(bf16[4,2,3,192,128]{4,3,2,1,0:T(8,128)(2,1)} %get-tuple-element.11), channel_id=1, source_target_pairs={{8,0},{16,8},{24,16},{32,24},{40,32},{48,40},{56,48},{64,56},{72,6... | collective-permute-start | bytes 3538952 | tf_op jit(solution)/shard_map/ppermute | solution.py:345
  97.3 3.9 %collective-permute-start = (bf16[4,2,3,192,128]{4,3,2,1,0:T(8,128)(2,1)}, bf16[4,2,3,192,128]{4,3,2,1,0:T(8,128)(2,1)}, u32[]{:S(2)}, u32[]{:S(2)}) collective-permute-start(bf16[4,2,3,192,128]{4,3,2,1,0:T(8,128)(2,1)} %get-tuple-element.12), channel_id=1, source_target_pairs={{0,8},{8,16},{16,24},{24,32},{32,40},{40,48},{48,56},{56,64},{64,7... | collective-permute-start | bytes 3538952 | tf_op jit(solution)/shard_map/ppermute | solution.py:344
  101.2 0.8 copy.10.counts_ref
  102.0 1.5 reshape.9
  103.5 1.6 copy.9.listed_ref
  105.1 0.1 pad_add_fusion.place_ref
  105.1 0.0 copy-start
  105.1 0.7 copy-done
  105.9 17.6 %shard_map.56 = (f32[1536,384]{1,0:T(8,128)S(1)}, f32[1536,384]{1,0:T(8,128)S(1)}, s32[36,8]{1,0:T(8,128)S(1)}) custom-call(s32[2]{0:T(128)S(1)} %pad_add_fusion.place_ref, s32[24,144]{1,0:T(8,128)S(1)} %copy-done, s32[24,12]{1,0:T(8,128)S(1)} %copy.10.counts_ref, bf16[8,3,3,192,128]{4,3,2,1,0:T(8,128)(2,1)S(1)} %all_to_all.10.own_ref), custom_call_target="tpu_custom_call" | custom-call | flops 3623878656 | bytes 8257536 | tf_op jit(solution)/shard_map/pallas_call | solution.py:206
  123.5 1.6 collective-permute-done.1.right_ref
  125.1 4.9 %collective-permute-done.left_ref = bf16[4,2,3,192,128]{4,3,2,1,0:T(8,128)(2,1)} collective-permute-done((bf16[4,2,3,192,128]{4,3,2,1,0:T(8,128)(2,1)}, bf16[4,2,3,192,128]{4,3,2,1,0:T(8,128)(2,1)}, u32[]{:S(2)}, u32[]{:S(2)}) %collective-permute-start) | collective-permute-done | bytes 1179680 | tf_op jit(solution)/shard_map/ppermute | solution.py:344
  130.0 8.1 %shard_map.57 = bf16[1536,384]{1,0:T(8,128)(2,1)S(1)} custom-call(s32[36,8]{1,0:T(8,128)S(1)} %get-tuple-element.8.halo_ref, bf16[8,3,3,192,128]{4,3,2,1,0:T(8,128)(2,1)S(1)} %all_to_all.10.own_ref, bf16[4,2,3,192,128]{4,3,2,1,0:T(8,128)(2,1)} %collective-permute-done.left_ref, bf16[4,2,3,192,128]{4,3,2,1,0:T(8,128)(2,1)} %collective-permute-done.1.right_ref, ...), custom_call_target="tpu_custom_call" | custom-call | flops 905969664 | bytes 9437184 | tf_op jit(solution)/shard_map/pallas_call | solution.py:307
  138.2 36.5 %all_to_all.11 = bf16[8,192,384]{2,1,0:T(8,128)(2,1)S(1)} all-to-all(bf16[8,192,384]{2,1,0:T(8,128)(2,1)S(1)} %bitcast.8), channel_id=1, replica_groups=mesh['seq'=64,'head'=8] {'head'}, dimensions={0} | all-to-all | bytes 2359296 | tf_op jit(solution)/shard_map/all_to_all | solution.py:338
  174.7 1.2 copy.12
Async XLA Ops:
  95.4 29.7 %collective-permute-start.1 = (bf16[4,2,3,192,128]{4,3,2,1,0:T(8,128)(2,1)}, bf16[4,2,3,192,128]{4,3,2,1,0:T(8,128)(2,1)}, u32[]{:S(2)}, u32[]{:S(2)}) collective-permute-start(bf16[4,2,3,192,128]{4,3,2,1,0:T(8,128)(2,1)} %get-tuple-element.11), channel_id=1, source_target_pairs={{8,0},{16,8},{24,16},{32,24},{40,32},{48,40},{56,48},{64,56},{72,6... | collective-permute-start | bytes 3538952 | tf_op jit(solution)/shard_map/ppermute | solution.py:345
  97.3 32.7 %collective-permute-start = (bf16[4,2,3,192,128]{4,3,2,1,0:T(8,128)(2,1)}, bf16[4,2,3,192,128]{4,3,2,1,0:T(8,128)(2,1)}, u32[]{:S(2)}, u32[]{:S(2)}) collective-permute-start(bf16[4,2,3,192,128]{4,3,2,1,0:T(8,128)(2,1)} %get-tuple-element.12), channel_id=1, source_target_pairs={{0,8},{8,16},{16,24},{24,32},{32,40},{40,48},{48,56},{56,64},{64,7... | collective-permute-start | bytes 3538952 | tf_op jit(solution)/shard_map/ppermute | solution.py:344
  105.1 0.7 copy-start

commit v5 on v4

--- a/solution.py
+++ b/solution.py
@@ -8,7 +8,7 @@
 from jax.sharding import PartitionSpec as P
 
 VMEM_BYTES = 60 * 1024 * 1024
-GROUP = 6
+OWN_SLOTS = 16
 HALO_SLOTS = 8
 
 
@@ -104,94 +104,130 @@
     return lambda: ref[pl.ds(pl.multiple_of(at * tile_len, tile_len), tile_len), :]
 
 
-def attend_local(own, listed, counts, place, tile_len, reach):
+def sort_lists(listed, counts, place, tiles_here, heads, reach):
+    slots = listed.shape[1] // tiles_here
+
+    def kernel(place_ref, listed_ref, counts_ref, inside_ref, halo_ref):
+        first_head = place_ref[0]
+        first_tile = place_ref[1]
+
+        @pl.loop(0, heads)
+        def _(head):
+            @pl.loop(0, tiles_here)
+            def _(tile):
+                line = head * tiles_here + tile
+                limit = counts_ref[first_head + head, tile]
+                for spare in range(OWN_SLOTS):
+                    inside_ref[line, spare] = 0
+                for spare in range(HALO_SLOTS):
+                    halo_ref[line, spare] = 0
+                inside = jnp.int32(0)
+                outside = jnp.int32(0)
+                for slot in range(slots):
+                    at = listed_ref[first_head + head, tile * slots + slot] - first_tile
+                    is_inside = (at >= 0) & (at < tiles_here)
+                    active = slot < limit
+
+                    @pl.when(active & is_inside)
+                    def _():
+                        inside_ref[line, inside] = at
+
+                    @pl.when(active & ~is_inside)
+                    def _():
+                        halo_ref[line, jnp.minimum(outside, HALO_SLOTS - 2)] = jnp.where(
+                            at < 0, at + reach, at - tiles_here + reach
+                        )
+
+                    inside = inside + (active & is_inside).astype(jnp.int32)
+                    outside = outside + (active & ~is_inside).astype(jnp.int32)
+                inside_ref[line, OWN_SLOTS - 1] = inside
+                halo_ref[line, HALO_SLOTS - 1] = outside
+
+    smem = pl.BlockSpec(memory_space=pltpu.SMEM)
+    lines = heads * tiles_here
+    return pl.pallas_call(
+        kernel,
+        in_specs=[smem, smem, smem],
+        out_specs=[smem, smem],
+        out_shape=[
+            jax.ShapeDtypeStruct((lines, OWN_SLOTS), jnp.int32),
+            jax.ShapeDtypeStruct((lines, HALO_SLOTS), jnp.int32),
+        ],
+    )(place, listed, counts)
+
+
+def tiles_of_step(step, tiles_here):
+    last = tiles_here - 1
+    return [2 * step, 2 * step + 1, last - 2 * step, last - 1 - 2 * step]
+
+
+def most_of(limits):
+    most = limits[0]
+    for limit in limits[1:]:
+        most = jnp.maximum(most, limit)
+    return most
+
+
+def attend_local(own, query, inside, tile_len):
     sources, _, heads, tokens, head_dim = own.shape
     rows = sources * tokens
     tiles_here = rows // tile_len
-    slots = listed.shape[1] // tiles_here
+    slots = tiles_here
     factor = math.log2(math.e) / math.sqrt(head_dim)
-    group_count = tiles_here // GROUP
-
-    def kernel(place_ref, listed_ref, counts_ref, own_ref, mixed_ref, stats_ref, halo_ref,
-               buf, inside_ref, sems):
+
+    def kernel(inside_ref, own_ref, query_ref, mixed_ref, stats_ref, buf, sems):
         def copies(head):
+            pairs = [(own_ref, 0), (own_ref, 1), (query_ref, 0)]
             return [
                 pltpu.make_async_copy(
-                    own_ref.at[:, index, head], buf.at[index, head], sems.at[head, index]
+                    ref.at[:, index, head], buf.at[number, head], sems.at[head, number]
                 )
-                for index in range(3)
+                for number, (ref, index) in enumerate(pairs)
             ]
 
         for head in range(heads):
             for copy in copies(head):
                 copy.start()
-        first_head = place_ref[0]
-        first_tile = place_ref[1]
-        for member in range(GROUP):
-            for slot in range(slots):
-                inside_ref[member, slot] = 0
 
         @pl.loop(0, heads)
         def _(head):
             for copy in copies(head):
                 copy.wait()
             key_rows, value_rows, query_rows = [
-                buf.at[index, head].reshape(rows, head_dim) for index in range(3)
+                buf.at[number, head].reshape(rows, head_dim) for number in range(3)
             ]
-            row = first_head + head
             column = pl.ds(pl.multiple_of(head * head_dim, head_dim), head_dim)
 
-            @pl.loop(0, group_count)
-            def _(group):
-                tiles = [group * GROUP + member for member in range(GROUP)]
-                limits = []
-                for member, tile in enumerate(tiles):
-                    limit = counts_ref[row, tile]
-                    line = head * tiles_here + tile
-                    inside = jnp.int32(0)
-                    outside = jnp.int32(0)
-                    for spare in range(HALO_SLOTS):
-                        halo_ref[line, spare] = 0
-                    for slot in range(slots):
-                        at = listed_ref[row, tile * slots + slot] - first_tile
-                        active = slot < limit
-                        is_inside = (at >= 0) & (at < tiles_here)
-                        inside_ref[member, inside] = at
-                        halo_ref[line, jnp.minimum(outside, HALO_SLOTS - 2)] = jnp.where(
-                            at < 0, at + reach, at - tiles_here + reach
-                        )
-                        inside = inside + (active & is_inside).astype(jnp.int32)
-                        outside = outside + (active & ~is_inside).astype(jnp.int32)
-                    halo_ref[line, HALO_SLOTS - 1] = outside
-                    limits.append(inside)
-                most = limits[0]
-                for limit in limits[1:]:
-                    most = jnp.maximum(most, limit)
+            @pl.loop(0, tiles_here // 4)
+            def _(step):
+                tiles = tiles_of_step(step, tiles_here)
+                lines = [head * tiles_here + tile for tile in tiles]
+                limits = [inside_ref[line, OWN_SLOTS - 1] for line in lines]
+                most = most_of(limits)
 
                 def work(used):
                     begun = []
-                    for member, tile in enumerate(tiles):
-                        token = pl.multiple_of(tile * tile_len, tile_len)
-                        query_now = query_rows[pl.ds(token, tile_len), :]
-                        places = [inside_ref[member, slot] for slot in range(used)]
+                    for line, tile, limit in zip(lines, tiles, limits):
+                        here = pl.ds(pl.multiple_of(tile * tile_len, tile_len), tile_len)
+                        places = [inside_ref[line, slot] for slot in range(used)]
                         scores, largest = scores_of(
-                            query_now,
+                            query_rows[here, :],
                             [tile_rows(key_rows, at, tiles_here, tile_len) for at in places],
-                            limits[member],
+                            limit,
                             1,
                         )
-                        begun.append((token, places, scores, jnp.max(largest, axis=1, keepdims=True)))
-                    for token, places, scores, peak in begun:
+                        peak = jnp.max(largest, axis=1, keepdims=True) * factor
+                        begun.append((here, places, scores, peak))
+                    for here, places, scores, peak in begun:
                         total, mixed = mix(
                             scores,
-                            peak * factor,
+                            peak,
                             factor,
                             [tile_rows(value_rows, at, tiles_here, tile_len) for at in places],
                         )
-                        mixed_ref[pl.ds(token, tile_len), column] = mixed / total
-                        level = peak * factor + jnp.log2(total)
-                        stats_ref[pl.ds(token, tile_len), column] = jnp.broadcast_to(
-                            level, (tile_len, head_dim)
+                        mixed_ref[here, column] = mixed / total
+                        stats_ref[here, column] = jnp.broadcast_to(
+                            peak + jnp.log2(total), (tile_len, head_dim)
                         )
 
                 for used in range(2, slots + 1, 2):
@@ -200,17 +236,17 @@
                         work(used)
 
     smem = pl.BlockSpec(memory_space=pltpu.SMEM)
+    hbm = pl.BlockSpec(memory_space=pl.ANY)
     vmem = pl.BlockSpec(memory_space=pltpu.VMEM)
     pairs = heads * tiles_here * slots
     state = jax.ShapeDtypeStruct((rows, heads * head_dim), jnp.float32)
     return pl.pallas_call(
         kernel,
-        in_specs=[smem, smem, smem, pl.BlockSpec(memory_space=pl.ANY)],
-        out_specs=[vmem, vmem, smem],
-        out_shape=[state, state, jax.ShapeDtypeStruct((heads * tiles_here, HALO_SLOTS), jnp.int32)],
+        in_specs=[smem, hbm, hbm],
+        out_specs=[vmem, vmem],
+        out_shape=[state, state],
         scratch_shapes=[
             pltpu.VMEM((3, heads, sources, tokens, head_dim), jnp.bfloat16),
-            pltpu.SMEM((GROUP, slots), jnp.int32),
             pltpu.SemaphoreType.DMA((heads, 3)),
         ],
         compiler_params=pltpu.CompilerParams(vmem_limit_bytes=VMEM_BYTES // 3),
@@ -219,11 +255,11 @@
             bytes_accessed=2 * heads * head_dim * 7 * rows,
             transcendentals=pairs * tile_len * tile_len,
         ),
-    )(place, listed, counts, own)
-
-
-def attend_halo(own, left, right, mixed, stats, halo, tile_len):
-    sources, _, heads, tokens, head_dim = own.shape
+    )(inside, own, query)
+
+
+def attend_halo(query, left, right, mixed, stats, halo, tile_len):
+    sources, _, heads, tokens, head_dim = query.shape
     half = left.shape[0]
     rows = sources * tokens
     halo_rows = 2 * half * tokens
@@ -231,10 +267,10 @@
     tiles_here = rows // tile_len
     factor = math.log2(math.e) / math.sqrt(head_dim)
 
-    def kernel(halo_ref, own_ref, left_ref, right_ref, mixed_ref, stats_ref, out_ref,
+    def kernel(halo_ref, query_ref, left_ref, right_ref, mixed_ref, stats_ref, out_ref,
                buf, query_buf, sems):
         def copies(head):
-            pairs = [(own_ref.at[:, 2, head], query_buf.at[head])]
+            pairs = [(query_ref.at[:, 0, head], query_buf.at[head])]
             for index in range(2):
                 pairs.append((left_ref.at[:, index, head], buf.at[index, head, pl.ds(0, half)]))
                 pairs.append((right_ref.at[:, index, head], buf.at[index, head, pl.ds(half, half)]))
@@ -258,14 +294,11 @@
             column = pl.ds(pl.multiple_of(head * head_dim, head_dim), head_dim)
 
             @pl.loop(0, tiles_here // 4)
-            def _(group):
-                last = tiles_here - 1
-                tiles = [2 * group, 2 * group + 1, last - 2 * group, last - 1 - 2 * group]
+            def _(step):
+                tiles = tiles_of_step(step, tiles_here)
                 lines = [head * tiles_here + tile for tile in tiles]
                 limits = [halo_ref[line, HALO_SLOTS - 1] for line in lines]
-                most = limits[0]
-                for limit in limits[1:]:
-                    most = jnp.maximum(most, limit)
+                most = most_of(limits)
 
                 def work(used):
                     begun = []
@@ -320,7 +353,7 @@
             bytes_accessed=2 * heads * head_dim * (2 * halo_rows + 6 * rows),
             transcendentals=pairs * tile_len * tile_len,
         ),
-    )(halo, own, left, right, mixed, stats)
+    )(halo, query, left, right, mixed, stats)
 
 
 def body(queries, keys, values, neighbours, counts):
@@ -337,18 +370,19 @@
     def exchange(array):
         return lax.all_to_all(array, "head", split_axis=0, concat_axis=0, tiled=True)
 
-    packed = prepare([keys, values, queries], [True, False, True], group_size, per_device, head_dim)
-    own = exchange(packed)
-    up = [(i, i + 1) for i in range(blocks - 1)]
-    down = [(i + 1, i) for i in range(blocks - 1)]
-    left = lax.ppermute(own[group_size - half :, :2], "seq", up)
-    right = lax.ppermute(own[:half, :2], "seq", down)
+    own = exchange(prepare([keys, values], [True, False], group_size, per_device, head_dim))
+    query = exchange(prepare([queries], [True], group_size, per_device, head_dim))
     place = jnp.stack(
         [lax.axis_index("head") * per_device, lax.axis_index("seq") * tiles_here]
     ).astype(jnp.int32)
     listed = neighbours.reshape(head_count, -1)
-    mixed, stats, halo = attend_local(own, listed, counts, place, tile_len, halo_tiles)
-    result = attend_halo(own, left, right, mixed, stats, halo, tile_len)
+    inside, halo = sort_lists(listed, counts, place, tiles_here, per_device, halo_tiles)
+    up = [(i, i + 1) for i in range(blocks - 1)]
+    down = [(i + 1, i) for i in range(blocks - 1)]
+    left = lax.ppermute(own[group_size - half :], "seq", up)
+    right = lax.ppermute(own[:half], "seq", down)
+    mixed, stats = attend_local(own, query, inside, tile_len)
+    result = attend_halo(query, left, right, mixed, stats, halo, tile_len)
     result = exchange(result.reshape(group_size, local_tokens, per_device * head_dim))
     return jnp.moveaxis(result, 0, 1).reshape(local_tokens, feature_width)
 

time: 176 us -> 174 us (0.989)
  blocking collectives: 126 us -> 38.9 us
  waiting for transfers between devices: 6.51 us -> 75.6 us
  starting transfers between devices: 5.83 us -> 19.5 us
  Pallas kernels: 29.9 us -> 31.9 us
    all_to_all x2 -> x1, blocking collectives: 126 us -> 38.9 us  [exchange(): lax.all_to_all(array, 'head', split_axis=0, concat_axis=0, tiled=True)]
    all_to_all x0 -> x2, waiting for transfers between devices: none -> 64 us  [exchange(): lax.all_to_all(array, 'head', split_axis=0, concat_axis=0, tiled=True)]
    all_to_all x0 -> x2, starting transfers between devices: none -> 10.7 us  [exchange(): lax.all_to_all(array, 'head', split_axis=0, concat_axis=0, tiled=True)]
    ppermute x2, waiting for transfers between devices: 6.51 us -> 11.6 us  [the longest x1 11.6 us: body(): left = lax.ppermute(own[group_size - half:], 'seq', up)]
    ppermute x2, starting transfers between devices: 5.83 us -> 8.87 us  [the longest x1 5.45 us: body(): right = lax.ppermute(own[:half], 'seq', down)]
    pallas_call x1 -> x2, Pallas kernels: 4.11 us -> 5.96 us  [prepare(): pl.pallas_call(kernel, grid=(tokens // step,), in_specs=[pl.BlockSpec((st...]
    pallas_call x1 -> x2, Pallas kernels: 17.6 us -> 18.7 us  [the longest x1 10.7 us: attend_local(): pl.pallas_call(kernel, in_specs=[smem, hbm, hbm], out_specs=[vmem, vmem],...]
  transfers between devices with their start and end apart: 2 -> 4, of which waited for: 2 -> 3; matrix products, arithmetic and copies ran while one was open for 2% -> 3% of each run, Pallas kernels for 10% -> 12%
where the time goes in v5:
time: 174 us
  waiting for transfers between devices  75.6 us (43%)
  blocking collectives  38.9 us (22%)
  Pallas kernels  31.9 us (18%)
  starting transfers between devices  19.5 us (11%)
  local copies, waits for them, and re-layouts  7.32 us (4%)
    all_to_all x2, waiting for transfers between devices, exchange(): lax.all_to_all(array, 'head', split_axis=0, concat_axis=0, tiled=True)  64 us
    all_to_all x1, blocking collectives, exchange(): lax.all_to_all(array, 'head', split_axis=0, concat_axis=0, tiled=True)  38.9 us
    ppermute x1, waiting for transfers between devices, body(): left = lax.ppermute(own[group_size - half:], 'seq', up)  11.6 us
    pallas_call x1, Pallas kernels, attend_local(): pl.pallas_call(kernel, in_specs=[smem, hbm, hbm], out_specs=[vmem, vmem],...  10.7 us
    all_to_all x2, starting transfers between devices, exchange(): lax.all_to_all(array, 'head', split_axis=0, concat_axis=0, tiled=True)  10.7 us
    pallas_call x1, Pallas kernels, sort_lists(): pl.pallas_call(kernel, in_specs=[smem, smem, smem], out_specs=[smem, smem...  8.08 us
    pallas_call x1, Pallas kernels, attend_halo(): pl.pallas_call(kernel, in_specs=[smem, hbm, hbm, hbm, vmem, vmem], out_sp...  7.17 us
    pallas_call x2, Pallas kernels, prepare(): pl.pallas_call(kernel, grid=(tokens // step,), in_specs=[pl.BlockSpec((st...  5.96 us
  transfers between devices with their start and end apart: 4, of which 3 were waited for; matrix products, arithmetic and copies ran while one was open for 3% of the time, Pallas kernels for 12%

profile of v5, /device:TPU:448, one launch (start us, length us, event | category | flops | bytes accessed | tf_op | source)
XLA Modules:
  0.0 173.9 jit_solution(5159144283376293471)
XLA Ops:
  0.0 3.3 %shard_map.57 = bf16[8,2,3,192,128]{4,3,2,1,0:T(8,128)(2,1)} custom-call(bf16[192,3072]{1,0:T(8,128)(2,1)} %refs_0_.3, bf16[192,3072]{1,0:T(8,128)(2,1)} %refs_1_.1), custom_call_target="tpu_custom_call" | custom-call | flops 150994944 | bytes 4718592 | tf_op jit(solution)/shard_map/pallas_call | solution.py:48
  3.3 7.1 %all-to-all-start.1 = ((bf16[8,2,3,192,128]{4,3,2,1,0:T(8,128)(2,1)}), bf16[8,2,3,192,128]{4,3,2,1,0:T(8,128)(2,1)S(1)}, u32[]{:S(2)}, u32[]{:S(2)}) async-start(bf16[8,2,3,192,128]{4,3,2,1,0:T(8,128)(2,1)} %shard_map.57), calls=%async_computation.1 | async-start | bytes 4718592 | tf_op jit(solution)/shard_map/all_to_all | solution.py:371
  10.4 2.7 %shard_map.56 = bf16[8,1,3,192,128]{4,3,2,1,0:T(8,128)(2,1)} custom-call(bf16[192,3072]{1,0:T(8,128)(2,1)} %refs_0_.2), custom_call_target="tpu_custom_call" | custom-call | flops 150994944 | bytes 2359296 | tf_op jit(solution)/shard_map/pallas_call | solution.py:48
  13.1 54.4 %all-to-all-done.1.own_ref = bf16[8,2,3,192,128]{4,3,2,1,0:T(8,128)(2,1)S(1)} async-done(((bf16[8,2,3,192,128]{4,3,2,1,0:T(8,128)(2,1)}), bf16[8,2,3,192,128]{4,3,2,1,0:T(8,128)(2,1)S(1)}, u32[]{:S(2)}, u32[]{:S(2)}) %all-to-all-start.1) | async-done | bytes 2359328 | tf_op jit(solution)/shard_map/all_to_all | solution.py:371
  67.4 3.6 %all-to-all-start = ((bf16[8,1,3,192,128]{4,3,2,1,0:T(8,128)(2,1)}), bf16[8,1,3,192,128]{4,3,2,1,0:T(8,128)(2,1)S(1)}, u32[]{:S(2)}, u32[]{:S(2)}) async-start(bf16[8,1,3,192,128]{4,3,2,1,0:T(8,128)(2,1)} %shard_map.56), calls=%async_computation | async-start | bytes 2359296 | tf_op jit(solution)/shard_map/all_to_all | solution.py:371
  71.0 0.0 copy-start.2
  71.0 1.6 fusion
  72.6 3.4 %collective-permute-start = (bf16[4,2,3,192,128]{4,3,2,1,0:T(8,128)(2,1)}, bf16[4,2,3,192,128]{4,3,2,1,0:T(8,128)(2,1)}, u32[]{:S(2)}, u32[]{:S(2)}) collective-permute-start(bf16[4,2,3,192,128]{4,3,2,1,0:T(8,128)(2,1)} %get-tuple-element.14), channel_id=1, source_target_pairs={{0,8},{8,16},{16,24},{24,32},{32,40},{40,48},{48,56},{56,64},{64,7... | collective-permute-start | bytes 3538952 | tf_op jit(solution)/shard_map/ppermute | solution.py:382
  76.0 5.4 %collective-permute-start.1 = (bf16[4,2,3,192,128]{4,3,2,1,0:T(8,128)(2,1)}, bf16[4,2,3,192,128]{4,3,2,1,0:T(8,128)(2,1)}, u32[]{:S(2)}, u32[]{:S(2)}) collective-permute-start(bf16[4,2,3,192,128]{4,3,2,1,0:T(8,128)(2,1)} %get-tuple-element.13), channel_id=1, source_target_pairs={{8,0},{16,8},{24,16},{32,24},{40,32},{48,40},{56,48},{64,56},{72,6... | collective-permute-start | bytes 3538952 | tf_op jit(solution)/shard_map/ppermute | solution.py:383
  81.5 1.5 reshape.9
  83.0 1.6 copy.9.listed_ref
  84.6 0.0 copy-done.2
  84.6 0.7 copy.10.counts_ref
  85.3 0.6 pad_add_fusion.place_ref
  85.9 8.1 %shard_map.55 = (s32[36,16]{1,0:T(8,128)}, s32[36,8]{1,0:T(8,128)}) custom-call(s32[2]{0:T(128)} %pad_add_fusion.place_ref, s32[24,144]{1,0:T(8,128)} %copy.9.listed_ref, s32[24,12]{1,0:T(8,128)} %copy.10.counts_ref), custom_call_target="tpu_custom_call" | custom-call | tf_op jit(solution)/shard_map/pallas_call | solution.py:148
  93.9 9.6 %all-to-all-done.query_ref = bf16[8,1,3,192,128]{4,3,2,1,0:T(8,128)(2,1)S(1)} async-done(((bf16[8,1,3,192,128]{4,3,2,1,0:T(8,128)(2,1)}), bf16[8,1,3,192,128]{4,3,2,1,0:T(8,128)(2,1)S(1)}, u32[]{:S(2)}, u32[]{:S(2)}) %all-to-all-start) | async-done | bytes 1179680 | tf_op jit(solution)/shard_map/all_to_all | solution.py:371
  103.5 0.0 copy-start.1
  103.5 0.7 copy-done.1
  104.3 0.0 copy-start
  104.3 10.7 %shard_map.58 = (f32[1536,384]{1,0:T(8,128)S(1)}, f32[1536,384]{1,0:T(8,128)S(1)}) custom-call(s32[36,16]{1,0:T(8,128)S(1)} %copy-done.1, bf16[8,2,3,192,128]{4,3,2,1,0:T(8,128)(2,1)S(1)} %all-to-all-done.1.own_ref, bf16[8,1,3,192,128]{4,3,2,1,0:T(8,128)(2,1)S(1)} %all-to-all-done.query_ref), custom_call_target="tpu_custom_call" | custom-call | flops 3623878656 | bytes 8257536 | tf_op jit(solution)/shard_map/pallas_call | solution.py:243
  114.9 11.6 %collective-permute-done.left_ref = bf16[4,2,3,192,128]{4,3,2,1,0:T(8,128)(2,1)} collective-permute-done((bf16[4,2,3,192,128]{4,3,2,1,0:T(8,128)(2,1)}, bf16[4,2,3,192,128]{4,3,2,1,0:T(8,128)(2,1)}, u32[]{:S(2)}, u32[]{:S(2)}) %collective-permute-start) | collective-permute-done | bytes 1179680 | tf_op jit(solution)/shard_map/ppermute | solution.py:382
  126.6 0.0 collective-permute-done.1.right_ref
  126.6 0.0 copy-done
  126.6 7.2 %shard_map.59 = bf16[1536,384]{1,0:T(8,128)(2,1)S(1)} custom-call(s32[36,8]{1,0:T(8,128)S(1)} %copy-done, bf16[8,1,3,192,128]{4,3,2,1,0:T(8,128)(2,1)S(1)} %all-to-all-done.query_ref, bf16[4,2,3,192,128]{4,3,2,1,0:T(8,128)(2,1)} %collective-permute-done.left_ref, bf16[4,2,3,192,128]{4,3,2,1,0:T(8,128)(2,1)} %collective-permute-done.1.right_ref, ...), custom_call_target="tpu_custom_call" | custom-call | flops 905969664 | bytes 9437184 | tf_op jit(solution)/shard_map/pallas_call | solution.py:340
  133.8 38.9 %all_to_all.15 = bf16[8,192,384]{2,1,0:T(8,128)(2,1)S(1)} all-to-all(bf16[8,192,384]{2,1,0:T(8,128)(2,1)S(1)} %bitcast.8), channel_id=1, replica_groups=mesh['seq'=64,'head'=8] {'head'}, dimensions={0} | all-to-all | bytes 2359296 | tf_op jit(solution)/shard_map/all_to_all | solution.py:371
  172.7 1.2 copy.12
Async XLA Ops:
  3.3 64.1 %all-to-all-start.1 = ((bf16[8,2,3,192,128]{4,3,2,1,0:T(8,128)(2,1)}), bf16[8,2,3,192,128]{4,3,2,1,0:T(8,128)(2,1)S(1)}, u32[]{:S(2)}, u32[]{:S(2)}) async-start(bf16[8,2,3,192,128]{4,3,2,1,0:T(8,128)(2,1)} %shard_map.57), calls=%async_computation.1 | async-start | bytes 4718592 | tf_op jit(solution)/shard_map/all_to_all | solution.py:371
  67.4 36.1 %all-to-all-start = ((bf16[8,1,3,192,128]{4,3,2,1,0:T(8,128)(2,1)}), bf16[8,1,3,192,128]{4,3,2,1,0:T(8,128)(2,1)S(1)}, u32[]{:S(2)}, u32[]{:S(2)}) async-start(bf16[8,1,3,192,128]{4,3,2,1,0:T(8,128)(2,1)} %shard_map.56), calls=%async_computation | async-start | bytes 2359296 | tf_op jit(solution)/shard_map/all_to_all | solution.py:371
  71.0 13.6 %copy-start.2 = (s32[24,12]{0,1:T(8,128)S(1)}, s32[24,12]{0,1:T(8,128)}, u32[]{:S(2)}) copy-start(s32[24,12]{0,1:T(8,128)} %param.9) | copy-start | bytes 3460
  72.6 54.0 %collective-permute-start = (bf16[4,2,3,192,128]{4,3,2,1,0:T(8,128)(2,1)}, bf16[4,2,3,192,128]{4,3,2,1,0:T(8,128)(2,1)}, u32[]{:S(2)}, u32[]{:S(2)}) collective-permute-start(bf16[4,2,3,192,128]{4,3,2,1,0:T(8,128)(2,1)} %get-tuple-element.14), channel_id=1, source_target_pairs={{0,8},{8,16},{16,24},{24,32},{32,40},{40,48},{48,56},{56,64},{64,7... | collective-permute-start | bytes 3538952 | tf_op jit(solution)/shard_map/ppermute | solution.py:382
  76.0 50.5 %collective-permute-start.1 = (bf16[4,2,3,192,128]{4,3,2,1,0:T(8,128)(2,1)}, bf16[4,2,3,192,128]{4,3,2,1,0:T(8,128)(2,1)}, u32[]{:S(2)}, u32[]{:S(2)}) collective-permute-start(bf16[4,2,3,192,128]{4,3,2,1,0:T(8,128)(2,1)} %get-tuple-element.13), channel_id=1, source_target_pairs={{8,0},{16,8},{24,16},{32,24},{40,32},{48,40},{56,48},{64,56},{72,6... | collective-permute-start | bytes 3538952 | tf_op jit(solution)/shard_map/ppermute | solution.py:383
  103.5 0.7 copy-start.1
  104.3 22.3 %copy-start = (s32[36,8]{1,0:T(8,128)S(1)}, s32[36,8]{1,0:T(8,128)}, u32[]{:S(2)}) copy-start(s32[36,8]{1,0:T(8,128)} %get-tuple-element.9.halo_ref) | copy-start | bytes 3460

commit v6 on v5

--- a/solution.py
+++ b/solution.py
@@ -8,6 +8,7 @@
 from jax.sharding import PartitionSpec as P
 
 VMEM_BYTES = 60 * 1024 * 1024
+ROW = 4
 OWN_SLOTS = 16
 HALO_SLOTS = 8
 
@@ -22,6 +23,19 @@
     return (1 - 2 * jnp.bitwise_and(parity, 1)).astype(jnp.float32).astype(jnp.bfloat16)
 
 
+def odd_row(block):
+    return (block // ROW) % 2
+
+
+def owner_block(member, odd, group_size):
+    return ((member // 2 + (member % 2) * odd) % (group_size // 2)) * 2 + member % 2
+
+
+def owner_of(block, head_block, group_size):
+    shift = (head_block % 2) * odd_row(block)
+    return ((head_block // 2 - shift) % (group_size // 2)) * 2 + head_block % 2
+
+
 def prepare(arrays, rotated, group_size, per_device, head_dim):
     tokens, width = arrays[0].shape
     count = len(arrays)
@@ -35,11 +49,13 @@
         def _():
             sign_ref[...] = sign_block(head_dim)
 
+        odd = odd_row(lax.axis_index("seq"))
         for index, ref in enumerate(refs[:-2]):
             for group in range(group_size):
+                first = owner_block(group, odd, group_size) * per_device
                 for head in range(per_device):
-                    column = (group * per_device + head) * head_dim
-                    block = ref[:, column : column + head_dim]
+                    column = pl.multiple_of((first + head) * head_dim, head_dim)
+                    block = ref[:, pl.ds(column, head_dim)]
                     if rotated[index]:
                         turned = jnp.dot(block, sign_ref[...], preferred_element_type=jnp.float32)
                         block = (turned * scale).astype(jnp.bfloat16)
@@ -258,80 +274,97 @@
     )(inside, own, query)
 
 
-def attend_halo(query, left, right, mixed, stats, halo, tile_len):
+def attend_halo(query, left, right, crossed, mixed, stats, halo, ends, tile_len):
     sources, _, heads, tokens, head_dim = query.shape
-    half = left.shape[0]
+    half = left[0].shape[0]
     rows = sources * tokens
     halo_rows = 2 * half * tokens
     halo_tiles = halo_rows // tile_len
+    reach = halo_tiles // 2
     tiles_here = rows // tile_len
     factor = math.log2(math.e) / math.sqrt(head_dim)
-
-    def kernel(halo_ref, query_ref, left_ref, right_ref, mixed_ref, stats_ref, out_ref,
-               buf, query_buf, sems):
-        def copies(head):
-            pairs = [(query_ref.at[:, 0, head], query_buf.at[head])]
-            for index in range(2):
-                pairs.append((left_ref.at[:, index, head], buf.at[index, head, pl.ds(0, half)]))
-                pairs.append((right_ref.at[:, index, head], buf.at[index, head, pl.ds(half, half)]))
-            return [
-                pltpu.make_async_copy(there, here, sems.at[head, number])
-                for number, (there, here) in enumerate(pairs)
-            ]
-
+    needs = [max(reach - tile, tile - tiles_here + 1 + reach) for tile in range(tiles_here)]
+
+    def kernel(halo_ref, ends_ref, query_ref, left_k, left_v, right_k, right_v, crossed_k, crossed_v,
+               mixed_ref, stats_ref, out_ref, buf, query_buf, sems):
+        def query_copy(head):
+            return pltpu.make_async_copy(
+                query_ref.at[:, 0, head], query_buf.at[head], sems.at[head, 0]
+            )
+
+        def side_copy(head, index, side, ref):
+            return pltpu.make_async_copy(
+                ref.at[:, head],
+                buf.at[index, head, pl.ds(side * half, half)],
+                sems.at[head, 1 + 2 * index + side],
+            )
+
+        sides = [
+            (0, 0, left_k, crossed_k),
+            (0, 1, right_k, crossed_k),
+            (1, 0, left_v, crossed_v),
+            (1, 1, right_v, crossed_v),
+        ]
         for head in range(heads):
-            for copy in copies(head):
-                copy.start()
+            query_copy(head).start()
+            for index, side, straight, other in sides:
+                is_other = ends_ref[side] == 1
+
+                @pl.when(is_other)
+                def _():
+                    side_copy(head, index, side, other).start()
+
+                @pl.when(jnp.logical_not(is_other))
+                def _():
+                    side_copy(head, index, side, straight).start()
 
         @pl.loop(0, heads)
         def _(head):
-            for copy in copies(head):
-                copy.wait()
+            query_copy(head).wait()
+            for index, side, straight, _ in sides:
+                side_copy(head, index, side, straight).wait()
             key_rows, value_rows = [
                 buf.at[index, head].reshape(halo_rows, head_dim) for index in range(2)
             ]
             query_rows = query_buf.at[head].reshape(rows, head_dim)
             column = pl.ds(pl.multiple_of(head * head_dim, head_dim), head_dim)
-
-            @pl.loop(0, tiles_here // 4)
-            def _(step):
-                tiles = tiles_of_step(step, tiles_here)
-                lines = [head * tiles_here + tile for tile in tiles]
-                limits = [halo_ref[line, HALO_SLOTS - 1] for line in lines]
-                most = most_of(limits)
-
-                def work(used):
-                    begun = []
-                    for line, tile, limit in zip(lines, tiles, limits):
-                        here = pl.ds(pl.multiple_of(tile * tile_len, tile_len), tile_len)
-                        if not used:
-                            out_ref[here, column] = mixed_ref[here, column].astype(jnp.bfloat16)
-                            continue
-                        places = [halo_ref[line, slot] for slot in range(used)]
-                        scores, largest = scores_of(
-                            query_rows[here, :],
-                            [tile_rows(key_rows, at, halo_tiles, tile_len) for at in places],
-                            limit,
-                            0,
-                        )
-                        level = stats_ref[here, column]
-                        newest = jnp.maximum(level, jnp.max(largest, axis=1, keepdims=True) * factor)
-                        begun.append((here, places, scores, newest, jnp.exp2(level - newest)))
-                    for here, places, scores, newest, fade in begun:
-                        added, update = mix(
-                            scores,
-                            newest,
-                            factor,
-                            [tile_rows(value_rows, at, halo_tiles, tile_len) for at in places],
-                        )
-                        out_ref[here, column] = (
-                            (mixed_ref[here, column] * fade + update) / (fade + added)
-                        ).astype(jnp.bfloat16)
-
-                for used in range(0, HALO_SLOTS - 1, 2):
-                    @pl.when((most + 1) // 2 == used // 2)
-                    def _():
-                        work(used)
+            lines = [head * tiles_here + tile for tile in range(tiles_here)]
+            limits = [halo_ref[line, HALO_SLOTS - 1] for line in lines]
+            most = most_of(limits)
+
+            def work(cap):
+                begun = []
+                for tile in range(tiles_here):
+                    here = slice(tile * tile_len, (tile + 1) * tile_len)
+                    used = min(cap, needs[tile] + needs[tile] % 2)
+                    if not used:
+                        out_ref[here, column] = mixed_ref[here, column].astype(jnp.bfloat16)
+                        continue
+                    places = [halo_ref[lines[tile], slot] for slot in range(used)]
+                    scores, largest = scores_of(
+                        query_rows[here, :],
+                        [tile_rows(key_rows, at, halo_tiles, tile_len) for at in places],
+                        limits[tile],
+                        0,
+                    )
+                    level = stats_ref[here, column]
+                    newest = jnp.maximum(level, jnp.max(largest, axis=1, keepdims=True) * factor)
+                    begun.append((here, places, scores, newest, jnp.exp2(level - newest)))
+                for here, places, scores, newest, fade in begun:
+                    added, update = mix(
+                        scores,
+                        newest,
+                        factor,
+                        [tile_rows(value_rows, at, halo_tiles, tile_len) for at in places],
+                    )
+                    out_ref[here, column] = (
+                        (mixed_ref[here, column] * fade + update) / (fade + added)
+                    ).astype(jnp.bfloat16)
+
+            for cap in range(0, HALO_SLOTS - 1, 2):
+                @pl.when((most + 1) // 2 == cap // 2)
+                def _():
+                    work(cap)
 
     smem = pl.BlockSpec(memory_space=pltpu.SMEM)
     hbm = pl.BlockSpec(memory_space=pl.ANY)
@@ -339,7 +372,7 @@
     pairs = heads * tiles_here * (HALO_SLOTS - 2) // 2
     return pl.pallas_call(
         kernel,
-        in_specs=[smem, hbm, hbm, hbm, vmem, vmem],
+        in_specs=[smem, smem] + [hbm] * 7 + [vmem, vmem],
         out_specs=vmem,
         out_shape=jax.ShapeDtypeStruct((rows, heads * head_dim), jnp.bfloat16),
         scratch_shapes=[
@@ -353,7 +386,55 @@
             bytes_accessed=2 * heads * head_dim * (2 * halo_rows + 6 * rows),
             transcendentals=pairs * tile_len * tile_len,
         ),
-    )(halo, query, left, right, mixed, stats)
+    )(halo, ends, query, *left, *right, *crossed, mixed, stats)
+
+
+def routes(blocks, group_size):
+    on = []
+    across = []
+    for block in range(blocks):
+        there = block + 1
+        if there % ROW == 0:
+            there = block + 1 - ROW if odd_row(block) == 0 else block + 1 + ROW
+        if there < blocks:
+            on += [(block * group_size + m, there * group_size + m) for m in range(group_size)]
+        if block % ROW in (0, ROW - 1):
+            other = block + ROW if odd_row(block) == 0 else block - ROW
+            across += [
+                tuple(at * group_size + owner_of(at, head_block, group_size) for at in (block, other))
+                for head_block in range(group_size)
+            ]
+    back = []
+    for block in range(blocks):
+        there = block - 1
+        if block % ROW == 0:
+            there = block - 1 + ROW if odd_row(block) == 1 else block - 1 - ROW
+        if there >= 0:
+            back += [(block * group_size + m, there * group_size + m) for m in range(group_size)]
+    return on, back, across
+
+
+def assemble(parts):
+    members, tokens, width = parts.shape
+    step = tokens // 2
+
+    def kernel(parts_ref, out_ref):
+        odd = odd_row(lax.axis_index("seq"))
+        for member in range(members):
+            column = pl.multiple_of(owner_block(member, odd, members) * width, width)
+            out_ref[:, pl.ds(column, width)] = parts_ref[member]
+
+    return pl.pallas_call(
+        kernel,
+        grid=(tokens // step,),
+        in_specs=[pl.BlockSpec((members, step, width), lambda g: (0, g, 0))],
+        out_specs=pl.BlockSpec((step, members * width), lambda g: (g, 0)),
+        out_shape=jax.ShapeDtypeStruct((tokens, members * width), parts.dtype),
+        compiler_params=pltpu.CompilerParams(vmem_limit_bytes=VMEM_BYTES),
+        cost_estimate=pl.CostEstimate(
+            flops=0, bytes_accessed=4 * tokens * members * width, transcendentals=0
+        ),
+    )(parts)
 
 
 def body(queries, keys, values, neighbours, counts):
@@ -372,19 +453,24 @@
 
     own = exchange(prepare([keys, values], [True, False], group_size, per_device, head_dim))
     query = exchange(prepare([queries], [True], group_size, per_device, head_dim))
-    place = jnp.stack(
-        [lax.axis_index("head") * per_device, lax.axis_index("seq") * tiles_here]
-    ).astype(jnp.int32)
+    block = lax.axis_index("seq")
+    head_block = owner_block(lax.axis_index("head"), odd_row(block), group_size)
+    place = jnp.stack([head_block * per_device, block * tiles_here]).astype(jnp.int32)
+    at_start = block % ROW == 0
+    ends = jnp.stack([at_start, block % ROW == ROW - 1]).astype(jnp.int32)
     listed = neighbours.reshape(head_count, -1)
     inside, halo = sort_lists(listed, counts, place, tiles_here, per_device, halo_tiles)
-    up = [(i, i + 1) for i in range(blocks - 1)]
-    down = [(i + 1, i) for i in range(blocks - 1)]
-    left = lax.ppermute(own[group_size - half :], "seq", up)
-    right = lax.ppermute(own[:half], "seq", down)
+    on, back, across = routes(blocks, group_size)
+    both = ("seq", "head")
+    left = [lax.ppermute(own[group_size - half :, index], both, on) for index in range(2)]
+    right = [lax.ppermute(own[:half, index], both, back) for index in range(2)]
+    crossed = [
+        lax.ppermute(jnp.where(at_start, one, two), both, across) for one, two in zip(left, right)
+    ]
     mixed, stats = attend_local(own, query, inside, tile_len)
-    result = attend_halo(query, left, right, mixed, stats, halo, tile_len)
+    result = attend_halo(query, left, right, crossed, mixed, stats, halo, ends, tile_len)
     result = exchange(result.reshape(group_size, local_tokens, per_device * head_dim))
-    return jnp.moveaxis(result, 0, 1).reshape(local_tokens, feature_width)
+    return assemble(result)
 
 
 def solution(mesh):

time: 174 us -> 185 us (1.063); the launches traced: 174 us -> 182 us
  starting transfers between devices: 19.5 us -> 32.5 us
  waiting for transfers between devices: 75.6 us -> 70.7 us
  Pallas kernels: 31.9 us -> 27.8 us
  other arithmetic: 0.57 us -> 4.64 us
    ppermute x2 -> x6, starting transfers between devices: 8.87 us -> 21.8 us  [the longest x2 9.78 us: body(): right = [lax.ppermute(own[:half, index], both, back) for index in range(2)]]
    all_to_all x2, waiting for transfers between devices: 64 us -> 54.4 us  [exchange(): lax.all_to_all(array, 'head', split_axis=0, concat_axis=0, tiled=True)]
    ppermute x2 -> x6, waiting for transfers between devices: 11.6 us -> 16.3 us  [the longest x2 11 us: body(): lax.ppermute(own[group_size - half:, index], both, on)]
    pallas_call x1, Pallas kernels: 10.7 us -> 6.4 us  [attend_local(): pl.pallas_call(kernel, in_specs=[smem, hbm, hbm], out_specs=[vmem, vmem],...]
    select_n x0 -> x2, other arithmetic: none -> 3.9 us  [body(): jnp.where(at_start, one, two)]
    pallas_call x1 -> x2, Pallas kernels: 7.17 us -> 7.49 us  [the longest x1 5.34 us: attend_halo(): pl.pallas_call(kernel, in_specs=[smem, smem] + [hbm] * 7 + [vmem, vmem],...]
  transfers between devices with their start and end apart: 4 -> 8, of which waited for: 3 -> 5; matrix products, arithmetic and copies ran while one was open for 3% -> 5% of each run, Pallas kernels for 12% -> 9%
where the time goes in v6:
time: 185 us; the launch traced here: 182 us
  waiting for transfers between devices  70.7 us (38%)
  blocking collectives  40 us (22%)
  starting transfers between devices  32.5 us (18%)
  Pallas kernels  27.8 us (15%)
  local copies, waits for them, and re-layouts  5.93 us (3%)
  other arithmetic  4.64 us (3%)
    all_to_all x2, waiting for transfers between devices, exchange(): lax.all_to_all(array, 'head', split_axis=0, concat_axis=0, tiled=True)  54.4 us
    all_to_all x1, blocking collectives, exchange(): lax.all_to_all(array, 'head', split_axis=0, concat_axis=0, tiled=True)  40 us
    ppermute x2, waiting for transfers between devices, body(): lax.ppermute(own[group_size - half:, index], both, on)  11 us
    all_to_all x2, starting transfers between devices, exchange(): lax.all_to_all(array, 'head', split_axis=0, concat_axis=0, tiled=True)  10.7 us
    ppermute x2, starting transfers between devices, body(): right = [lax.ppermute(own[:half, index], both, back) for index in range(2)]  9.78 us
    ppermute x2, starting transfers between devices, body(): lax.ppermute(jnp.where(at_start, one, two), both, across)  8.19 us
    pallas_call x1, Pallas kernels, sort_lists(): pl.pallas_call(kernel, in_specs=[smem, smem, smem], out_specs=[smem, smem...  8.08 us
    pallas_call x1, Pallas kernels, attend_local(): pl.pallas_call(kernel, in_specs=[smem, hbm, hbm], out_specs=[vmem, vmem],...  6.4 us
  transfers between devices with their start and end apart: 8, of which 5 were waited for; matrix products, arithmetic and copies ran while one was open for 5% of the time, Pallas kernels for 9%

profile of v6, /device:TPU:448, one launch (start us, length us, event | category | flops | bytes accessed | tf_op | source)
XLA Modules:
  0.0 181.8 jit_solution(16055323985168316960)
XLA Ops:
  0.0 3.2 %shard_map.57 = bf16[8,2,3,192,128]{4,3,2,1,0:T(8,128)(2,1)} custom-call(bf16[192,3072]{1,0:T(8,128)(2,1)} %refs_0_.3, bf16[192,3072]{1,0:T(8,128)(2,1)} %refs_1_.1), custom_call_target="tpu_custom_call" | custom-call | flops 150994944 | bytes 4718592 | tf_op jit(solution)/shard_map/pallas_call | solution.py:64
  3.2 7.1 %all-to-all-start.1 = ((bf16[8,2,3,192,128]{4,3,2,1,0:T(8,128)(2,1)}), bf16[8,2,3,192,128]{4,3,2,1,0:T(8,128)(2,1)S(1)}, u32[]{:S(2)}, u32[]{:S(2)}) async-start(bf16[8,2,3,192,128]{4,3,2,1,0:T(8,128)(2,1)} %shard_map.57), calls=%async_computation.1 | async-start | bytes 4718592 | tf_op jit(solution)/shard_map/all_to_all | solution.py:452
  10.3 2.7 %shard_map.56 = bf16[8,1,3,192,128]{4,3,2,1,0:T(8,128)(2,1)} custom-call(bf16[192,3072]{1,0:T(8,128)(2,1)} %refs_0_.2), custom_call_target="tpu_custom_call" | custom-call | flops 150994944 | bytes 2359296 | tf_op jit(solution)/shard_map/pallas_call | solution.py:64
  13.0 54.4 %all-to-all-done.1.own_ref = bf16[8,2,3,192,128]{4,3,2,1,0:T(8,128)(2,1)S(1)} async-done(((bf16[8,2,3,192,128]{4,3,2,1,0:T(8,128)(2,1)}), bf16[8,2,3,192,128]{4,3,2,1,0:T(8,128)(2,1)S(1)}, u32[]{:S(2)}, u32[]{:S(2)}) %all-to-all-start.1) | async-done | bytes 2359328 | tf_op jit(solution)/shard_map/all_to_all | solution.py:452
  67.3 3.6 %all-to-all-start = ((bf16[8,1,3,192,128]{4,3,2,1,0:T(8,128)(2,1)}), bf16[8,1,3,192,128]{4,3,2,1,0:T(8,128)(2,1)S(1)}, u32[]{:S(2)}, u32[]{:S(2)}) async-start(bf16[8,1,3,192,128]{4,3,2,1,0:T(8,128)(2,1)} %shard_map.56), calls=%async_computation | async-start | bytes 2359296 | tf_op jit(solution)/shard_map/all_to_all | solution.py:452
  70.9 1.4 slice_bitcast_fusion
  72.3 4.6 %collective-permute-start.3 = (bf16[4,3,192,128]{3,2,1,0:T(8,128)(2,1)}, bf16[4,3,192,128]{3,2,1,0:T(8,128)(2,1)}, u32[]{:S(2)}, u32[]{:S(2)}) collective-permute-start(bf16[4,3,192,128]{3,2,1,0:T(8,128)(2,1)} %get-tuple-element.13), channel_id=1, source_target_pairs={{8,0},{9,1},{10,2},{11,3},{12,4},{13,5},{14,6},{15,7},{16,8},{17,9... | collective-permute-start | bytes 1769480 | tf_op jit(solution)/shard_map/ppermute | solution.py:466
  77.0 1.9 %collective-permute-start.1 = (bf16[4,3,192,128]{3,2,1,0:T(8,128)(2,1)}, bf16[4,3,192,128]{3,2,1,0:T(8,128)(2,1)}, u32[]{:S(2)}, u32[]{:S(2)}) collective-permute-start(bf16[4,3,192,128]{3,2,1,0:T(8,128)(2,1)} %get-tuple-element.15), channel_id=1, source_target_pairs={{0,8},{1,9},{2,10},{3,11},{4,12},{5,13},{6,14},{7,15},{8,16},{9,17... | collective-permute-start | bytes 1769480 | tf_op jit(solution)/shard_map/ppermute | solution.py:465
  78.9 5.1 %collective-permute-start.2 = (bf16[4,3,192,128]{3,2,1,0:T(8,128)(2,1)}, bf16[4,3,192,128]{3,2,1,0:T(8,128)(2,1)}, u32[]{:S(2)}, u32[]{:S(2)}) collective-permute-start(bf16[4,3,192,128]{3,2,1,0:T(8,128)(2,1)} %get-tuple-element.14), channel_id=1, source_target_pairs={{8,0},{9,1},{10,2},{11,3},{12,4},{13,5},{14,6},{15,7},{16,8},{17,9... | collective-permute-start | bytes 1769480 | tf_op jit(solution)/shard_map/ppermute | solution.py:466
  84.1 1.9 %collective-permute-start = (bf16[4,3,192,128]{3,2,1,0:T(8,128)(2,1)}, bf16[4,3,192,128]{3,2,1,0:T(8,128)(2,1)}, u32[]{:S(2)}, u32[]{:S(2)}) collective-permute-start(bf16[4,3,192,128]{3,2,1,0:T(8,128)(2,1)} %get-tuple-element.16), channel_id=1, source_target_pairs={{0,8},{1,9},{2,10},{3,11},{4,12},{5,13},{6,14},{7,15},{8,16},{9,17... | collective-permute-start | bytes 1769480 | tf_op jit(solution)/shard_map/ppermute | solution.py:465
  86.0 4.9 %collective-permute-done.3.right_v = bf16[4,3,192,128]{3,2,1,0:T(8,128)(2,1)} collective-permute-done((bf16[4,3,192,128]{3,2,1,0:T(8,128)(2,1)}, bf16[4,3,192,128]{3,2,1,0:T(8,128)(2,1)}, u32[]{:S(2)}, u32[]{:S(2)}) %collective-permute-start.3) | collective-permute-done | bytes 589856 | tf_op jit(solution)/shard_map/ppermute | solution.py:466
  90.9 5.6 %collective-permute-done.1.left_v = bf16[4,3,192,128]{3,2,1,0:T(8,128)(2,1)} collective-permute-done((bf16[4,3,192,128]{3,2,1,0:T(8,128)(2,1)}, bf16[4,3,192,128]{3,2,1,0:T(8,128)(2,1)}, u32[]{:S(2)}, u32[]{:S(2)}) %collective-permute-start.1) | collective-permute-done | bytes 589856 | tf_op jit(solution)/shard_map/ppermute | solution.py:465
  96.6 1.9 %broadcast_select_fusion = bf16[4,3,192,128]{3,2,1,0:T(8,128)(2,1)} fusion(bf16[4,3,192,128]{3,2,1,0:T(8,128)(2,1)} %collective-permute-done.1.left_v, bf16[4,3,192,128]{3,2,1,0:T(8,128)(2,1)} %collective-permute-done.3.right_v, pred[]{:T(512)} %eq.13), kind=kLoop, calls=%fused_computation.4 | loop fusion | flops 294912 | bytes 1769473 | tf_op jit(solution)/shard_map/jit(_where)/select_n | solution.py:468
  98.5 0.0 copy-start.2
  98.5 4.2 %collective-permute-start.5 = (bf16[4,3,192,128]{3,2,1,0:T(8,128)(2,1)}, bf16[4,3,192,128]{3,2,1,0:T(8,128)(2,1)}, u32[]{:S(2)}, u32[]{:S(2)}) collective-permute-start(bf16[4,3,192,128]{3,2,1,0:T(8,128)(2,1)} %broadcast_select_fusion), channel_id=1, source_target_pairs={{0,32},{1,39},{2,34},{3,33},{4,36},{5,35},{6,38},{7,37},{24,56},{2... | collective-permute-start | bytes 1769480 | tf_op jit(solution)/shard_map/ppermute | solution.py:468
  102.7 0.4 collective-permute-done.2.right_k
  103.1 5.3 %collective-permute-done.left_k = bf16[4,3,192,128]{3,2,1,0:T(8,128)(2,1)} collective-permute-done((bf16[4,3,192,128]{3,2,1,0:T(8,128)(2,1)}, bf16[4,3,192,128]{3,2,1,0:T(8,128)(2,1)}, u32[]{:S(2)}, u32[]{:S(2)}) %collective-permute-start) | collective-permute-done | bytes 589856 | tf_op jit(solution)/shard_map/ppermute | solution.py:465
  108.4 1.9 %broadcast_select_fusion.1 = bf16[4,3,192,128]{3,2,1,0:T(8,128)(2,1)} fusion(bf16[4,3,192,128]{3,2,1,0:T(8,128)(2,1)} %collective-permute-done.left_k, bf16[4,3,192,128]{3,2,1,0:T(8,128)(2,1)} %collective-permute-done.2.right_k, pred[]{:T(512)} %eq.13), kind=kLoop, calls=%fused_computation.5 | loop fusion | flops 294912 | bytes 1769473 | tf_op jit(solution)/shard_map/jit(_where)/select_n | solution.py:468
  110.4 4.0 %collective-permute-start.4 = (bf16[4,3,192,128]{3,2,1,0:T(8,128)(2,1)}, bf16[4,3,192,128]{3,2,1,0:T(8,128)(2,1)}, u32[]{:S(2)}, u32[]{:S(2)}) collective-permute-start(bf16[4,3,192,128]{3,2,1,0:T(8,128)(2,1)} %broadcast_select_fusion.1), channel_id=1, source_target_pairs={{0,32},{1,39},{2,34},{3,33},{4,36},{5,35},{6,38},{7,37},{24,56},{2... | collective-permute-start | bytes 1769480 | tf_op jit(solution)/shard_map/ppermute | solution.py:468
  114.5 0.0 copy-done.2
  114.5 0.7 copy.15.counts_ref
  115.2 1.5 reshape.6
  116.7 1.6 copy.14.listed_ref
  118.3 0.7 pad_add_fusion.place_ref
  118.9 8.1 %shard_map.55 = (s32[36,16]{1,0:T(8,128)}, s32[36,8]{1,0:T(8,128)}) custom-call(s32[2]{0:T(128)} %pad_add_fusion.place_ref, s32[24,144]{1,0:T(8,128)} %copy.14.listed_ref, s32[24,12]{1,0:T(8,128)} %copy.15.counts_ref), custom_call_target="tpu_custom_call" | custom-call | tf_op jit(solution)/shard_map/pallas_call | solution.py:164
  127.0 0.1 add_convert_fusion.ends_ref
  127.1 0.0 all-to-all-done.query_ref
  127.1 0.0 copy-start.1
  127.1 0.7 copy-done.1
  127.8 0.0 copy-start
  127.8 6.4 %shard_map.58 = (f32[1536,384]{1,0:T(8,128)S(1)}, f32[1536,384]{1,0:T(8,128)S(1)}) custom-call(s32[36,16]{1,0:T(8,128)S(1)} %copy-done.1, bf16[8,2,3,192,128]{4,3,2,1,0:T(8,128)(2,1)S(1)} %all-to-all-done.1.own_ref, bf16[8,1,3,192,128]{4,3,2,1,0:T(8,128)(2,1)S(1)} %all-to-all-done.query_ref), custom_call_target="tpu_custom_call" | custom-call | flops 3623878656 | bytes 8257536 | tf_op jit(solution)/shard_map/pallas_call | solution.py:259
  134.3 0.0 collective-permute-done.5.crossed_v
  134.3 0.0 collective-permute-done.4.crossed_k
  134.3 0.0 copy-done
  134.3 5.3 %shard_map.59 = bf16[1536,384]{1,0:T(8,128)(2,1)S(1)} custom-call(s32[36,8]{1,0:T(8,128)S(1)} %copy-done, s32[2]{0:T(128)S(1)} %add_convert_fusion.ends_ref, bf16[8,1,3,192,128]{4,3,2,1,0:T(8,128)(2,1)S(1)} %all-to-all-done.query_ref, bf16[4,3,192,128]{3,2,1,0:T(8,128)(2,1)} %collective-permute-done.left_k, ...), custom_call_target="tpu_custom_call" | custom-call | flops 905969664 | bytes 9437184 | tf_op jit(solution)/shard_map/pallas_call | solution.py:373
  139.6 40.0 %all_to_all.15.parts_ref = bf16[8,192,384]{2,1,0:T(8,128)(2,1)} all-to-all(bf16[8,192,384]{2,1,0:T(8,128)(2,1)S(1)} %bitcast.23), channel_id=1, replica_groups=mesh['seq'=64,'head'=8] {'head'}, dimensions={0} | all-to-all | bytes 2359296 | tf_op jit(solution)/shard_map/all_to_all | solution.py:452
  179.6 2.1 %shard_map.60 = bf16[192,3072]{1,0:T(8,128)(2,1)} custom-call(bf16[8,192,384]{2,1,0:T(8,128)(2,1)} %all_to_all.15.parts_ref), custom_call_target="tpu_custom_call" | custom-call | bytes 2359296 | tf_op jit(solution)/shard_map/pallas_call | solution.py:427
Async XLA Ops:
  3.2 64.2 %all-to-all-start.1 = ((bf16[8,2,3,192,128]{4,3,2,1,0:T(8,128)(2,1)}), bf16[8,2,3,192,128]{4,3,2,1,0:T(8,128)(2,1)S(1)}, u32[]{:S(2)}, u32[]{:S(2)}) async-start(bf16[8,2,3,192,128]{4,3,2,1,0:T(8,128)(2,1)} %shard_map.57), calls=%async_computation.1 | async-start | bytes 4718592 | tf_op jit(solution)/shard_map/all_to_all | solution.py:452
  67.3 59.8 %all-to-all-start = ((bf16[8,1,3,192,128]{4,3,2,1,0:T(8,128)(2,1)}), bf16[8,1,3,192,128]{4,3,2,1,0:T(8,128)(2,1)S(1)}, u32[]{:S(2)}, u32[]{:S(2)}) async-start(bf16[8,1,3,192,128]{4,3,2,1,0:T(8,128)(2,1)} %shard_map.56), calls=%async_computation | async-start | bytes 2359296 | tf_op jit(solution)/shard_map/all_to_all | solution.py:452
  72.3 18.6 %collective-permute-start.3 = (bf16[4,3,192,128]{3,2,1,0:T(8,128)(2,1)}, bf16[4,3,192,128]{3,2,1,0:T(8,128)(2,1)}, u32[]{:S(2)}, u32[]{:S(2)}) collective-permute-start(bf16[4,3,192,128]{3,2,1,0:T(8,128)(2,1)} %get-tuple-element.13), channel_id=1, source_target_pairs={{8,0},{9,1},{10,2},{11,3},{12,4},{13,5},{14,6},{15,7},{16,8},{17,9... | collective-permute-start | bytes 1769480 | tf_op jit(solution)/shard_map/ppermute | solution.py:466
  77.0 19.6 %collective-permute-start.1 = (bf16[4,3,192,128]{3,2,1,0:T(8,128)(2,1)}, bf16[4,3,192,128]{3,2,1,0:T(8,128)(2,1)}, u32[]{:S(2)}, u32[]{:S(2)}) collective-permute-start(bf16[4,3,192,128]{3,2,1,0:T(8,128)(2,1)} %get-tuple-element.15), channel_id=1, source_target_pairs={{0,8},{1,9},{2,10},{3,11},{4,12},{5,13},{6,14},{7,15},{8,16},{9,17... | collective-permute-start | bytes 1769480 | tf_op jit(solution)/shard_map/ppermute | solution.py:465
  78.9 24.2 %collective-permute-start.2 = (bf16[4,3,192,128]{3,2,1,0:T(8,128)(2,1)}, bf16[4,3,192,128]{3,2,1,0:T(8,128)(2,1)}, u32[]{:S(2)}, u32[]{:S(2)}) collective-permute-start(bf16[4,3,192,128]{3,2,1,0:T(8,128)(2,1)} %get-tuple-element.14), channel_id=1, source_target_pairs={{8,0},{9,1},{10,2},{11,3},{12,4},{13,5},{14,6},{15,7},{16,8},{17,9... | collective-permute-start | bytes 1769480 | tf_op jit(solution)/shard_map/ppermute | solution.py:466
  84.1 24.4 %collective-permute-start = (bf16[4,3,192,128]{3,2,1,0:T(8,128)(2,1)}, bf16[4,3,192,128]{3,2,1,0:T(8,128)(2,1)}, u32[]{:S(2)}, u32[]{:S(2)}) collective-permute-start(bf16[4,3,192,128]{3,2,1,0:T(8,128)(2,1)} %get-tuple-element.16), channel_id=1, source_target_pairs={{0,8},{1,9},{2,10},{3,11},{4,12},{5,13},{6,14},{7,15},{8,16},{9,17... | collective-permute-start | bytes 1769480 | tf_op jit(solution)/shard_map/ppermute | solution.py:465
  98.5 16.0 %copy-start.2 = (s32[24,12]{0,1:T(8,128)S(1)}, s32[24,12]{0,1:T(8,128)}, u32[]{:S(2)}) copy-start(s32[24,12]{0,1:T(8,128)} %param.9) | copy-start | bytes 3460
  98.5 35.7 %collective-permute-start.5 = (bf16[4,3,192,128]{3,2,1,0:T(8,128)(2,1)}, bf16[4,3,192,128]{3,2,1,0:T(8,128)(2,1)}, u32[]{:S(2)}, u32[]{:S(2)}) collective-permute-start(bf16[4,3,192,128]{3,2,1,0:T(8,128)(2,1)} %broadcast_select_fusion), channel_id=1, source_target_pairs={{0,32},{1,39},{2,34},{3,33},{4,36},{5,35},{6,38},{7,37},{24,56},{2... | collective-permute-start | bytes 1769480 | tf_op jit(solution)/shard_map/ppermute | solution.py:468
  110.4 23.9 %collective-permute-start.4 = (bf16[4,3,192,128]{3,2,1,0:T(8,128)(2,1)}, bf16[4,3,192,128]{3,2,1,0:T(8,128)(2,1)}, u32[]{:S(2)}, u32[]{:S(2)}) collective-permute-start(bf16[4,3,192,128]{3,2,1,0:T(8,128)(2,1)} %broadcast_select_fusion.1), channel_id=1, source_target_pairs={{0,32},{1,39},{2,34},{3,33},{4,36},{5,35},{6,38},{7,37},{24,56},{2... | collective-permute-start | bytes 1769480 | tf_op jit(solution)/shard_map/ppermute | solution.py:468
  127.1 0.7 copy-start.1
  127.8 6.4 %copy-start = (s32[36,8]{1,0:T(8,128)S(1)}, s32[36,8]{1,0:T(8,128)}, u32[]{:S(2)}) copy-start(s32[36,8]{1,0:T(8,128)} %get-tuple-element.9.halo_ref) | copy-start | bytes 3460

commit v7 on v6

--- a/solution.py
+++ b/solution.py
@@ -10,6 +10,7 @@
 VMEM_BYTES = 60 * 1024 * 1024
 ROW = 4
 OWN_SLOTS = 16
+INNER, OUTER, CROSSED = range(3)
 HALO_SLOTS = 8
 
 
@@ -274,9 +275,9 @@
     )(inside, own, query)
 
 
-def attend_halo(query, left, right, crossed, mixed, stats, halo, ends, tile_len):
+def attend_halo(query, outer, inner, crossed, mixed, stats, halo, kinds, tile_len):
     sources, _, heads, tokens, head_dim = query.shape
-    half = left[0].shape[0]
+    half = inner.shape[0]
     rows = sources * tokens
     halo_rows = 2 * half * tokens
     halo_tiles = halo_rows // tile_len
@@ -285,44 +286,41 @@
     factor = math.log2(math.e) / math.sqrt(head_dim)
     needs = [max(reach - tile, tile - tiles_here + 1 + reach) for tile in range(tiles_here)]
 
-    def kernel(halo_ref, ends_ref, query_ref, left_k, left_v, right_k, right_v, crossed_k, crossed_v,
+    def kernel(halo_ref, kinds_ref, query_ref, outer_k, outer_v, crossed_k, crossed_v, inner_ref,
                mixed_ref, stats_ref, out_ref, buf, query_buf, sems):
         def query_copy(head):
             return pltpu.make_async_copy(
                 query_ref.at[:, 0, head], query_buf.at[head], sems.at[head, 0]
             )
 
-        def side_copy(head, index, side, ref):
+        def side_copy(head, index, side, kind):
+            if kind == INNER:
+                source = inner_ref.at[:, index, head]
+            elif kind == OUTER:
+                source = (outer_k, outer_v)[index].at[:, head]
+            else:
+                source = (crossed_k, crossed_v)[index].at[:, head]
             return pltpu.make_async_copy(
-                ref.at[:, head],
+                source,
                 buf.at[index, head, pl.ds(side * half, half)],
                 sems.at[head, 1 + 2 * index + side],
             )
 
-        sides = [
-            (0, 0, left_k, crossed_k),
-            (0, 1, right_k, crossed_k),
-            (1, 0, left_v, crossed_v),
-            (1, 1, right_v, crossed_v),
-        ]
         for head in range(heads):
             query_copy(head).start()
-            for index, side, straight, other in sides:
-                is_other = ends_ref[side] == 1
-
-                @pl.when(is_other)
-                def _():
-                    side_copy(head, index, side, other).start()
-
-                @pl.when(jnp.logical_not(is_other))
-                def _():
-                    side_copy(head, index, side, straight).start()
+            for side in range(2):
+                for kind in (INNER, OUTER, CROSSED):
+                    @pl.when(kinds_ref[side] == kind)
+                    def _():
+                        for index in range(2):
+                            side_copy(head, index, side, kind).start()
 
         @pl.loop(0, heads)
         def _(head):
             query_copy(head).wait()
-            for index, side, straight, _ in sides:
-                side_copy(head, index, side, straight).wait()
+            for side in range(2):
+                for index in range(2):
+                    side_copy(head, index, side, INNER).wait()
             key_rows, value_rows = [
                 buf.at[index, head].reshape(halo_rows, head_dim) for index in range(2)
             ]
@@ -372,7 +370,7 @@
     pairs = heads * tiles_here * (HALO_SLOTS - 2) // 2
     return pl.pallas_call(
         kernel,
-        in_specs=[smem, smem] + [hbm] * 7 + [vmem, vmem],
+        in_specs=[smem, smem] + [hbm] * 6 + [vmem, vmem],
         out_specs=vmem,
         out_shape=jax.ShapeDtypeStruct((rows, heads * head_dim), jnp.bfloat16),
         scratch_shapes=[
@@ -386,32 +384,38 @@
             bytes_accessed=2 * heads * head_dim * (2 * halo_rows + 6 * rows),
             transcendentals=pairs * tile_len * tile_len,
         ),
-    )(halo, ends, query, *left, *right, *crossed, mixed, stats)
+    )(halo, kinds, query, *outer, *crossed, inner, mixed, stats)
 
 
 def routes(blocks, group_size):
-    on = []
-    across = []
-    for block in range(blocks):
+    def on(block):
         there = block + 1
         if there % ROW == 0:
             there = block + 1 - ROW if odd_row(block) == 0 else block + 1 + ROW
-        if there < blocks:
-            on += [(block * group_size + m, there * group_size + m) for m in range(group_size)]
+        return there
+
+    def back(block):
+        there = block - 1
+        if block % ROW == 0:
+            there = block - 1 + ROW if odd_row(block) == 1 else block - 1 - ROW
+        return there
+
+    outer, inner, across = [], [], []
+    for block in range(blocks):
+        odd_place = block % 2 == 1
+        for pairs, there in (
+            (outer, on(block) if odd_place else back(block)),
+            (inner, back(block) if odd_place else on(block)),
+        ):
+            if 0 <= there < blocks:
+                pairs += [(block * group_size + m, there * group_size + m) for m in range(group_size)]
         if block % ROW in (0, ROW - 1):
             other = block + ROW if odd_row(block) == 0 else block - ROW
             across += [
                 tuple(at * group_size + owner_of(at, head_block, group_size) for at in (block, other))
                 for head_block in range(group_size)
             ]
-    back = []
-    for block in range(blocks):
-        there = block - 1
-        if block % ROW == 0:
-            there = block - 1 + ROW if odd_row(block) == 1 else block - 1 - ROW
-        if there >= 0:
-            back += [(block * group_size + m, there * group_size + m) for m in range(group_size)]
-    return on, back, across
+    return outer, inner, across
 
 
 def assemble(parts):
@@ -452,23 +456,31 @@
         return lax.all_to_all(array, "head", split_axis=0, concat_axis=0, tiled=True)
 
     own = exchange(prepare([keys, values], [True, False], group_size, per_device, head_dim))
-    query = exchange(prepare([queries], [True], group_size, per_device, head_dim))
     block = lax.axis_index("seq")
     head_block = owner_block(lax.axis_index("head"), odd_row(block), group_size)
     place = jnp.stack([head_block * per_device, block * tiles_here]).astype(jnp.int32)
-    at_start = block % ROW == 0
-    ends = jnp.stack([at_start, block % ROW == ROW - 1]).astype(jnp.int32)
+    x = block % ROW
+    odd_place = x % 2 == 1
+    kinds = jnp.stack(
+        [
+            jnp.where(odd_place, INNER, jnp.where(x == 0, CROSSED, OUTER)),
+            jnp.where(odd_place, jnp.where(x == ROW - 1, CROSSED, OUTER), INNER),
+        ]
+    ).astype(jnp.int32)
     listed = neighbours.reshape(head_count, -1)
     inside, halo = sort_lists(listed, counts, place, tiles_here, per_device, halo_tiles)
-    on, back, across = routes(blocks, group_size)
+    queries, inside, halo, kinds = lax.optimization_barrier((queries, inside, halo, kinds))
+    query = exchange(prepare([queries], [True], group_size, per_device, head_dim))
+    outer_route, inner_route, across = routes(blocks, group_size)
     both = ("seq", "head")
-    left = [lax.ppermute(own[group_size - half :, index], both, on) for index in range(2)]
-    right = [lax.ppermute(own[:half, index], both, back) for index in range(2)]
-    crossed = [
-        lax.ppermute(jnp.where(at_start, one, two), both, across) for one, two in zip(left, right)
-    ]
+    first = jnp.where(odd_place, half, 0)
+    outer_part = lax.dynamic_slice_in_dim(own, first, half, 0)
+    inner_part = lax.dynamic_slice_in_dim(own, half - first, half, 0)
+    outer = [lax.ppermute(outer_part[:, index], both, outer_route) for index in range(2)]
+    inner = lax.ppermute(inner_part, both, inner_route)
+    crossed = [lax.ppermute(part, both, across) for part in outer]
     mixed, stats = attend_local(own, query, inside, tile_len)
-    result = attend_halo(query, left, right, crossed, mixed, stats, halo, ends, tile_len)
+    result = attend_halo(query, outer, inner, crossed, mixed, stats, halo, kinds, tile_len)
     result = exchange(result.reshape(group_size, local_tokens, per_device * head_dim))
     return assemble(result)
 

time: 185 us -> 165 us (0.89)
  waiting for transfers between devices: 70.7 us -> 61.7 us
  starting transfers between devices: 32.5 us -> 28.1 us
  other arithmetic: 4.64 us -> 0.58 us
  local copies, waits for them, and re-layouts: 5.93 us -> 3.31 us
    all_to_all x2, waiting for transfers between devices: 54.4 us -> 44.3 us  [exchange(): lax.all_to_all(array, 'head', split_axis=0, concat_axis=0, tiled=True)]
    ppermute x6 -> x5, starting transfers between devices: 21.8 us -> 17.3 us  [the longest x2 8.04 us: body(): crossed = [lax.ppermute(part, both, across) for part in outer]]
    select_n x2 -> x0, other arithmetic: 3.9 us -> none  [body(): jnp.where(at_start, one, two)]
    reshape x2, local copies, waits for them, and re-layouts: 3.09 us -> 0.69 us  [body(): listed = neighbours.reshape(head_count, -1)]
    ppermute x6 -> x5, waiting for transfers between devices: 16.3 us -> 17.4 us  [the longest x2 17 us: body(): lax.ppermute(outer_part[:, index], both, outer_route)]
  transfers between devices with their start and end apart: 8 -> 7, of which waited for: 5 -> 4; matrix products, arithmetic and copies ran while one was open for 5% -> 2% of each run, Pallas kernels for 9% -> 11%
where the time goes in v7:
time: 165 us; the launch traced here: 164 us
  waiting for transfers between devices  61.7 us (37%)
  blocking collectives  41.3 us (25%)
  Pallas kernels  28.4 us (17%)
  starting transfers between devices  28.1 us (17%)
  local copies, waits for them, and re-layouts  3.31 us (2%)
    all_to_all x2, waiting for transfers between devices, exchange(): lax.all_to_all(array, 'head', split_axis=0, concat_axis=0, tiled=True)  44.3 us
    all_to_all x1, blocking collectives, exchange(): lax.all_to_all(array, 'head', split_axis=0, concat_axis=0, tiled=True)  41.3 us
    ppermute x2, waiting for transfers between devices, body(): lax.ppermute(outer_part[:, index], both, outer_route)  17 us
    all_to_all x2, starting transfers between devices, exchange(): lax.all_to_all(array, 'head', split_axis=0, concat_axis=0, tiled=True)  10.8 us
    pallas_call x1, Pallas kernels, sort_lists(): pl.pallas_call(kernel, in_specs=[smem, smem, smem], out_specs=[smem, smem...  8.08 us
    ppermute x2, starting transfers between devices, body(): crossed = [lax.ppermute(part, both, across) for part in outer]  8.04 us
    ppermute x2, starting transfers between devices, body(): lax.ppermute(outer_part[:, index], both, outer_route)  7.07 us
    pallas_call x1, Pallas kernels, attend_local(): pl.pallas_call(kernel, in_specs=[smem, hbm, hbm], out_specs=[vmem, vmem],...  7.01 us
  transfers between devices with their start and end apart: 7, of which 4 were waited for; matrix products, arithmetic and copies ran while one was open for 2% of the time, Pallas kernels for 11%

profile of v7, /device:TPU:448, one launch (start us, length us, event | category | flops | bytes accessed | tf_op | source)
XLA Modules:
  0.0 163.6 jit_solution(5211538737884358424)
XLA Ops:
  0.0 3.2 %shard_map.57 = bf16[8,2,3,192,128]{4,3,2,1,0:T(8,128)(2,1)} custom-call(bf16[192,3072]{1,0:T(8,128)(2,1)} %refs_0_.2, bf16[192,3072]{1,0:T(8,128)(2,1)} %refs_1_.1), custom_call_target="tpu_custom_call" | custom-call | flops 150994944 | bytes 4718592 | tf_op jit(solution)/shard_map/pallas_call | solution.py:65
  3.2 0.0 copy-start.2
  3.2 0.0 copy-start.3
  3.2 7.2 %all-to-all-start.1 = ((bf16[8,2,3,192,128]{4,3,2,1,0:T(8,128)(2,1)}), bf16[8,2,3,192,128]{4,3,2,1,0:T(8,128)(2,1)S(1)}, u32[]{:S(2)}, u32[]{:S(2)}) async-start(bf16[8,2,3,192,128]{4,3,2,1,0:T(8,128)(2,1)} %shard_map.57), calls=%async_computation.1 | async-start | bytes 4718592 | tf_op jit(solution)/shard_map/all_to_all | solution.py:456
  10.4 0.0 copy-done.2
  10.4 0.7 copy.8.listed_ref
  11.1 0.0 copy-done.3
  11.1 0.7 copy.9.counts_ref
  11.8 0.6 pad_add_fusion
  12.4 8.1 %shard_map.55 = (s32[36,16]{1,0:T(8,128)}, s32[36,8]{1,0:T(8,128)}) custom-call(s32[2]{0:T(128)} %get-tuple-element.23.place_ref, s32[24,144]{1,0:T(8,128)} %copy.8.listed_ref, s32[24,12]{1,0:T(8,128)} %copy.9.counts_ref), custom_call_target="tpu_custom_call" | custom-call | tf_op jit(solution)/shard_map/pallas_call | solution.py:165
  20.5 2.7 %shard_map.56 = bf16[8,1,3,192,128]{4,3,2,1,0:T(8,128)(2,1)} custom-call(bf16[192,3072]{1,0:T(8,128)(2,1)} %refs_0_.1), custom_call_target="tpu_custom_call" | custom-call | flops 150994944 | bytes 2359296 | tf_op jit(solution)/shard_map/pallas_call | solution.py:65
  23.2 44.3 %all-to-all-done.1.own_ref = bf16[8,2,3,192,128]{4,3,2,1,0:T(8,128)(2,1)S(1)} async-done(((bf16[8,2,3,192,128]{4,3,2,1,0:T(8,128)(2,1)}), bf16[8,2,3,192,128]{4,3,2,1,0:T(8,128)(2,1)S(1)}, u32[]{:S(2)}, u32[]{:S(2)}) %all-to-all-start.1) | async-done | bytes 2359328 | tf_op jit(solution)/shard_map/all_to_all | solution.py:456
  67.5 3.6 %all-to-all-start = ((bf16[8,1,3,192,128]{4,3,2,1,0:T(8,128)(2,1)}), bf16[8,1,3,192,128]{4,3,2,1,0:T(8,128)(2,1)S(1)}, u32[]{:S(2)}, u32[]{:S(2)}) async-start(bf16[8,1,3,192,128]{4,3,2,1,0:T(8,128)(2,1)} %shard_map.56), calls=%async_computation | async-start | bytes 2359296 | tf_op jit(solution)/shard_map/all_to_all | solution.py:456
  71.0 0.1 dynamic-slice_bitcast_fusion
  71.1 4.7 %collective-permute-start = (bf16[4,3,192,128]{3,2,1,0:T(8,128)(2,1)S(1)}, bf16[4,3,192,128]{3,2,1,0:T(8,128)(2,1)}, u32[]{:S(2)}, u32[]{:S(2)}) collective-permute-start(bf16[4,3,192,128]{3,2,1,0:T(8,128)(2,1)S(1)} %get-tuple-element.22), channel_id=1, source_target_pairs={{8,16},{9,17},{10,18},{11,19},{12,20},{13,21},{14,22},{15,23},{16,... | collective-permute-start | bytes 1769480 | tf_op jit(solution)/shard_map/ppermute | solution.py:479
  75.8 2.4 %collective-permute-start.1 = (bf16[4,3,192,128]{3,2,1,0:T(8,128)(2,1)S(1)}, bf16[4,3,192,128]{3,2,1,0:T(8,128)(2,1)}, u32[]{:S(2)}, u32[]{:S(2)}) collective-permute-start(bf16[4,3,192,128]{3,2,1,0:T(8,128)(2,1)S(1)} %get-tuple-element.21), channel_id=1, source_target_pairs={{8,16},{9,17},{10,18},{11,19},{12,20},{13,21},{14,22},{15,23},{16,... | collective-permute-start | bytes 1769480 | tf_op jit(solution)/shard_map/ppermute | solution.py:479
  78.2 1.1 constant_dynamic-slice_fusion
  79.4 2.2 %collective-permute-start.4 = (bf16[4,2,3,192,128]{4,3,2,1,0:T(8,128)(2,1)}, bf16[4,2,3,192,128]{4,3,2,1,0:T(8,128)(2,1)}, u32[]{:S(2)}, u32[]{:S(2)}) collective-permute-start(bf16[4,2,3,192,128]{4,3,2,1,0:T(8,128)(2,1)} %constant_dynamic-slice_fusion), channel_id=1, source_target_pairs={{0,8},{1,9},{2,10},{3,11},{4,12},{5,13},{6,14},{7,15},{8,0},{9,1},... | collective-permute-start | bytes 3538952 | tf_op jit(solution)/shard_map/ppermute | solution.py:480
  81.6 9.0 %collective-permute-done.outer_k = bf16[4,3,192,128]{3,2,1,0:T(8,128)(2,1)} collective-permute-done((bf16[4,3,192,128]{3,2,1,0:T(8,128)(2,1)S(1)}, bf16[4,3,192,128]{3,2,1,0:T(8,128)(2,1)}, u32[]{:S(2)}, u32[]{:S(2)}) %collective-permute-start) | collective-permute-done | bytes 589856 | tf_op jit(solution)/shard_map/ppermute | solution.py:479
  90.5 4.0 %collective-permute-start.2 = (bf16[4,3,192,128]{3,2,1,0:T(8,128)(2,1)}, bf16[4,3,192,128]{3,2,1,0:T(8,128)(2,1)}, u32[]{:S(2)}, u32[]{:S(2)}) collective-permute-start(bf16[4,3,192,128]{3,2,1,0:T(8,128)(2,1)} %collective-permute-done.outer_k), channel_id=1, source_target_pairs={{0,32},{1,39},{2,34},{3,33},{4,36},{5,35},{6,38},{7,37},{24,56},{2... | collective-permute-start | bytes 1769480 | tf_op jit(solution)/shard_map/ppermute | solution.py:481
  94.6 8.1 %collective-permute-done.1.outer_v = bf16[4,3,192,128]{3,2,1,0:T(8,128)(2,1)} collective-permute-done((bf16[4,3,192,128]{3,2,1,0:T(8,128)(2,1)S(1)}, bf16[4,3,192,128]{3,2,1,0:T(8,128)(2,1)}, u32[]{:S(2)}, u32[]{:S(2)}) %collective-permute-start.1) | collective-permute-done | bytes 589856 | tf_op jit(solution)/shard_map/ppermute | solution.py:479
  102.6 4.0 %collective-permute-start.3 = (bf16[4,3,192,128]{3,2,1,0:T(8,128)(2,1)}, bf16[4,3,192,128]{3,2,1,0:T(8,128)(2,1)}, u32[]{:S(2)}, u32[]{:S(2)}) collective-permute-start(bf16[4,3,192,128]{3,2,1,0:T(8,128)(2,1)} %collective-permute-done.1.outer_v), channel_id=1, source_target_pairs={{0,32},{1,39},{2,34},{3,33},{4,36},{5,35},{6,38},{7,37},{24,56},{2... | collective-permute-start | bytes 1769480 | tf_op jit(solution)/shard_map/ppermute | solution.py:481
  106.6 0.0 all-to-all-done.query_ref
  106.7 0.0 copy-start.1
  106.7 0.7 copy-done.1
  107.4 0.0 copy-start
  107.4 7.0 %shard_map.58 = (f32[1536,384]{1,0:T(8,128)S(1)}, f32[1536,384]{1,0:T(8,128)S(1)}) custom-call(s32[36,16]{1,0:T(8,128)S(1)} %copy-done.1, bf16[8,2,3,192,128]{4,3,2,1,0:T(8,128)(2,1)S(1)} %all-to-all-done.1.own_ref, bf16[8,1,3,192,128]{4,3,2,1,0:T(8,128)(2,1)S(1)} %all-to-all-done.query_ref), custom_call_target="tpu_custom_call" | custom-call | flops 3623878656 | bytes 8257536 | tf_op jit(solution)/shard_map/pallas_call | solution.py:260
  114.4 0.0 collective-permute-done.2.crossed_k
  114.4 0.4 collective-permute-done.3.crossed_v
  114.8 0.0 collective-permute-done.4.inner_ref
  114.8 0.0 copy-done
  114.8 5.3 %shard_map.59 = bf16[1536,384]{1,0:T(8,128)(2,1)S(1)} custom-call(s32[36,8]{1,0:T(8,128)S(1)} %copy-done, s32[2]{0:T(128)S(1)} %get-tuple-element.16.kinds_ref, bf16[8,1,3,192,128]{4,3,2,1,0:T(8,128)(2,1)S(1)} %all-to-all-done.query_ref, bf16[4,3,192,128]{3,2,1,0:T(8,128)(2,1)} %collective-permute-done.outer_k, ...), custom_call_target="tpu_custom_call" | custom-call | flops 905969664 | bytes 9437184 | tf_op jit(solution)/shard_map/pallas_call | solution.py:371
  120.2 41.3 %all_to_all.15.parts_ref = bf16[8,192,384]{2,1,0:T(8,128)(2,1)} all-to-all(bf16[8,192,384]{2,1,0:T(8,128)(2,1)S(1)} %bitcast.11), channel_id=1, replica_groups=mesh['seq'=64,'head'=8] {'head'}, dimensions={0} | all-to-all | bytes 2359296 | tf_op jit(solution)/shard_map/all_to_all | solution.py:456
  161.5 2.1 %shard_map.60 = bf16[192,3072]{1,0:T(8,128)(2,1)} custom-call(bf16[8,192,384]{2,1,0:T(8,128)(2,1)} %all_to_all.15.parts_ref), custom_call_target="tpu_custom_call" | custom-call | bytes 2359296 | tf_op jit(solution)/shard_map/pallas_call | solution.py:431
  (1 shorter events, 0.0 us)
Async XLA Ops:
  3.2 7.2 %copy-start.2 = (s32[24,12,12]{0,2,1:T(8,128)S(1)}, s32[24,12,12]{0,2,1:T(8,128)}, u32[]{:S(2)}) copy-start(s32[24,12,12]{0,2,1:T(8,128)} %param.8) | copy-start | bytes 41476
  3.2 7.9 %copy-start.3 = (s32[24,12]{0,1:T(8,128)S(1)}, s32[24,12]{0,1:T(8,128)}, u32[]{:S(2)}) copy-start(s32[24,12]{0,1:T(8,128)} %param.9) | copy-start | bytes 3460
  3.2 64.3 %all-to-all-start.1 = ((bf16[8,2,3,192,128]{4,3,2,1,0:T(8,128)(2,1)}), bf16[8,2,3,192,128]{4,3,2,1,0:T(8,128)(2,1)S(1)}, u32[]{:S(2)}, u32[]{:S(2)}) async-start(bf16[8,2,3,192,128]{4,3,2,1,0:T(8,128)(2,1)} %shard_map.57), calls=%async_computation.1 | async-start | bytes 4718592 | tf_op jit(solution)/shard_map/all_to_all | solution.py:456
  67.5 39.2 %all-to-all-start = ((bf16[8,1,3,192,128]{4,3,2,1,0:T(8,128)(2,1)}), bf16[8,1,3,192,128]{4,3,2,1,0:T(8,128)(2,1)S(1)}, u32[]{:S(2)}, u32[]{:S(2)}) async-start(bf16[8,1,3,192,128]{4,3,2,1,0:T(8,128)(2,1)} %shard_map.56), calls=%async_computation | async-start | bytes 2359296 | tf_op jit(solution)/shard_map/all_to_all | solution.py:456
  71.1 19.4 %collective-permute-start = (bf16[4,3,192,128]{3,2,1,0:T(8,128)(2,1)S(1)}, bf16[4,3,192,128]{3,2,1,0:T(8,128)(2,1)}, u32[]{:S(2)}, u32[]{:S(2)}) collective-permute-start(bf16[4,3,192,128]{3,2,1,0:T(8,128)(2,1)S(1)} %get-tuple-element.22), channel_id=1, source_target_pairs={{8,16},{9,17},{10,18},{11,19},{12,20},{13,21},{14,22},{15,23},{16,... | collective-permute-start | bytes 1769480 | tf_op jit(solution)/shard_map/ppermute | solution.py:479
  75.8 26.8 %collective-permute-start.1 = (bf16[4,3,192,128]{3,2,1,0:T(8,128)(2,1)S(1)}, bf16[4,3,192,128]{3,2,1,0:T(8,128)(2,1)}, u32[]{:S(2)}, u32[]{:S(2)}) collective-permute-start(bf16[4,3,192,128]{3,2,1,0:T(8,128)(2,1)S(1)} %get-tuple-element.21), channel_id=1, source_target_pairs={{8,16},{9,17},{10,18},{11,19},{12,20},{13,21},{14,22},{15,23},{16,... | collective-permute-start | bytes 1769480 | tf_op jit(solution)/shard_map/ppermute | solution.py:479
  79.4 35.5 %collective-permute-start.4 = (bf16[4,2,3,192,128]{4,3,2,1,0:T(8,128)(2,1)}, bf16[4,2,3,192,128]{4,3,2,1,0:T(8,128)(2,1)}, u32[]{:S(2)}, u32[]{:S(2)}) collective-permute-start(bf16[4,2,3,192,128]{4,3,2,1,0:T(8,128)(2,1)} %constant_dynamic-slice_fusion), channel_id=1, source_target_pairs={{0,8},{1,9},{2,10},{3,11},{4,12},{5,13},{6,14},{7,15},{8,0},{9,1},... | collective-permute-start | bytes 3538952 | tf_op jit(solution)/shard_map/ppermute | solution.py:480
  90.5 23.9 %collective-permute-start.2 = (bf16[4,3,192,128]{3,2,1,0:T(8,128)(2,1)}, bf16[4,3,192,128]{3,2,1,0:T(8,128)(2,1)}, u32[]{:S(2)}, u32[]{:S(2)}) collective-permute-start(bf16[4,3,192,128]{3,2,1,0:T(8,128)(2,1)} %collective-permute-done.outer_k), channel_id=1, source_target_pairs={{0,32},{1,39},{2,34},{3,33},{4,36},{5,35},{6,38},{7,37},{24,56},{2... | collective-permute-start | bytes 1769480 | tf_op jit(solution)/shard_map/ppermute | solution.py:481
  102.6 12.2 %collective-permute-start.3 = (bf16[4,3,192,128]{3,2,1,0:T(8,128)(2,1)}, bf16[4,3,192,128]{3,2,1,0:T(8,128)(2,1)}, u32[]{:S(2)}, u32[]{:S(2)}) collective-permute-start(bf16[4,3,192,128]{3,2,1,0:T(8,128)(2,1)} %collective-permute-done.1.outer_v), channel_id=1, source_target_pairs={{0,32},{1,39},{2,34},{3,33},{4,36},{5,35},{6,38},{7,37},{24,56},{2... | collective-permute-start | bytes 1769480 | tf_op jit(solution)/shard_map/ppermute | solution.py:481
  106.7 0.7 copy-start.1
  107.4 7.4 %copy-start = (s32[36,8]{1,0:T(8,128)S(1)}, s32[36,8]{1,0:T(8,128)}, u32[]{:S(2)}) copy-start(s32[36,8]{1,0:T(8,128)} %get-tuple-element.15.halo_ref) | copy-start | bytes 3460

commit v8 on v7

--- a/solution.py
+++ b/solution.py
@@ -9,6 +9,7 @@
 
 VMEM_BYTES = 60 * 1024 * 1024
 ROW = 4
+STEP_TILES = 6
 OWN_SLOTS = 16
 INNER, OUTER, CROSSED = range(3)
 HALO_SLOTS = 8
@@ -174,8 +175,8 @@
 
 
 def tiles_of_step(step, tiles_here):
-    last = tiles_here - 1
-    return [2 * step, 2 * step + 1, last - 2 * step, last - 1 - 2 * step]
+    first = [STEP_TILES // 2 * step + number for number in range(STEP_TILES // 2)]
+    return first + [tiles_here - 1 - tile for tile in first]
 
 
 def most_of(limits):
@@ -215,7 +216,7 @@
             ]
             column = pl.ds(pl.multiple_of(head * head_dim, head_dim), head_dim)
 
-            @pl.loop(0, tiles_here // 4)
+            @pl.loop(0, tiles_here // STEP_TILES)
             def _(step):
                 tiles = tiles_of_step(step, tiles_here)
                 lines = [head * tiles_here + tile for tile in tiles]
@@ -319,8 +320,7 @@
         def _(head):
             query_copy(head).wait()
             for side in range(2):
-                for index in range(2):
-                    side_copy(head, index, side, INNER).wait()
+                side_copy(head, 0, side, INNER).wait()
             key_rows, value_rows = [
                 buf.at[index, head].reshape(halo_rows, head_dim) for index in range(2)
             ]
@@ -348,6 +348,8 @@
                     level = stats_ref[here, column]
                     newest = jnp.maximum(level, jnp.max(largest, axis=1, keepdims=True) * factor)
                     begun.append((here, places, scores, newest, jnp.exp2(level - newest)))
+                for side in range(2):
+                    side_copy(head, 1, side, INNER).wait()
                 for here, places, scores, newest, fade in begun:
                     added, update = mix(
                         scores,

time: 165 us -> 167 us (1.012)
  Pallas kernels: 28.4 us -> 30.5 us
  transfers between devices with their start and end apart: 7 -> 7, of which waited for: 4 -> 3; matrix products, arithmetic and copies ran while one was open for 2% -> 2% of each run, Pallas kernels for 11% -> 12%
where the time goes in v8:
time: 167 us; the launch traced here: 165 us
  waiting for transfers between devices  61.3 us (37%)
  blocking collectives  41.2 us (25%)
  Pallas kernels  30.5 us (18%)
  starting transfers between devices  28.1 us (17%)
  local copies, waits for them, and re-layouts  3.31 us (2%)
    all_to_all x2, waiting for transfers between devices, exchange(): lax.all_to_all(array, 'head', split_axis=0, concat_axis=0, tiled=True)  44.3 us
    all_to_all x1, blocking collectives, exchange(): lax.all_to_all(array, 'head', split_axis=0, concat_axis=0, tiled=True)  41.2 us
    ppermute x2, waiting for transfers between devices, body(): lax.ppermute(outer_part[:, index], both, outer_route)  17 us
    all_to_all x2, starting transfers between devices, exchange(): lax.all_to_all(array, 'head', split_axis=0, concat_axis=0, tiled=True)  10.8 us
    pallas_call x1, Pallas kernels, attend_local(): pl.pallas_call(kernel, in_specs=[smem, hbm, hbm], out_specs=[vmem, vmem],...  8.57 us
    pallas_call x1, Pallas kernels, sort_lists(): pl.pallas_call(kernel, in_specs=[smem, smem, smem], out_specs=[smem, smem...  8.08 us
    ppermute x2, starting transfers between devices, body(): crossed = [lax.ppermute(part, both, across) for part in outer]  8.04 us
    ppermute x2, starting transfers between devices, body(): lax.ppermute(outer_part[:, index], both, outer_route)  7.07 us
  transfers between devices with their start and end apart: 7, of which 3 were waited for; matrix products, arithmetic and copies ran while one was open for 2% of the time, Pallas kernels for 12%

profile of v8, /device:TPU:448, one launch (start us, length us, event | category | flops | bytes accessed | tf_op | source)
XLA Modules:
  0.0 165.1 jit_solution(5704115402174189634)
XLA Ops:
  0.0 3.2 %shard_map.57 = bf16[8,2,3,192,128]{4,3,2,1,0:T(8,128)(2,1)} custom-call(bf16[192,3072]{1,0:T(8,128)(2,1)} %refs_0_.2, bf16[192,3072]{1,0:T(8,128)(2,1)} %refs_1_.1), custom_call_target="tpu_custom_call" | custom-call | flops 150994944 | bytes 4718592 | tf_op jit(solution)/shard_map/pallas_call | solution.py:66
  3.2 0.0 copy-start.2
  3.2 0.0 copy-start.3
  3.2 7.2 %all-to-all-start.1 = ((bf16[8,2,3,192,128]{4,3,2,1,0:T(8,128)(2,1)}), bf16[8,2,3,192,128]{4,3,2,1,0:T(8,128)(2,1)S(1)}, u32[]{:S(2)}, u32[]{:S(2)}) async-start(bf16[8,2,3,192,128]{4,3,2,1,0:T(8,128)(2,1)} %shard_map.57), calls=%async_computation.1 | async-start | bytes 4718592 | tf_op jit(solution)/shard_map/all_to_all | solution.py:458
  10.4 0.0 copy-done.2
  10.4 0.7 copy.8.listed_ref
  11.1 0.0 copy-done.3
  11.1 0.7 copy.9.counts_ref
  11.8 0.6 pad_add_fusion
  12.4 8.1 %shard_map.55 = (s32[36,16]{1,0:T(8,128)}, s32[36,8]{1,0:T(8,128)}) custom-call(s32[2]{0:T(128)} %get-tuple-element.23.place_ref, s32[24,144]{1,0:T(8,128)} %copy.8.listed_ref, s32[24,12]{1,0:T(8,128)} %copy.9.counts_ref), custom_call_target="tpu_custom_call" | custom-call | tf_op jit(solution)/shard_map/pallas_call | solution.py:166
  20.5 2.7 %shard_map.56 = bf16[8,1,3,192,128]{4,3,2,1,0:T(8,128)(2,1)} custom-call(bf16[192,3072]{1,0:T(8,128)(2,1)} %refs_0_.1), custom_call_target="tpu_custom_call" | custom-call | flops 150994944 | bytes 2359296 | tf_op jit(solution)/shard_map/pallas_call | solution.py:66
  23.2 44.3 %all-to-all-done.1.own_ref = bf16[8,2,3,192,128]{4,3,2,1,0:T(8,128)(2,1)S(1)} async-done(((bf16[8,2,3,192,128]{4,3,2,1,0:T(8,128)(2,1)}), bf16[8,2,3,192,128]{4,3,2,1,0:T(8,128)(2,1)S(1)}, u32[]{:S(2)}, u32[]{:S(2)}) %all-to-all-start.1) | async-done | bytes 2359328 | tf_op jit(solution)/shard_map/all_to_all | solution.py:458
  67.5 3.6 %all-to-all-start = ((bf16[8,1,3,192,128]{4,3,2,1,0:T(8,128)(2,1)}), bf16[8,1,3,192,128]{4,3,2,1,0:T(8,128)(2,1)S(1)}, u32[]{:S(2)}, u32[]{:S(2)}) async-start(bf16[8,1,3,192,128]{4,3,2,1,0:T(8,128)(2,1)} %shard_map.56), calls=%async_computation | async-start | bytes 2359296 | tf_op jit(solution)/shard_map/all_to_all | solution.py:458
  71.0 0.1 dynamic-slice_bitcast_fusion
  71.1 4.7 %collective-permute-start = (bf16[4,3,192,128]{3,2,1,0:T(8,128)(2,1)S(1)}, bf16[4,3,192,128]{3,2,1,0:T(8,128)(2,1)}, u32[]{:S(2)}, u32[]{:S(2)}) collective-permute-start(bf16[4,3,192,128]{3,2,1,0:T(8,128)(2,1)S(1)} %get-tuple-element.22), channel_id=1, source_target_pairs={{8,16},{9,17},{10,18},{11,19},{12,20},{13,21},{14,22},{15,23},{16,... | collective-permute-start | bytes 1769480 | tf_op jit(solution)/shard_map/ppermute | solution.py:481
  75.8 2.4 %collective-permute-start.1 = (bf16[4,3,192,128]{3,2,1,0:T(8,128)(2,1)S(1)}, bf16[4,3,192,128]{3,2,1,0:T(8,128)(2,1)}, u32[]{:S(2)}, u32[]{:S(2)}) collective-permute-start(bf16[4,3,192,128]{3,2,1,0:T(8,128)(2,1)S(1)} %get-tuple-element.21), channel_id=1, source_target_pairs={{8,16},{9,17},{10,18},{11,19},{12,20},{13,21},{14,22},{15,23},{16,... | collective-permute-start | bytes 1769480 | tf_op jit(solution)/shard_map/ppermute | solution.py:481
  78.2 1.1 constant_dynamic-slice_fusion
  79.4 2.2 %collective-permute-start.4 = (bf16[4,2,3,192,128]{4,3,2,1,0:T(8,128)(2,1)}, bf16[4,2,3,192,128]{4,3,2,1,0:T(8,128)(2,1)}, u32[]{:S(2)}, u32[]{:S(2)}) collective-permute-start(bf16[4,2,3,192,128]{4,3,2,1,0:T(8,128)(2,1)} %constant_dynamic-slice_fusion), channel_id=1, source_target_pairs={{0,8},{1,9},{2,10},{3,11},{4,12},{5,13},{6,14},{7,15},{8,0},{9,1},... | collective-permute-start | bytes 3538952 | tf_op jit(solution)/shard_map/ppermute | solution.py:482
  81.6 9.0 %collective-permute-done.outer_k = bf16[4,3,192,128]{3,2,1,0:T(8,128)(2,1)} collective-permute-done((bf16[4,3,192,128]{3,2,1,0:T(8,128)(2,1)S(1)}, bf16[4,3,192,128]{3,2,1,0:T(8,128)(2,1)}, u32[]{:S(2)}, u32[]{:S(2)}) %collective-permute-start) | collective-permute-done | bytes 589856 | tf_op jit(solution)/shard_map/ppermute | solution.py:481
  90.5 4.0 %collective-permute-start.2 = (bf16[4,3,192,128]{3,2,1,0:T(8,128)(2,1)}, bf16[4,3,192,128]{3,2,1,0:T(8,128)(2,1)}, u32[]{:S(2)}, u32[]{:S(2)}) collective-permute-start(bf16[4,3,192,128]{3,2,1,0:T(8,128)(2,1)} %collective-permute-done.outer_k), channel_id=1, source_target_pairs={{0,32},{1,39},{2,34},{3,33},{4,36},{5,35},{6,38},{7,37},{24,56},{2... | collective-permute-start | bytes 1769480 | tf_op jit(solution)/shard_map/ppermute | solution.py:483
  94.6 8.1 %collective-permute-done.1.outer_v = bf16[4,3,192,128]{3,2,1,0:T(8,128)(2,1)} collective-permute-done((bf16[4,3,192,128]{3,2,1,0:T(8,128)(2,1)S(1)}, bf16[4,3,192,128]{3,2,1,0:T(8,128)(2,1)}, u32[]{:S(2)}, u32[]{:S(2)}) %collective-permute-start.1) | collective-permute-done | bytes 589856 | tf_op jit(solution)/shard_map/ppermute | solution.py:481
  102.6 4.0 %collective-permute-start.3 = (bf16[4,3,192,128]{3,2,1,0:T(8,128)(2,1)}, bf16[4,3,192,128]{3,2,1,0:T(8,128)(2,1)}, u32[]{:S(2)}, u32[]{:S(2)}) collective-permute-start(bf16[4,3,192,128]{3,2,1,0:T(8,128)(2,1)} %collective-permute-done.1.outer_v), channel_id=1, source_target_pairs={{0,32},{1,39},{2,34},{3,33},{4,36},{5,35},{6,38},{7,37},{24,56},{2... | collective-permute-start | bytes 1769480 | tf_op jit(solution)/shard_map/ppermute | solution.py:483
  106.6 0.0 all-to-all-done.query_ref
  106.7 0.0 copy-start.1
  106.7 0.7 copy-done.1
  107.4 0.0 copy-start
  107.4 8.6 %shard_map.58 = (f32[1536,384]{1,0:T(8,128)S(1)}, f32[1536,384]{1,0:T(8,128)S(1)}) custom-call(s32[36,16]{1,0:T(8,128)S(1)} %copy-done.1, bf16[8,2,3,192,128]{4,3,2,1,0:T(8,128)(2,1)S(1)} %all-to-all-done.1.own_ref, bf16[8,1,3,192,128]{4,3,2,1,0:T(8,128)(2,1)S(1)} %all-to-all-done.query_ref), custom_call_target="tpu_custom_call" | custom-call | flops 3623878656 | bytes 8257536 | tf_op jit(solution)/shard_map/pallas_call | solution.py:261
  116.0 0.0 collective-permute-done.2.crossed_k
  116.0 0.0 collective-permute-done.3.crossed_v
  116.0 0.0 collective-permute-done.4.inner_ref
  116.0 0.0 copy-done
  116.0 5.8 %shard_map.59 = bf16[1536,384]{1,0:T(8,128)(2,1)S(1)} custom-call(s32[36,8]{1,0:T(8,128)S(1)} %copy-done, s32[2]{0:T(128)S(1)} %get-tuple-element.16.kinds_ref, bf16[8,1,3,192,128]{4,3,2,1,0:T(8,128)(2,1)S(1)} %all-to-all-done.query_ref, bf16[4,3,192,128]{3,2,1,0:T(8,128)(2,1)} %collective-permute-done.outer_k, ...), custom_call_target="tpu_custom_call" | custom-call | flops 905969664 | bytes 9437184 | tf_op jit(solution)/shard_map/pallas_call | solution.py:373
  121.8 41.2 %all_to_all.15.parts_ref = bf16[8,192,384]{2,1,0:T(8,128)(2,1)} all-to-all(bf16[8,192,384]{2,1,0:T(8,128)(2,1)S(1)} %bitcast.11), channel_id=1, replica_groups=mesh['seq'=64,'head'=8] {'head'}, dimensions={0} | all-to-all | bytes 2359296 | tf_op jit(solution)/shard_map/all_to_all | solution.py:458
  163.0 2.1 %shard_map.60 = bf16[192,3072]{1,0:T(8,128)(2,1)} custom-call(bf16[8,192,384]{2,1,0:T(8,128)(2,1)} %all_to_all.15.parts_ref), custom_call_target="tpu_custom_call" | custom-call | bytes 2359296 | tf_op jit(solution)/shard_map/pallas_call | solution.py:433
  (1 shorter events, 0.0 us)
Async XLA Ops:
  3.2 7.2 %copy-start.2 = (s32[24,12,12]{0,2,1:T(8,128)S(1)}, s32[24,12,12]{0,2,1:T(8,128)}, u32[]{:S(2)}) copy-start(s32[24,12,12]{0,2,1:T(8,128)} %param.8) | copy-start | bytes 41476
  3.2 7.9 %copy-start.3 = (s32[24,12]{0,1:T(8,128)S(1)}, s32[24,12]{0,1:T(8,128)}, u32[]{:S(2)}) copy-start(s32[24,12]{0,1:T(8,128)} %param.9) | copy-start | bytes 3460
  3.2 64.3 %all-to-all-start.1 = ((bf16[8,2,3,192,128]{4,3,2,1,0:T(8,128)(2,1)}), bf16[8,2,3,192,128]{4,3,2,1,0:T(8,128)(2,1)S(1)}, u32[]{:S(2)}, u32[]{:S(2)}) async-start(bf16[8,2,3,192,128]{4,3,2,1,0:T(8,128)(2,1)} %shard_map.57), calls=%async_computation.1 | async-start | bytes 4718592 | tf_op jit(solution)/shard_map/all_to_all | solution.py:458
  67.5 39.2 %all-to-all-start = ((bf16[8,1,3,192,128]{4,3,2,1,0:T(8,128)(2,1)}), bf16[8,1,3,192,128]{4,3,2,1,0:T(8,128)(2,1)S(1)}, u32[]{:S(2)}, u32[]{:S(2)}) async-start(bf16[8,1,3,192,128]{4,3,2,1,0:T(8,128)(2,1)} %shard_map.56), calls=%async_computation | async-start | bytes 2359296 | tf_op jit(solution)/shard_map/all_to_all | solution.py:458
  71.1 19.4 %collective-permute-start = (bf16[4,3,192,128]{3,2,1,0:T(8,128)(2,1)S(1)}, bf16[4,3,192,128]{3,2,1,0:T(8,128)(2,1)}, u32[]{:S(2)}, u32[]{:S(2)}) collective-permute-start(bf16[4,3,192,128]{3,2,1,0:T(8,128)(2,1)S(1)} %get-tuple-element.22), channel_id=1, source_target_pairs={{8,16},{9,17},{10,18},{11,19},{12,20},{13,21},{14,22},{15,23},{16,... | collective-permute-start | bytes 1769480 | tf_op jit(solution)/shard_map/ppermute | solution.py:481
  75.8 26.8 %collective-permute-start.1 = (bf16[4,3,192,128]{3,2,1,0:T(8,128)(2,1)S(1)}, bf16[4,3,192,128]{3,2,1,0:T(8,128)(2,1)}, u32[]{:S(2)}, u32[]{:S(2)}) collective-permute-start(bf16[4,3,192,128]{3,2,1,0:T(8,128)(2,1)S(1)} %get-tuple-element.21), channel_id=1, source_target_pairs={{8,16},{9,17},{10,18},{11,19},{12,20},{13,21},{14,22},{15,23},{16,... | collective-permute-start | bytes 1769480 | tf_op jit(solution)/shard_map/ppermute | solution.py:481
  79.4 36.6 %collective-permute-start.4 = (bf16[4,2,3,192,128]{4,3,2,1,0:T(8,128)(2,1)}, bf16[4,2,3,192,128]{4,3,2,1,0:T(8,128)(2,1)}, u32[]{:S(2)}, u32[]{:S(2)}) collective-permute-start(bf16[4,2,3,192,128]{4,3,2,1,0:T(8,128)(2,1)} %constant_dynamic-slice_fusion), channel_id=1, source_target_pairs={{0,8},{1,9},{2,10},{3,11},{4,12},{5,13},{6,14},{7,15},{8,0},{9,1},... | collective-permute-start | bytes 3538952 | tf_op jit(solution)/shard_map/ppermute | solution.py:482
  90.5 25.4 %collective-permute-start.2 = (bf16[4,3,192,128]{3,2,1,0:T(8,128)(2,1)}, bf16[4,3,192,128]{3,2,1,0:T(8,128)(2,1)}, u32[]{:S(2)}, u32[]{:S(2)}) collective-permute-start(bf16[4,3,192,128]{3,2,1,0:T(8,128)(2,1)} %collective-permute-done.outer_k), channel_id=1, source_target_pairs={{0,32},{1,39},{2,34},{3,33},{4,36},{5,35},{6,38},{7,37},{24,56},{2... | collective-permute-start | bytes 1769480 | tf_op jit(solution)/shard_map/ppermute | solution.py:483
  102.6 13.4 %collective-permute-start.3 = (bf16[4,3,192,128]{3,2,1,0:T(8,128)(2,1)}, bf16[4,3,192,128]{3,2,1,0:T(8,128)(2,1)}, u32[]{:S(2)}, u32[]{:S(2)}) collective-permute-start(bf16[4,3,192,128]{3,2,1,0:T(8,128)(2,1)} %collective-permute-done.1.outer_v), channel_id=1, source_target_pairs={{0,32},{1,39},{2,34},{3,33},{4,36},{5,35},{6,38},{7,37},{24,56},{2... | collective-permute-start | bytes 1769480 | tf_op jit(solution)/shard_map/ppermute | solution.py:483
  106.7 0.7 copy-start.1
  107.4 8.6 %copy-start = (s32[36,8]{1,0:T(8,128)S(1)}, s32[36,8]{1,0:T(8,128)}, u32[]{:S(2)}) copy-start(s32[36,8]{1,0:T(8,128)} %get-tuple-element.15.halo_ref) | copy-start | bytes 3460

commit v9 on v8

--- a/solution.py
+++ b/solution.py
@@ -426,17 +426,18 @@
 
     def kernel(parts_ref, out_ref):
         odd = odd_row(lax.axis_index("seq"))
+        first = pl.multiple_of(pl.program_id(0) * step, step)
         for member in range(members):
             column = pl.multiple_of(owner_block(member, odd, members) * width, width)
-            out_ref[:, pl.ds(column, width)] = parts_ref[member]
+            out_ref[:, pl.ds(column, width)] = parts_ref[member, pl.ds(first, step), :]
 
     return pl.pallas_call(
         kernel,
         grid=(tokens // step,),
-        in_specs=[pl.BlockSpec((members, step, width), lambda g: (0, g, 0))],
+        in_specs=[pl.BlockSpec(memory_space=pltpu.VMEM)],
         out_specs=pl.BlockSpec((step, members * width), lambda g: (g, 0)),
         out_shape=jax.ShapeDtypeStruct((tokens, members * width), parts.dtype),
-        compiler_params=pltpu.CompilerParams(vmem_limit_bytes=VMEM_BYTES),
+        compiler_params=pltpu.CompilerParams(vmem_limit_bytes=VMEM_BYTES // 3),
         cost_estimate=pl.CostEstimate(
             flops=0, bytes_accessed=4 * tokens * members * width, transcendentals=0
         ),

time: 167 us -> 164 us (0.982)
  blocking collectives: 41.2 us -> 38.5 us
    all_to_all x1, blocking collectives: 41.2 us -> 38.5 us  [exchange(): lax.all_to_all(array, 'head', split_axis=0, concat_axis=0, tiled=True)]
where the time goes in v9:
time: 164 us; the launch traced here: 162 us
  waiting for transfers between devices  61.3 us (37%)
  blocking collectives  38.5 us (23%)
  Pallas kernels  29.7 us (18%)
  starting transfers between devices  28.1 us (17%)
  local copies, waits for them, and re-layouts  3.31 us (2%)
    all_to_all x2, waiting for transfers between devices, exchange(): lax.all_to_all(array, 'head', split_axis=0, concat_axis=0, tiled=True)  44.3 us
    all_to_all x1, blocking collectives, exchange(): lax.all_to_all(array, 'head', split_axis=0, concat_axis=0, tiled=True)  38.5 us
    ppermute x2, waiting for transfers between devices, body(): lax.ppermute(outer_part[:, index], both, outer_route)  17 us
    all_to_all x2, starting transfers between devices, exchange(): lax.all_to_all(array, 'head', split_axis=0, concat_axis=0, tiled=True)  10.8 us
    pallas_call x1, Pallas kernels, attend_local(): pl.pallas_call(kernel, in_specs=[smem, hbm, hbm], out_specs=[vmem, vmem],...  8.93 us
    pallas_call x1, Pallas kernels, sort_lists(): pl.pallas_call(kernel, in_specs=[smem, smem, smem], out_specs=[smem, smem...  8.08 us
    ppermute x2, starting transfers between devices, body(): crossed = [lax.ppermute(part, both, across) for part in outer]  8.04 us
    ppermute x2, starting transfers between devices, body(): lax.ppermute(outer_part[:, index], both, outer_route)  7.07 us
  transfers between devices with their start and end apart: 7, of which 3 were waited for; matrix products, arithmetic and copies ran while one was open for 2% of the time, Pallas kernels for 12%

profile of v9, /device:TPU:448, one launch (start us, length us, event | category | flops | bytes accessed | tf_op | source)
XLA Modules:
  0.0 161.8 jit_solution(1915200396662016413)
XLA Ops:
  0.0 3.2 %shard_map.57 = bf16[8,2,3,192,128]{4,3,2,1,0:T(8,128)(2,1)} custom-call(bf16[192,3072]{1,0:T(8,128)(2,1)} %refs_0_.2, bf16[192,3072]{1,0:T(8,128)(2,1)} %refs_1_.1), custom_call_target="tpu_custom_call" | custom-call | flops 150994944 | bytes 4718592 | tf_op jit(solution)/shard_map/pallas_call | solution.py:66
  3.2 0.0 copy-start.2
  3.2 0.0 copy-start.3
  3.2 7.2 %all-to-all-start.1 = ((bf16[8,2,3,192,128]{4,3,2,1,0:T(8,128)(2,1)}), bf16[8,2,3,192,128]{4,3,2,1,0:T(8,128)(2,1)S(1)}, u32[]{:S(2)}, u32[]{:S(2)}) async-start(bf16[8,2,3,192,128]{4,3,2,1,0:T(8,128)(2,1)} %shard_map.57), calls=%async_computation.1 | async-start | bytes 4718592 | tf_op jit(solution)/shard_map/all_to_all | solution.py:459
  10.4 0.0 copy-done.2
  10.4 0.7 copy.8.listed_ref
  11.1 0.0 copy-done.3
  11.1 0.7 copy.9.counts_ref
  11.8 0.6 pad_add_fusion
  12.4 8.1 %shard_map.55 = (s32[36,16]{1,0:T(8,128)}, s32[36,8]{1,0:T(8,128)}) custom-call(s32[2]{0:T(128)} %get-tuple-element.23.place_ref, s32[24,144]{1,0:T(8,128)} %copy.8.listed_ref, s32[24,12]{1,0:T(8,128)} %copy.9.counts_ref), custom_call_target="tpu_custom_call" | custom-call | tf_op jit(solution)/shard_map/pallas_call | solution.py:166
  20.5 2.7 %shard_map.56 = bf16[8,1,3,192,128]{4,3,2,1,0:T(8,128)(2,1)} custom-call(bf16[192,3072]{1,0:T(8,128)(2,1)} %refs_0_.1), custom_call_target="tpu_custom_call" | custom-call | flops 150994944 | bytes 2359296 | tf_op jit(solution)/shard_map/pallas_call | solution.py:66
  23.2 44.3 %all-to-all-done.1.own_ref = bf16[8,2,3,192,128]{4,3,2,1,0:T(8,128)(2,1)S(1)} async-done(((bf16[8,2,3,192,128]{4,3,2,1,0:T(8,128)(2,1)}), bf16[8,2,3,192,128]{4,3,2,1,0:T(8,128)(2,1)S(1)}, u32[]{:S(2)}, u32[]{:S(2)}) %all-to-all-start.1) | async-done | bytes 2359328 | tf_op jit(solution)/shard_map/all_to_all | solution.py:459
  67.5 3.6 %all-to-all-start = ((bf16[8,1,3,192,128]{4,3,2,1,0:T(8,128)(2,1)}), bf16[8,1,3,192,128]{4,3,2,1,0:T(8,128)(2,1)S(1)}, u32[]{:S(2)}, u32[]{:S(2)}) async-start(bf16[8,1,3,192,128]{4,3,2,1,0:T(8,128)(2,1)} %shard_map.56), calls=%async_computation | async-start | bytes 2359296 | tf_op jit(solution)/shard_map/all_to_all | solution.py:459
  71.0 0.1 dynamic-slice_bitcast_fusion
  71.1 4.7 %collective-permute-start = (bf16[4,3,192,128]{3,2,1,0:T(8,128)(2,1)S(1)}, bf16[4,3,192,128]{3,2,1,0:T(8,128)(2,1)}, u32[]{:S(2)}, u32[]{:S(2)}) collective-permute-start(bf16[4,3,192,128]{3,2,1,0:T(8,128)(2,1)S(1)} %get-tuple-element.22), channel_id=1, source_target_pairs={{8,16},{9,17},{10,18},{11,19},{12,20},{13,21},{14,22},{15,23},{16,... | collective-permute-start | bytes 1769480 | tf_op jit(solution)/shard_map/ppermute | solution.py:482
  75.8 2.4 %collective-permute-start.1 = (bf16[4,3,192,128]{3,2,1,0:T(8,128)(2,1)S(1)}, bf16[4,3,192,128]{3,2,1,0:T(8,128)(2,1)}, u32[]{:S(2)}, u32[]{:S(2)}) collective-permute-start(bf16[4,3,192,128]{3,2,1,0:T(8,128)(2,1)S(1)} %get-tuple-element.21), channel_id=1, source_target_pairs={{8,16},{9,17},{10,18},{11,19},{12,20},{13,21},{14,22},{15,23},{16,... | collective-permute-start | bytes 1769480 | tf_op jit(solution)/shard_map/ppermute | solution.py:482
  78.2 1.1 constant_dynamic-slice_fusion
  79.4 2.2 %collective-permute-start.4 = (bf16[4,2,3,192,128]{4,3,2,1,0:T(8,128)(2,1)}, bf16[4,2,3,192,128]{4,3,2,1,0:T(8,128)(2,1)}, u32[]{:S(2)}, u32[]{:S(2)}) collective-permute-start(bf16[4,2,3,192,128]{4,3,2,1,0:T(8,128)(2,1)} %constant_dynamic-slice_fusion), channel_id=1, source_target_pairs={{0,8},{1,9},{2,10},{3,11},{4,12},{5,13},{6,14},{7,15},{8,0},{9,1},... | collective-permute-start | bytes 3538952 | tf_op jit(solution)/shard_map/ppermute | solution.py:483
  81.6 9.0 %collective-permute-done.outer_k = bf16[4,3,192,128]{3,2,1,0:T(8,128)(2,1)} collective-permute-done((bf16[4,3,192,128]{3,2,1,0:T(8,128)(2,1)S(1)}, bf16[4,3,192,128]{3,2,1,0:T(8,128)(2,1)}, u32[]{:S(2)}, u32[]{:S(2)}) %collective-permute-start) | collective-permute-done | bytes 589856 | tf_op jit(solution)/shard_map/ppermute | solution.py:482
  90.5 4.0 %collective-permute-start.2 = (bf16[4,3,192,128]{3,2,1,0:T(8,128)(2,1)}, bf16[4,3,192,128]{3,2,1,0:T(8,128)(2,1)}, u32[]{:S(2)}, u32[]{:S(2)}) collective-permute-start(bf16[4,3,192,128]{3,2,1,0:T(8,128)(2,1)} %collective-permute-done.outer_k), channel_id=1, source_target_pairs={{0,32},{1,39},{2,34},{3,33},{4,36},{5,35},{6,38},{7,37},{24,56},{2... | collective-permute-start | bytes 1769480 | tf_op jit(solution)/shard_map/ppermute | solution.py:484
  94.6 8.1 %collective-permute-done.1.outer_v = bf16[4,3,192,128]{3,2,1,0:T(8,128)(2,1)} collective-permute-done((bf16[4,3,192,128]{3,2,1,0:T(8,128)(2,1)S(1)}, bf16[4,3,192,128]{3,2,1,0:T(8,128)(2,1)}, u32[]{:S(2)}, u32[]{:S(2)}) %collective-permute-start.1) | collective-permute-done | bytes 589856 | tf_op jit(solution)/shard_map/ppermute | solution.py:482
  102.6 4.0 %collective-permute-start.3 = (bf16[4,3,192,128]{3,2,1,0:T(8,128)(2,1)}, bf16[4,3,192,128]{3,2,1,0:T(8,128)(2,1)}, u32[]{:S(2)}, u32[]{:S(2)}) collective-permute-start(bf16[4,3,192,128]{3,2,1,0:T(8,128)(2,1)} %collective-permute-done.1.outer_v), channel_id=1, source_target_pairs={{0,32},{1,39},{2,34},{3,33},{4,36},{5,35},{6,38},{7,37},{24,56},{2... | collective-permute-start | bytes 1769480 | tf_op jit(solution)/shard_map/ppermute | solution.py:484
  106.6 0.0 all-to-all-done.query_ref
  106.7 0.0 copy-start.1
  106.7 0.7 copy-done.1
  107.4 0.0 copy-start
  107.4 8.9 %shard_map.58 = (f32[1536,384]{1,0:T(8,128)S(1)}, f32[1536,384]{1,0:T(8,128)S(1)}) custom-call(s32[36,16]{1,0:T(8,128)S(1)} %copy-done.1, bf16[8,2,3,192,128]{4,3,2,1,0:T(8,128)(2,1)S(1)} %all-to-all-done.1.own_ref, bf16[8,1,3,192,128]{4,3,2,1,0:T(8,128)(2,1)S(1)} %all-to-all-done.query_ref), custom_call_target="tpu_custom_call" | custom-call | flops 3623878656 | bytes 8257536 | tf_op jit(solution)/shard_map/pallas_call | solution.py:261
  116.3 0.0 collective-permute-done.2.crossed_k
  116.3 0.0 collective-permute-done.3.crossed_v
  116.3 0.0 collective-permute-done.4.inner_ref
  116.4 0.0 copy-done
  116.4 5.8 %shard_map.59 = bf16[1536,384]{1,0:T(8,128)(2,1)S(1)} custom-call(s32[36,8]{1,0:T(8,128)S(1)} %copy-done, s32[2]{0:T(128)S(1)} %get-tuple-element.16.kinds_ref, bf16[8,1,3,192,128]{4,3,2,1,0:T(8,128)(2,1)S(1)} %all-to-all-done.query_ref, bf16[4,3,192,128]{3,2,1,0:T(8,128)(2,1)} %collective-permute-done.outer_k, ...), custom_call_target="tpu_custom_call" | custom-call | flops 905969664 | bytes 9437184 | tf_op jit(solution)/shard_map/pallas_call | solution.py:373
  122.2 38.5 %all_to_all.15.parts_ref = bf16[8,192,384]{2,1,0:T(8,128)(2,1)S(1)} all-to-all(bf16[8,192,384]{2,1,0:T(8,128)(2,1)S(1)} %bitcast.11), channel_id=1, replica_groups=mesh['seq'=64,'head'=8] {'head'}, dimensions={0} | all-to-all | bytes 2359296 | tf_op jit(solution)/shard_map/all_to_all | solution.py:459
  160.7 1.1 shard_map.60
  (1 shorter events, 0.0 us)
Async XLA Ops:
  3.2 7.2 %copy-start.2 = (s32[24,12,12]{0,2,1:T(8,128)S(1)}, s32[24,12,12]{0,2,1:T(8,128)}, u32[]{:S(2)}) copy-start(s32[24,12,12]{0,2,1:T(8,128)} %param.8) | copy-start | bytes 41476
  3.2 7.9 %copy-start.3 = (s32[24,12]{0,1:T(8,128)S(1)}, s32[24,12]{0,1:T(8,128)}, u32[]{:S(2)}) copy-start(s32[24,12]{0,1:T(8,128)} %param.9) | copy-start | bytes 3460
  3.2 64.3 %all-to-all-start.1 = ((bf16[8,2,3,192,128]{4,3,2,1,0:T(8,128)(2,1)}), bf16[8,2,3,192,128]{4,3,2,1,0:T(8,128)(2,1)S(1)}, u32[]{:S(2)}, u32[]{:S(2)}) async-start(bf16[8,2,3,192,128]{4,3,2,1,0:T(8,128)(2,1)} %shard_map.57), calls=%async_computation.1 | async-start | bytes 4718592 | tf_op jit(solution)/shard_map/all_to_all | solution.py:459
  67.5 39.2 %all-to-all-start = ((bf16[8,1,3,192,128]{4,3,2,1,0:T(8,128)(2,1)}), bf16[8,1,3,192,128]{4,3,2,1,0:T(8,128)(2,1)S(1)}, u32[]{:S(2)}, u32[]{:S(2)}) async-start(bf16[8,1,3,192,128]{4,3,2,1,0:T(8,128)(2,1)} %shard_map.56), calls=%async_computation | async-start | bytes 2359296 | tf_op jit(solution)/shard_map/all_to_all | solution.py:459
  71.1 19.4 %collective-permute-start = (bf16[4,3,192,128]{3,2,1,0:T(8,128)(2,1)S(1)}, bf16[4,3,192,128]{3,2,1,0:T(8,128)(2,1)}, u32[]{:S(2)}, u32[]{:S(2)}) collective-permute-start(bf16[4,3,192,128]{3,2,1,0:T(8,128)(2,1)S(1)} %get-tuple-element.22), channel_id=1, source_target_pairs={{8,16},{9,17},{10,18},{11,19},{12,20},{13,21},{14,22},{15,23},{16,... | collective-permute-start | bytes 1769480 | tf_op jit(solution)/shard_map/ppermute | solution.py:482
  75.8 26.8 %collective-permute-start.1 = (bf16[4,3,192,128]{3,2,1,0:T(8,128)(2,1)S(1)}, bf16[4,3,192,128]{3,2,1,0:T(8,128)(2,1)}, u32[]{:S(2)}, u32[]{:S(2)}) collective-permute-start(bf16[4,3,192,128]{3,2,1,0:T(8,128)(2,1)S(1)} %get-tuple-element.21), channel_id=1, source_target_pairs={{8,16},{9,17},{10,18},{11,19},{12,20},{13,21},{14,22},{15,23},{16,... | collective-permute-start | bytes 1769480 | tf_op jit(solution)/shard_map/ppermute | solution.py:482
  79.4 37.0 %collective-permute-start.4 = (bf16[4,2,3,192,128]{4,3,2,1,0:T(8,128)(2,1)}, bf16[4,2,3,192,128]{4,3,2,1,0:T(8,128)(2,1)}, u32[]{:S(2)}, u32[]{:S(2)}) collective-permute-start(bf16[4,2,3,192,128]{4,3,2,1,0:T(8,128)(2,1)} %constant_dynamic-slice_fusion), channel_id=1, source_target_pairs={{0,8},{1,9},{2,10},{3,11},{4,12},{5,13},{6,14},{7,15},{8,0},{9,1},... | collective-permute-start | bytes 3538952 | tf_op jit(solution)/shard_map/ppermute | solution.py:483
  90.5 25.8 %collective-permute-start.2 = (bf16[4,3,192,128]{3,2,1,0:T(8,128)(2,1)}, bf16[4,3,192,128]{3,2,1,0:T(8,128)(2,1)}, u32[]{:S(2)}, u32[]{:S(2)}) collective-permute-start(bf16[4,3,192,128]{3,2,1,0:T(8,128)(2,1)} %collective-permute-done.outer_k), channel_id=1, source_target_pairs={{0,32},{1,39},{2,34},{3,33},{4,36},{5,35},{6,38},{7,37},{24,56},{2... | collective-permute-start | bytes 1769480 | tf_op jit(solution)/shard_map/ppermute | solution.py:484
  102.6 13.7 %collective-permute-start.3 = (bf16[4,3,192,128]{3,2,1,0:T(8,128)(2,1)}, bf16[4,3,192,128]{3,2,1,0:T(8,128)(2,1)}, u32[]{:S(2)}, u32[]{:S(2)}) collective-permute-start(bf16[4,3,192,128]{3,2,1,0:T(8,128)(2,1)} %collective-permute-done.1.outer_v), channel_id=1, source_target_pairs={{0,32},{1,39},{2,34},{3,33},{4,36},{5,35},{6,38},{7,37},{24,56},{2... | collective-permute-start | bytes 1769480 | tf_op jit(solution)/shard_map/ppermute | solution.py:484
  106.7 0.7 copy-start.1
  107.4 9.0 %copy-start = (s32[36,8]{1,0:T(8,128)S(1)}, s32[36,8]{1,0:T(8,128)}, u32[]{:S(2)}) copy-start(s32[36,8]{1,0:T(8,128)} %get-tuple-element.15.halo_ref) | copy-start | bytes 3460

commit v10 on v9

--- a/solution.py
+++ b/solution.py
@@ -288,11 +288,16 @@
     needs = [max(reach - tile, tile - tiles_here + 1 + reach) for tile in range(tiles_here)]
 
     def kernel(halo_ref, kinds_ref, query_ref, outer_k, outer_v, crossed_k, crossed_v, inner_ref,
-               mixed_ref, stats_ref, out_ref, buf, query_buf, sems):
-        def query_copy(head):
-            return pltpu.make_async_copy(
-                query_ref.at[:, 0, head], query_buf.at[head], sems.at[head, 0]
-            )
+               mixed_ref, stats_ref, out_ref, buf, sems):
+        def query_tile(head, tile):
+            pieces = []
+            at = tile * tile_len
+            while at < (tile + 1) * tile_len:
+                source, row = divmod(at, tokens)
+                length = min(tokens - row, (tile + 1) * tile_len - at)
+                pieces.append(query_ref[source, 0, head, row : row + length, :])
+                at += length
+            return jnp.concatenate(pieces, axis=0) if len(pieces) > 1 else pieces[0]
 
         def side_copy(head, index, side, kind):
             if kind == INNER:
@@ -304,11 +309,10 @@
             return pltpu.make_async_copy(
                 source,
                 buf.at[index, head, pl.ds(side * half, half)],
-                sems.at[head, 1 + 2 * index + side],
+                sems.at[head, 2 * index + side],
             )
 
         for head in range(heads):
-            query_copy(head).start()
             for side in range(2):
                 for kind in (INNER, OUTER, CROSSED):
                     @pl.when(kinds_ref[side] == kind)
@@ -318,13 +322,11 @@
 
         @pl.loop(0, heads)
         def _(head):
-            query_copy(head).wait()
             for side in range(2):
                 side_copy(head, 0, side, INNER).wait()
             key_rows, value_rows = [
                 buf.at[index, head].reshape(halo_rows, head_dim) for index in range(2)
             ]
-            query_rows = query_buf.at[head].reshape(rows, head_dim)
             column = pl.ds(pl.multiple_of(head * head_dim, head_dim), head_dim)
             lines = [head * tiles_here + tile for tile in range(tiles_here)]
             limits = [halo_ref[line, HALO_SLOTS - 1] for line in lines]
@@ -340,7 +342,7 @@
                         continue
                     places = [halo_ref[lines[tile], slot] for slot in range(used)]
                     scores, largest = scores_of(
-                        query_rows[here, :],
+                        query_tile(head, tile),
                         [tile_rows(key_rows, at, halo_tiles, tile_len) for at in places],
                         limits[tile],
                         0,
@@ -372,13 +374,12 @@
     pairs = heads * tiles_here * (HALO_SLOTS - 2) // 2
     return pl.pallas_call(
         kernel,
-        in_specs=[smem, smem] + [hbm] * 6 + [vmem, vmem],
+        in_specs=[smem, smem, vmem] + [hbm] * 5 + [vmem, vmem],
         out_specs=vmem,
         out_shape=jax.ShapeDtypeStruct((rows, heads * head_dim), jnp.bfloat16),
         scratch_shapes=[
             pltpu.VMEM((2, heads, 2 * half, tokens, head_dim), jnp.bfloat16),
-            pltpu.VMEM((heads, sources, tokens, head_dim), jnp.bfloat16),
-            pltpu.SemaphoreType.DMA((heads, 5)),
+            pltpu.SemaphoreType.DMA((heads, 4)),
         ],
         compiler_params=pltpu.CompilerParams(vmem_limit_bytes=VMEM_BYTES // 3),
         cost_estimate=pl.CostEstimate(

time: 164 us -> 164 us (level)
  no operation moved by 1% of the time
where the time goes in v10:
time: 164 us; the launch traced here: 162 us
  waiting for transfers between devices  61.4 us (37%)
  blocking collectives  38.3 us (23%)
  Pallas kernels  30 us (18%)
  starting transfers between devices  28.1 us (17%)
  local copies, waits for them, and re-layouts  3.31 us (2%)
    all_to_all x2, waiting for transfers between devices, exchange(): lax.all_to_all(array, 'head', split_axis=0, concat_axis=0, tiled=True)  44.3 us
    all_to_all x1, blocking collectives, exchange(): lax.all_to_all(array, 'head', split_axis=0, concat_axis=0, tiled=True)  38.3 us
    ppermute x2, waiting for transfers between devices, body(): lax.ppermute(outer_part[:, index], both, outer_route)  17 us
    all_to_all x2, starting transfers between devices, exchange(): lax.all_to_all(array, 'head', split_axis=0, concat_axis=0, tiled=True)  10.8 us
    pallas_call x1, Pallas kernels, attend_local(): pl.pallas_call(kernel, in_specs=[smem, hbm, hbm], out_specs=[vmem, vmem],...  8.92 us
    pallas_call x1, Pallas kernels, sort_lists(): pl.pallas_call(kernel, in_specs=[smem, smem, smem], out_specs=[smem, smem...  8.08 us
    ppermute x2, starting transfers between devices, body(): crossed = [lax.ppermute(part, both, across) for part in outer]  8.04 us
    ppermute x2, starting transfers between devices, body(): lax.ppermute(outer_part[:, index], both, outer_route)  7.07 us
  transfers between devices with their start and end apart: 7, of which 3 were waited for; matrix products, arithmetic and copies ran while one was open for 2% of the time, Pallas kernels for 12%

profile of v10, /device:TPU:448, one launch (start us, length us, event | category | flops | bytes accessed | tf_op | source)
XLA Modules:
  0.0 161.8 jit_solution(9229946242950935647)
XLA Ops:
  0.0 3.2 %shard_map.57 = bf16[8,2,3,192,128]{4,3,2,1,0:T(8,128)(2,1)} custom-call(bf16[192,3072]{1,0:T(8,128)(2,1)} %refs_0_.2, bf16[192,3072]{1,0:T(8,128)(2,1)} %refs_1_.1), custom_call_target="tpu_custom_call" | custom-call | flops 150994944 | bytes 4718592 | tf_op jit(solution)/shard_map/pallas_call | solution.py:66
  3.2 0.0 copy-start.2
  3.2 0.0 copy-start.3
  3.2 7.2 %all-to-all-start.1 = ((bf16[8,2,3,192,128]{4,3,2,1,0:T(8,128)(2,1)}), bf16[8,2,3,192,128]{4,3,2,1,0:T(8,128)(2,1)S(1)}, u32[]{:S(2)}, u32[]{:S(2)}) async-start(bf16[8,2,3,192,128]{4,3,2,1,0:T(8,128)(2,1)} %shard_map.57), calls=%async_computation.1 | async-start | bytes 4718592 | tf_op jit(solution)/shard_map/all_to_all | solution.py:460
  10.4 0.0 copy-done.2
  10.4 0.7 copy.8.listed_ref
  11.1 0.0 copy-done.3
  11.1 0.7 copy.9.counts_ref
  11.8 0.6 pad_add_fusion
  12.4 8.1 %shard_map.55 = (s32[36,16]{1,0:T(8,128)}, s32[36,8]{1,0:T(8,128)}) custom-call(s32[2]{0:T(128)} %get-tuple-element.23.place_ref, s32[24,144]{1,0:T(8,128)} %copy.8.listed_ref, s32[24,12]{1,0:T(8,128)} %copy.9.counts_ref), custom_call_target="tpu_custom_call" | custom-call | tf_op jit(solution)/shard_map/pallas_call | solution.py:166
  20.5 2.7 %shard_map.56 = bf16[8,1,3,192,128]{4,3,2,1,0:T(8,128)(2,1)} custom-call(bf16[192,3072]{1,0:T(8,128)(2,1)} %refs_0_.1), custom_call_target="tpu_custom_call" | custom-call | flops 150994944 | bytes 2359296 | tf_op jit(solution)/shard_map/pallas_call | solution.py:66
  23.2 44.3 %all-to-all-done.1.own_ref = bf16[8,2,3,192,128]{4,3,2,1,0:T(8,128)(2,1)S(1)} async-done(((bf16[8,2,3,192,128]{4,3,2,1,0:T(8,128)(2,1)}), bf16[8,2,3,192,128]{4,3,2,1,0:T(8,128)(2,1)S(1)}, u32[]{:S(2)}, u32[]{:S(2)}) %all-to-all-start.1) | async-done | bytes 2359328 | tf_op jit(solution)/shard_map/all_to_all | solution.py:460
  67.5 3.6 %all-to-all-start = ((bf16[8,1,3,192,128]{4,3,2,1,0:T(8,128)(2,1)}), bf16[8,1,3,192,128]{4,3,2,1,0:T(8,128)(2,1)S(1)}, u32[]{:S(2)}, u32[]{:S(2)}) async-start(bf16[8,1,3,192,128]{4,3,2,1,0:T(8,128)(2,1)} %shard_map.56), calls=%async_computation | async-start | bytes 2359296 | tf_op jit(solution)/shard_map/all_to_all | solution.py:460
  71.0 0.1 dynamic-slice_bitcast_fusion
  71.1 4.7 %collective-permute-start = (bf16[4,3,192,128]{3,2,1,0:T(8,128)(2,1)S(1)}, bf16[4,3,192,128]{3,2,1,0:T(8,128)(2,1)}, u32[]{:S(2)}, u32[]{:S(2)}) collective-permute-start(bf16[4,3,192,128]{3,2,1,0:T(8,128)(2,1)S(1)} %get-tuple-element.22), channel_id=1, source_target_pairs={{8,16},{9,17},{10,18},{11,19},{12,20},{13,21},{14,22},{15,23},{16,... | collective-permute-start | bytes 1769480 | tf_op jit(solution)/shard_map/ppermute | solution.py:483
  75.8 2.4 %collective-permute-start.1 = (bf16[4,3,192,128]{3,2,1,0:T(8,128)(2,1)S(1)}, bf16[4,3,192,128]{3,2,1,0:T(8,128)(2,1)}, u32[]{:S(2)}, u32[]{:S(2)}) collective-permute-start(bf16[4,3,192,128]{3,2,1,0:T(8,128)(2,1)S(1)} %get-tuple-element.21), channel_id=1, source_target_pairs={{8,16},{9,17},{10,18},{11,19},{12,20},{13,21},{14,22},{15,23},{16,... | collective-permute-start | bytes 1769480 | tf_op jit(solution)/shard_map/ppermute | solution.py:483
  78.2 1.1 constant_dynamic-slice_fusion
  79.4 2.2 %collective-permute-start.4 = (bf16[4,2,3,192,128]{4,3,2,1,0:T(8,128)(2,1)}, bf16[4,2,3,192,128]{4,3,2,1,0:T(8,128)(2,1)}, u32[]{:S(2)}, u32[]{:S(2)}) collective-permute-start(bf16[4,2,3,192,128]{4,3,2,1,0:T(8,128)(2,1)} %constant_dynamic-slice_fusion), channel_id=1, source_target_pairs={{0,8},{1,9},{2,10},{3,11},{4,12},{5,13},{6,14},{7,15},{8,0},{9,1},... | collective-permute-start | bytes 3538952 | tf_op jit(solution)/shard_map/ppermute | solution.py:484
  81.6 9.0 %collective-permute-done.outer_k = bf16[4,3,192,128]{3,2,1,0:T(8,128)(2,1)} collective-permute-done((bf16[4,3,192,128]{3,2,1,0:T(8,128)(2,1)S(1)}, bf16[4,3,192,128]{3,2,1,0:T(8,128)(2,1)}, u32[]{:S(2)}, u32[]{:S(2)}) %collective-permute-start) | collective-permute-done | bytes 589856 | tf_op jit(solution)/shard_map/ppermute | solution.py:483
  90.5 4.0 %collective-permute-start.2 = (bf16[4,3,192,128]{3,2,1,0:T(8,128)(2,1)}, bf16[4,3,192,128]{3,2,1,0:T(8,128)(2,1)}, u32[]{:S(2)}, u32[]{:S(2)}) collective-permute-start(bf16[4,3,192,128]{3,2,1,0:T(8,128)(2,1)} %collective-permute-done.outer_k), channel_id=1, source_target_pairs={{0,32},{1,39},{2,34},{3,33},{4,36},{5,35},{6,38},{7,37},{24,56},{2... | collective-permute-start | bytes 1769480 | tf_op jit(solution)/shard_map/ppermute | solution.py:485
  94.6 8.1 %collective-permute-done.1.outer_v = bf16[4,3,192,128]{3,2,1,0:T(8,128)(2,1)} collective-permute-done((bf16[4,3,192,128]{3,2,1,0:T(8,128)(2,1)S(1)}, bf16[4,3,192,128]{3,2,1,0:T(8,128)(2,1)}, u32[]{:S(2)}, u32[]{:S(2)}) %collective-permute-start.1) | collective-permute-done | bytes 589856 | tf_op jit(solution)/shard_map/ppermute | solution.py:483
  102.6 4.0 %collective-permute-start.3 = (bf16[4,3,192,128]{3,2,1,0:T(8,128)(2,1)}, bf16[4,3,192,128]{3,2,1,0:T(8,128)(2,1)}, u32[]{:S(2)}, u32[]{:S(2)}) collective-permute-start(bf16[4,3,192,128]{3,2,1,0:T(8,128)(2,1)} %collective-permute-done.1.outer_v), channel_id=1, source_target_pairs={{0,32},{1,39},{2,34},{3,33},{4,36},{5,35},{6,38},{7,37},{24,56},{2... | collective-permute-start | bytes 1769480 | tf_op jit(solution)/shard_map/ppermute | solution.py:485
  106.6 0.0 all-to-all-done.query_ref
  106.7 0.0 copy-start.1
  106.7 0.7 copy-done.1
  107.4 0.0 copy-start
  107.4 8.9 %shard_map.58 = (f32[1536,384]{1,0:T(8,128)S(1)}, f32[1536,384]{1,0:T(8,128)S(1)}) custom-call(s32[36,16]{1,0:T(8,128)S(1)} %copy-done.1, bf16[8,2,3,192,128]{4,3,2,1,0:T(8,128)(2,1)S(1)} %all-to-all-done.1.own_ref, bf16[8,1,3,192,128]{4,3,2,1,0:T(8,128)(2,1)S(1)} %all-to-all-done.query_ref), custom_call_target="tpu_custom_call" | custom-call | flops 3623878656 | bytes 8257536 | tf_op jit(solution)/shard_map/pallas_call | solution.py:261
  116.3 0.0 collective-permute-done.2.crossed_k
  116.3 0.0 collective-permute-done.3.crossed_v
  116.3 0.0 collective-permute-done.4.inner_ref
  116.3 0.0 copy-done
  116.4 6.1 %shard_map.59 = bf16[1536,384]{1,0:T(8,128)(2,1)S(1)} custom-call(s32[36,8]{1,0:T(8,128)S(1)} %copy-done, s32[2]{0:T(128)S(1)} %get-tuple-element.16.kinds_ref, bf16[8,1,3,192,128]{4,3,2,1,0:T(8,128)(2,1)S(1)} %all-to-all-done.query_ref, bf16[4,3,192,128]{3,2,1,0:T(8,128)(2,1)} %collective-permute-done.outer_k, ...), custom_call_target="tpu_custom_call" | custom-call | flops 905969664 | bytes 9437184 | tf_op jit(solution)/shard_map/pallas_call | solution.py:375
  122.4 38.3 %all_to_all.15.parts_ref = bf16[8,192,384]{2,1,0:T(8,128)(2,1)S(1)} all-to-all(bf16[8,192,384]{2,1,0:T(8,128)(2,1)S(1)} %bitcast.11), channel_id=1, replica_groups=mesh['seq'=64,'head'=8] {'head'}, dimensions={0} | all-to-all | bytes 2359296 | tf_op jit(solution)/shard_map/all_to_all | solution.py:460
  160.8 1.1 shard_map.60
  (1 shorter events, 0.0 us)
Async XLA Ops:
  3.2 7.2 %copy-start.2 = (s32[24,12,12]{0,2,1:T(8,128)S(1)}, s32[24,12,12]{0,2,1:T(8,128)}, u32[]{:S(2)}) copy-start(s32[24,12,12]{0,2,1:T(8,128)} %param.8) | copy-start | bytes 41476
  3.2 7.9 %copy-start.3 = (s32[24,12]{0,1:T(8,128)S(1)}, s32[24,12]{0,1:T(8,128)}, u32[]{:S(2)}) copy-start(s32[24,12]{0,1:T(8,128)} %param.9) | copy-start | bytes 3460
  3.2 64.3 %all-to-all-start.1 = ((bf16[8,2,3,192,128]{4,3,2,1,0:T(8,128)(2,1)}), bf16[8,2,3,192,128]{4,3,2,1,0:T(8,128)(2,1)S(1)}, u32[]{:S(2)}, u32[]{:S(2)}) async-start(bf16[8,2,3,192,128]{4,3,2,1,0:T(8,128)(2,1)} %shard_map.57), calls=%async_computation.1 | async-start | bytes 4718592 | tf_op jit(solution)/shard_map/all_to_all | solution.py:460
  67.5 39.2 %all-to-all-start = ((bf16[8,1,3,192,128]{4,3,2,1,0:T(8,128)(2,1)}), bf16[8,1,3,192,128]{4,3,2,1,0:T(8,128)(2,1)S(1)}, u32[]{:S(2)}, u32[]{:S(2)}) async-start(bf16[8,1,3,192,128]{4,3,2,1,0:T(8,128)(2,1)} %shard_map.56), calls=%async_computation | async-start | bytes 2359296 | tf_op jit(solution)/shard_map/all_to_all | solution.py:460
  71.1 19.4 %collective-permute-start = (bf16[4,3,192,128]{3,2,1,0:T(8,128)(2,1)S(1)}, bf16[4,3,192,128]{3,2,1,0:T(8,128)(2,1)}, u32[]{:S(2)}, u32[]{:S(2)}) collective-permute-start(bf16[4,3,192,128]{3,2,1,0:T(8,128)(2,1)S(1)} %get-tuple-element.22), channel_id=1, source_target_pairs={{8,16},{9,17},{10,18},{11,19},{12,20},{13,21},{14,22},{15,23},{16,... | collective-permute-start | bytes 1769480 | tf_op jit(solution)/shard_map/ppermute | solution.py:483
  75.8 26.8 %collective-permute-start.1 = (bf16[4,3,192,128]{3,2,1,0:T(8,128)(2,1)S(1)}, bf16[4,3,192,128]{3,2,1,0:T(8,128)(2,1)}, u32[]{:S(2)}, u32[]{:S(2)}) collective-permute-start(bf16[4,3,192,128]{3,2,1,0:T(8,128)(2,1)S(1)} %get-tuple-element.21), channel_id=1, source_target_pairs={{8,16},{9,17},{10,18},{11,19},{12,20},{13,21},{14,22},{15,23},{16,... | collective-permute-start | bytes 1769480 | tf_op jit(solution)/shard_map/ppermute | solution.py:483
  79.4 37.0 %collective-permute-start.4 = (bf16[4,2,3,192,128]{4,3,2,1,0:T(8,128)(2,1)}, bf16[4,2,3,192,128]{4,3,2,1,0:T(8,128)(2,1)}, u32[]{:S(2)}, u32[]{:S(2)}) collective-permute-start(bf16[4,2,3,192,128]{4,3,2,1,0:T(8,128)(2,1)} %constant_dynamic-slice_fusion), channel_id=1, source_target_pairs={{0,8},{1,9},{2,10},{3,11},{4,12},{5,13},{6,14},{7,15},{8,0},{9,1},... | collective-permute-start | bytes 3538952 | tf_op jit(solution)/shard_map/ppermute | solution.py:484
  90.5 25.8 %collective-permute-start.2 = (bf16[4,3,192,128]{3,2,1,0:T(8,128)(2,1)}, bf16[4,3,192,128]{3,2,1,0:T(8,128)(2,1)}, u32[]{:S(2)}, u32[]{:S(2)}) collective-permute-start(bf16[4,3,192,128]{3,2,1,0:T(8,128)(2,1)} %collective-permute-done.outer_k), channel_id=1, source_target_pairs={{0,32},{1,39},{2,34},{3,33},{4,36},{5,35},{6,38},{7,37},{24,56},{2... | collective-permute-start | bytes 1769480 | tf_op jit(solution)/shard_map/ppermute | solution.py:485
  102.6 13.7 %collective-permute-start.3 = (bf16[4,3,192,128]{3,2,1,0:T(8,128)(2,1)}, bf16[4,3,192,128]{3,2,1,0:T(8,128)(2,1)}, u32[]{:S(2)}, u32[]{:S(2)}) collective-permute-start(bf16[4,3,192,128]{3,2,1,0:T(8,128)(2,1)} %collective-permute-done.1.outer_v), channel_id=1, source_target_pairs={{0,32},{1,39},{2,34},{3,33},{4,36},{5,35},{6,38},{7,37},{24,56},{2... | collective-permute-start | bytes 1769480 | tf_op jit(solution)/shard_map/ppermute | solution.py:485
  106.7 0.7 copy-start.1
  107.4 9.0 %copy-start = (s32[36,8]{1,0:T(8,128)S(1)}, s32[36,8]{1,0:T(8,128)}, u32[]{:S(2)}) copy-start(s32[36,8]{1,0:T(8,128)} %get-tuple-element.15.halo_ref) | copy-start | bytes 3460
